TPU v7x, 256 devices: a whole 4x4x8 slice. The times are simulated.
256 devices in a mesh: prow: 32 (over x, z_hi, core), pcol: 8 (over z_lo, y).
Axes of the slice: x: 4, y: 4, z: 8 (z_hi: 4, z_lo: 2; z = z_hi * 2 + z_lo), core: 2. Of those that a mesh axis runs over, the one named last changes fastest.
Arguments:
- inverse_root: bfloat16 [16384, 16384], P('prow', 'pcol'), may hold values from -6 to 6
- panel: bfloat16 [16384, 8, 256], P('pcol', None, 'prow'), may hold values from -0.0625 to 0.0625
- block_mask: int32 [8, 64], replicated, may hold values 0 or 1
- diag_inverse: float32 [8, 256, 256], P(None, 'prow', 'pcol'), may hold values from -6 to 6
Outputs:
- panel_inverse: float32 [16384, 8, 256], P(('prow', 'pcol'))
- block_inverse: float32 [8, 256, 256], P(None, 'prow', 'pcol')
All inputs are finite; a program needn't handle non-finite values.
Results may differ from a plain program's by a relative error of at most 0.0003.
Values may be sent and summed in bfloat16 or wider, within the bound.
No kernel may reach another device: no remote copies, remote signals or barrier semaphores. Data moves between devices by JAX's collectives and lax.ppermute only.
A program may use at most 64 MiB of HBM per device.

v0:
```python
import jax
import jax.numpy as jnp
from jax import lax
from jax.sharding import PartitionSpec as P


def spread(block, axis, source):
    block = jnp.where(lax.axis_index(axis) == source, block, jnp.zeros_like(block))
    return lax.psum(block, axis)


def shards(inverse_root, panel, block_mask, diag_inverse):
    rows_here = inverse_root.shape[0]
    cols_here = inverse_root.shape[1]
    blocks = panel.shape[1]
    row_index = lax.axis_index("prow")
    col_index = lax.axis_index("pcol")
    prow_count = lax.axis_size("prow")
    pcol_count = lax.axis_size("pcol")
    column_panel = lax.all_gather(panel, "prow", axis=2, tiled=True)
    block_width = column_panel.shape[2]
    mask_rows = jnp.repeat(block_mask, block_width, axis=1)
    mask_here = lax.dynamic_slice_in_dim(mask_rows, col_index * cols_here, cols_here, 1)
    masked = column_panel * jnp.transpose(mask_here).astype(jnp.bfloat16)[:, :, None]
    partial_prod = jnp.dot(
        inverse_root,
        masked.reshape(cols_here, blocks * block_width),
        preferred_element_type=jnp.float32,
    ).reshape(rows_here, blocks, block_width)
    root_col = row_index * pcol_count // prow_count
    offset = jnp.clip(row_index * rows_here - col_index * cols_here, 0, cols_here - rows_here)
    row_slab = lax.dynamic_slice_in_dim(masked, offset, rows_here, 0)
    share_rows = rows_here // pcol_count
    product = lax.psum_scatter(partial_prod, "pcol", scatter_dimension=0, tiled=True)
    row_panel = spread(row_slab, "pcol", root_col)
    own_rows = lax.dynamic_slice_in_dim(row_panel, col_index * share_rows, share_rows, 0)
    diag_part = jnp.einsum(
        "rkv,rkw->kvw", own_rows.astype(jnp.float32), product, precision=lax.Precision.HIGHEST
    )
    by_cols = lax.psum_scatter(diag_part, "pcol", scatter_dimension=2, tiled=True)
    summed = lax.psum_scatter(by_cols, "prow", scatter_dimension=1, tiled=True)
    return (-product, diag_inverse + summed)


def solution(mesh):
    in_specs = (P("prow", "pcol"), P("pcol", None, "prow"), P(), P(None, "prow", "pcol"))
    out_specs = (P(("prow", "pcol"), None, None), P(None, "prow", "pcol"))
    return jax.shard_map(shards, mesh=mesh, in_specs=in_specs, out_specs=out_specs, check_vma=False)
```

profile of v0, /device:TPU:1, one launch (start us, length us, event | category | flops | bytes accessed | tf_op | source)
XLA Modules:
  0.0 406.7 jit_solution(3328189982459115104)
XLA Ops:
  7.2 1.9 copy.19
  9.2 0.0 all-reduce.2.cloned.1.call-start
  9.3 0.8 copy.20
  10.0 0.1 broadcast_in_dim.7
  10.2 81.3 %all-gather.2.cloned.1.call-done = bf16[2048,8,256]{0,1,2:T(8,128)(2,1)} async-done(((bf16[2048,8,8]{0,1,2:T(8,128)(2,1)}), bf16[2048,8,256]{0,1,2:T(8,128)(2,1)}) %all-gather.2.cloned.1.call-update) | async-done | bytes 8388624 | tf_op jit(solution)/shard_map/all_gather | solution.py:20
  91.5 12.8 %copy.21 = bf16[2048,8,256]{2,0,1:T(8,128)(2,1)} copy(bf16[2048,8,256]{0,1,2:T(8,128)(2,1)} %all-gather.2.cloned.1.call-done) | data formatting | bytes 16777216 | tf_op jit(solution)/shard_map/all_gather | solution.py:20
  104.3 5.2 %broadcast_multiply_fusion = bf16[2048,8,256]{2,0,1:T(8,128)(2,1)S(1)} fusion(bf16[2048,8,256]{2,0,1:T(8,128)(2,1)} %copy.21, bf16[2048,8]{0,1:T(8,128)(2,1)S(1)} %fusion.3), kind=kLoop, calls=%fused_computation | loop fusion | flops 4194304 | bytes 16809984 | tf_op jit(solution)/shard_map/mul | solution.py:24
  109.6 3.2 copy-done.1
  112.8 1.9 dynamic-slice_select_fusion
  114.8 0.0 reduce-scatter.4.cloned.1.call-start
  114.8 11.5 %copy.22 = bf16[2048,8,256]{0,2,1:T(8,128)(2,1)} copy(bf16[2048,8,256]{2,0,1:T(8,128)(2,1)} %copy-done.1) | data formatting | bytes 16777216 | tf_op jit(solution)/shard_map/mul | solution.py:24
  126.3 9.7 %fusion.5 = f32[2048,512]{1,0:T(8,128)} fusion(bf16[2048,2048]{0,1:T(8,128)(2,1)} %bitcast.9, bf16[512,2048]{1,0:T(8,128)(2,1)S(1)} %copy-done), kind=kOutput, calls=%fused_computation.9 | convolution fusion | flops 4294967296 | bytes 14680064 | tf_op jit(solution)/shard_map/dot_general | solution.py:25
  136.0 5.5 %copy.23 = f32[512,8,256]{2,1,0:T(8,128)} copy(f32[512,8,256]{0,2,1:T(8,128)} %bitcast.10) | data formatting | bytes 8388608 | tf_op jit(solution)/shard_map/reshape | solution.py:29
  141.5 0.0 reduce-scatter.6.cloned.1.call-start
  141.6 57.8 %all-reduce.2.cloned.1.call-done = bf16[512,8,256]{2,0,1:T(8,128)(2,1)} async-done(((bf16[512,8,256]{2,0,1:T(8,128)(2,1)}), bf16[512,8,256]{2,0,1:T(8,128)(2,1)}) %all-reduce.2.cloned.1.call-update) | async-done | bytes 2097168 | tf_op jit(solution)/shard_map/psum | solution.py:9
  199.3 62.1 %reduce-scatter.4.cloned.1.call-done = f32[64,8,256]{2,1,0:T(8,128)} async-done(((f32[512,8,256]{2,1,0:T(8,128)}), f32[64,8,256]{2,1,0:T(8,128)}) %reduce-scatter.4.cloned.1.call-update) | async-done | bytes 524304 | tf_op jit(solution)/shard_map/reduce_scatter | solution.py:34
  261.5 3.6 fusion
  265.1 0.0 reduce-scatter.8.cloned.1.call-start
  265.1 38.8 %reduce-scatter.6.cloned.1.call-done = f32[8,256,32]{1,2,0:T(8,128)} async-done(((f32[8,256,256]{1,2,0:T(8,128)}), f32[8,256,32]{1,2,0:T(8,128)}) %reduce-scatter.6.cloned.1.call-update) | async-done | bytes 262160 | tf_op jit(solution)/shard_map/reduce_scatter | solution.py:40
  303.9 2.3 copy.25
  306.2 0.8 neg.3
  307.1 91.7 %reduce-scatter.8.cloned.1.call-done = f32[8,8,32]{2,0,1:T(8,128)} async-done(((f32[8,256,32]{2,0,1:T(8,128)}), f32[8,8,32]{2,0,1:T(8,128)}) %reduce-scatter.8.cloned.1.call-update) | async-done | bytes 8208 | tf_op jit(solution)/shard_map/reduce_scatter | solution.py:41
  398.8 0.8 copy_add_fusion
  399.5 0.6 copy.27
  (14 shorter events, 0.2 us)
Async XLA Ops:
  7.2 119.1 %copy-start = (bf16[512,2048]{1,0:T(8,128)(2,1)S(1)}, bf16[512,2048]{1,0:T(8,128)(2,1)}, u32[]{:S(2)}) copy-start(bf16[512,2048]{1,0:T(8,128)(2,1)} %param.4) | copy-start | bytes 6291460
  7.2 84.3 %all-gather.2.cloned.1.call-start = ((), (), s32[]{:S(2)}) async-start(), calls=%async_computation.3 | async-start | bytes 8650752 | tf_op jit(solution)/shard_map/all_gather | solution.py:20
  9.2 190.1 %all-reduce.2.cloned.1.call-start = ((), (), s32[]{:S(2)}) async-start(), calls=%async_computation.5 | async-start | bytes 4194304 | tf_op jit(solution)/shard_map/psum | solution.py:9
  109.6 3.2 copy-start.1
  114.8 146.7 %reduce-scatter.4.cloned.1.call-start = ((), (), s32[]{:S(2)}) async-start(), calls=%async_computation.4 | async-start | bytes 4718592 | tf_op jit(solution)/shard_map/reduce_scatter | solution.py:34
  141.5 162.4 %reduce-scatter.6.cloned.1.call-start = ((), (), s32[]{:S(2)}) async-start(), calls=%async_computation.6 | async-start | bytes 2359296 | tf_op jit(solution)/shard_map/reduce_scatter | solution.py:40
  141.5 257.2 %copy-start.3 = (f32[8,8,32]{2,1,0:T(8,128)S(1)}, f32[8,8,32]{2,1,0:T(8,128)}, u32[]{:S(2)}) copy-start(f32[8,8,32]{2,1,0:T(8,128)} %param.7) | copy-start | bytes 24580
  261.5 44.8 %copy-start.2 = (f32[64,8,256]{2,1,0:T(8,128)S(1)}, f32[64,8,256]{2,1,0:T(8,128)}, u32[]{:S(2)}) copy-start(f32[64,8,256]{2,1,0:T(8,128)} %reduce-scatter.4.cloned.1.call-done) | copy-start | bytes 1572868
  265.1 133.7 %reduce-scatter.8.cloned.1.call-start = ((), (), s32[]{:S(2)}) async-start(), calls=%async_computation.7 | async-start | bytes 1081344 | tf_op jit(solution)/shard_map/reduce_scatter | solution.py:41
Sparse Core Ops, SparseCore 0:
  11.1 80.3 all-gather.1
  114.9 84.3 all-reduce.1
  201.9 59.5 reduce-scatter.3
  265.2 38.7 reduce-scatter.5
  307.6 91.1 reduce-scatter.7
where the time goes:
time: 409 us; the launch traced here: 407 us
  waiting for transfers between devices  332 us (81%)
  local copies, waits for them, and re-layouts  38.8 us (9%)
  between operations  13.9 us (3%)
  matrix products  13.3 us (3%)
  other arithmetic  8.77 us (2%)
    reduce_scatter x1, waiting for transfers between devices, shards(): summed = lax.psum_scatter(by_cols, 'prow', scatter_dimension=1, tiled=True)  91.7 us
    all_gather x1, waiting for transfers between devices, shards(): column_panel = lax.all_gather(panel, 'prow', axis=2, tiled=True)  81.3 us
    reduce_scatter x1, waiting for transfers between devices, shards(): lax.psum_scatter(partial_prod, 'pcol', scatter_dimension=0, tiled=True)  62.1 us
    psum x1, waiting for transfers between devices, spread(): return lax.psum(block, axis)  57.8 us
    reduce_scatter x1, waiting for transfers between devices, shards(): lax.psum_scatter(diag_part, 'pcol', scatter_dimension=2, tiled=True)  38.8 us
    all_gather x1, local copies, waits for them, and re-layouts, shards(): column_panel = lax.all_gather(panel, 'prow', axis=2, tiled=True)  12.8 us
    mul x1, local copies, waits for them, and re-layouts, shards(): column_panel * jnp.transpose(mask_here).astype(jnp.bfloat16)[:, :, None]  11.5 us
    dot_general x1, matrix products, shards(): jnp.dot(inverse_root, masked.reshape(cols_here, blocks * block_width), pr...  9.7 us
  transfers between devices with their start and end apart: 5, of which 5 were waited for; matrix products, arithmetic and copies ran while one was open for 7% of the time, Pallas kernels for 0%

commit v1 on v0

v1 whole, which is shorter than its diff:
```python
import functools

import jax
import jax.numpy as jnp
from jax import lax
from jax.experimental import pallas as pl
from jax.experimental.pallas import tpu as pltpu
from jax.sharding import Mesh, PartitionSpec as P

CHUNKS = (4, 4)
SCALE = 64.0
NT = (((1,), (1,)), ((), ()))
VMEM = pl.BlockSpec(memory_space=pltpu.VMEM)
SMEM = pl.BlockSpec(memory_space=pltpu.SMEM)


def product_kernel(rows, ids, own, fwd, bwd, far_a, far_b, weights, select, out, picked, gathered, pair):
    ix, iz = ids[0], ids[1]

    def place(piece, first, count, x):
        for s in range(count):
            z = lax.rem(iz + 4 - (first + s), 4)
            start = pl.multiple_of((x * 4 + z) * rows, 16)
            gathered[pl.ds(start, rows), :] = piece[s * rows:(s + 1) * rows, :]

    place(own, 0, 4, ix)
    place(fwd, 0, 4, lax.rem(ix + 3, 4))
    place(bwd, 0, 4, lax.rem(ix + 1, 4))
    place(far_a, 0, 2, lax.rem(ix + 2, 4))
    place(far_b, 2, 2, lax.rem(ix + 2, 4))
    for t in range(4):
        pair[0:128, :] = weights[2 * t]
        pair[128:256, :] = weights[2 * t + 1]
        prod = lax.dot_general(gathered[...], pair[...], NT, preferred_element_type=jnp.float32)
        out[2 * t] = prod[:, 0:128]
        out[2 * t + 1] = prod[:, 128:256]
    picked[...] = lax.dot_general(
        gathered[...], select[...], NT, preferred_element_type=jnp.float32
    ).astype(picked.dtype)


def product_call(kc, ids, own, fwd, bwd, far_a, far_b, weights, select):
    n = 128 * kc
    return pl.pallas_call(
        functools.partial(product_kernel, 8 * kc),
        out_shape=(
            jax.ShapeDtypeStruct((8, n, 128), jnp.float32),
            jax.ShapeDtypeStruct((n, 128), jnp.bfloat16),
        ),
        in_specs=[SMEM] + [VMEM] * 7,
        out_specs=(VMEM, VMEM),
        scratch_shapes=[pltpu.VMEM((n, 2048), jnp.bfloat16), pltpu.VMEM((256, 2048), jnp.bfloat16)],
        compiler_params=pltpu.CompilerParams(vmem_limit_bytes=40 * 2**20),
        cost_estimate=pl.CostEstimate(flops=2 * n * 2048 * 1152, bytes_accessed=2 * n * 2048 + 10 * 2**20, transcendentals=0),
    )(ids, own, fwd, bwd, far_a, far_b, weights, select)


def diag_kernel(kc, product, mine, other, keep, give, diag):
    total = product[...].reshape(16, kc, 8, 128)
    left = mine[...].astype(jnp.float32).reshape(16, kc, 8, 128)
    right = pltpu.roll(other[...].astype(jnp.float32), 64, 1).reshape(16, kc, 8, 128)
    low = lax.broadcasted_iota(jnp.int32, (128, 128), 1) < 64
    per_k = [total[:, k].reshape(128, 128) for k in range(kc)]
    for t in range(kc // 2):
        a, b = per_k[2 * t], per_k[2 * t + 1]
        keep[t] = -jnp.where(low, a, pltpu.roll(b, 64, 1))
        give[t] = -jnp.where(low, pltpu.roll(a, 64, 1), b)
    for k in range(kc):
        p = per_k[k]
        hi = p.astype(jnp.bfloat16)
        rest = p - hi.astype(jnp.float32)
        mid = rest.astype(jnp.bfloat16)
        lo = (rest - mid.astype(jnp.float32)).astype(jnp.bfloat16)
        m = jnp.concatenate([left[:, k].reshape(128, 128), right[:, k].reshape(128, 128)], axis=0).astype(jnp.bfloat16)
        d = lax.dot_general(lo, m, NT, preferred_element_type=jnp.float32)
        d += lax.dot_general(mid, m, NT, preferred_element_type=jnp.float32)
        d += lax.dot_general(hi, m, NT, preferred_element_type=jnp.float32)
        for j in range(8):
            diag[j, k * 16:(k + 1) * 16, :] = d[j * 16:(j + 1) * 16, :]


def diag_call(kc, product, mine, other):
    return pl.pallas_call(
        functools.partial(diag_kernel, kc),
        out_shape=(
            jax.ShapeDtypeStruct((kc // 2, 128, 128), jnp.float32),
            jax.ShapeDtypeStruct((kc // 2, 128, 128), jnp.float32),
            jax.ShapeDtypeStruct((8, kc * 16, 256), jnp.float32),
        ),
        in_specs=[VMEM] * 3,
        out_specs=(VMEM,) * 3,
        compiler_params=pltpu.CompilerParams(vmem_limit_bytes=32 * 2**20),
        cost_estimate=pl.CostEstimate(flops=2 * kc * 3 * 128 * 128 * 256, bytes_accessed=8 * kc * 2**18, transcendentals=0),
    )(product, mine, other)


def rows_kernel(count, ids, *refs):
    keeps, gots, out = refs[:count], refs[count:2 * count], refs[2 * count]
    first = ids[2] == 0
    pair = 0
    for keep, got in zip(keeps, gots):
        for t in range(keep.shape[0]):
            a, b = keep[t].reshape(16, 1, 8, 128), got[t].reshape(16, 1, 8, 128)
            even, odd = jnp.where(first, a, b), jnp.where(first, b, a)
            both = jnp.concatenate([even, odd], axis=1).reshape(256, 128).T
            out[:, 2 * pair, :] = both[0:64, :]
            out[:, 2 * pair + 1, :] = both[64:128, :]
            pair += 1


def rows_call(ids, keeps, gots):
    return pl.pallas_call(
        functools.partial(rows_kernel, len(keeps)),
        out_shape=jax.ShapeDtypeStruct((64, 8, 256), jnp.float32),
        in_specs=[SMEM] + [VMEM] * (2 * len(keeps)),
        out_specs=VMEM,
        compiler_params=pltpu.CompilerParams(vmem_limit_bytes=32 * 2**20),
        cost_estimate=pl.CostEstimate(flops=0, bytes_accessed=2**20, transcendentals=0),
    )(ids, *keeps, *gots)


def turn(size, shift):
    return [(i, (i + shift) % size) for i in range(size)]


def owner_route():
    route = []
    for x in range(4):
        for z in range(4):
            for low in range(2):
                for y in range(4):
                    row = 2 * (low * 4 + y) + z // 2
                    source = ((x * 4 + z) * 2 + low) * 4 + y
                    route.append((source, (row * 2 + z % 2) * 4 + x))
    return route


def shards(inverse_root, panel, block_mask, diag_inverse):
    ix, iz, ic = lax.axis_index("x"), lax.axis_index("zh"), lax.axis_index("core")
    col = lax.axis_index("zl") * 4 + lax.axis_index("y")
    ids = jnp.stack([ix, iz, ic]).astype(jnp.int32)
    swap = [(0, 1), (1, 0)]

    mask_here = lax.dynamic_slice_in_dim(block_mask, col * 8, 8, 1).astype(jnp.bfloat16)
    masked = jnp.transpose(panel, (1, 2, 0)) * jnp.repeat(mask_here, 256, axis=1)[:, None, :]

    starts = [sum(CHUNKS[:i]) for i in range(len(CHUNKS))]
    slabs = []
    for first, kc in zip(starts, CHUNKS):
        own = masked[first:first + kc].reshape(kc * 8, 2048)
        slabs.append((own, [lax.ppermute(own, "zh", turn(4, s)) for s in (1, 2, 3)]))

    other_root = lax.ppermute(inverse_root, "core", swap)
    weights = jnp.concatenate([inverse_root.reshape(8, 64, 2048), other_root.reshape(8, 64, 2048)], axis=1)

    lane = lax.broadcasted_iota(jnp.int32, (128, 2048), 0)
    at = lax.broadcasted_iota(jnp.int32, (128, 2048), 1)
    wanted = (iz // 2) * 1024 + (ic ^ (lane // 64)) * 512 + ((iz % 2) * 4 + ix) * 64 + lane % 64
    select = (at == wanted).astype(jnp.bfloat16)

    keeps, gots, summed = [], [], []
    for (own, others), kc in zip(slabs, CHUNKS):
        half = 16 * kc
        slab = jnp.concatenate([own] + others, axis=0)
        fwd = lax.ppermute(slab, "x", turn(4, 1))
        bwd = lax.ppermute(slab, "x", turn(4, -1))
        far_a = lax.ppermute(fwd[:half], "x", turn(4, 1))
        far_b = lax.ppermute(bwd[half:], "x", turn(4, -1))
        partial, picked = product_call(kc, ids, slab, fwd, bwd, far_a, far_b, weights, select)
        mine = lax.ppermute(picked, ("x", "zh", "zl", "y"), owner_route())
        other = lax.ppermute(mine, "core", swap)
        sent = (partial * SCALE).astype(jnp.float16)
        parts = lax.all_to_all(sent, ("zl", "y"), 0, 0, tiled=True)
        product = jnp.sum(parts.astype(jnp.float32), axis=0) * (1.0 / SCALE)
        keep, give, diag = diag_call(kc, product, mine, other)
        keeps.append(keep)
        gots.append(lax.ppermute(give, "core", swap))
        summed.append(jnp.sum(lax.all_to_all(diag, ("zl", "y"), 0, 0, tiled=True), axis=0))

    panel_inverse = rows_call(ids, keeps, gots)

    across = jnp.concatenate(summed, axis=0).T.reshape(2, 16, 8, 128)
    across = jnp.transpose(across, (1, 0, 2, 3))
    here = jnp.sum(lax.all_to_all(across, ("x", "zh"), 0, 0, tiled=True), axis=0)
    came = lax.ppermute(here[1], "core", swap)
    even, odd = jnp.where(ic == 0, here[0], came), jnp.where(ic == 0, came, here[0])
    both = jnp.stack([even.reshape(8, 8, 2, 8), odd.reshape(8, 8, 2, 8)], axis=3)
    block = jnp.transpose(both, (1, 0, 2, 3, 4)).reshape(8, 8, 32)
    return panel_inverse, diag_inverse + block


def solution(mesh):
    wide = Mesh(mesh.devices.reshape(4, 4, 2, 2, 4), ("x", "zh", "core", "zl", "y"))
    prow, pcol = ("x", "zh", "core"), ("zl", "y")
    in_specs = (P(prow, pcol), P(pcol, None, prow), P(), P(None, prow, pcol))
    out_specs = (P(prow + pcol, None, None), P(None, prow, pcol))
    return jax.shard_map(shards, mesh=wide, in_specs=in_specs, out_specs=out_specs, check_vma=False)
```

time: 409 us -> 205 us (0.50)
  waiting for transfers between devices: 332 us -> 73.3 us
  starting transfers between devices: 0.21 us -> 108 us
  local copies, waits for them, and re-layouts: 38.8 us -> 3.76 us
  matrix products: 13.3 us -> 0 us
  between operations: 13.9 us -> 0.95 us
  Pallas kernels: 0 us -> 11.1 us
    reduce_scatter x3 -> x0, waiting for transfers between devices: 193 us -> none  [the longest x1 91.7 us: shards(): summed = lax.psum_scatter(by_cols, 'prow', scatter_dimension=1, tiled=True)]
    all_gather x1 -> x0, waiting for transfers between devices: 81.3 us -> none  [shards(): column_panel = lax.all_gather(panel, 'prow', axis=2, tiled=True)]
    all_to_all x0 -> x5, starting transfers between devices: none -> 62.8 us  [the longest x2 35 us: shards(): lax.all_to_all(diag, ('zl', 'y'), 0, 0, tiled=True)]
    psum x1 -> x0, waiting for transfers between devices: 57.8 us -> none  [spread(): return lax.psum(block, axis)]
    ppermute x0 -> x22, waiting for transfers between devices: none -> 53 us  [the longest x6 24.9 us: shards(): lax.ppermute(own, 'zh', turn(4, s))]
    ppermute x0 -> x22, starting transfers between devices: none -> 45.2 us  [the longest x6 14.9 us: shards(): lax.ppermute(own, 'zh', turn(4, s))]
    all_to_all x0 -> x5, waiting for transfers between devices: none -> 20.3 us  [the longest x2 12.7 us: shards(): lax.all_to_all(diag, ('zl', 'y'), 0, 0, tiled=True)]
    dot_general x2 -> x0, matrix products: 13.3 us -> none  [the longest x1 9.7 us: shards(): jnp.dot(inverse_root, masked.reshape(cols_here, blocks * block_width), pr...]
  transfers between devices with their start and end apart: 5 -> 27, of which waited for: 5 -> 12; matrix products, arithmetic and copies ran while one was open for 7% -> 3% of each run, Pallas kernels for 0% -> 4%
where the time goes in v1:
time: 205 us
  starting transfers between devices  108 us (53%)
  waiting for transfers between devices  73.3 us (36%)
  Pallas kernels  11.1 us (5%)
  other arithmetic  7.63 us (4%)
  local copies, waits for them, and re-layouts  3.76 us (2%)
    all_to_all x2, starting transfers between devices, shards(): lax.all_to_all(diag, ('zl', 'y'), 0, 0, tiled=True)  35 us
    ppermute x6, waiting for transfers between devices, shards(): lax.ppermute(own, 'zh', turn(4, s))  24.9 us
    all_to_all x1, starting transfers between devices, shards(): lax.all_to_all(across, ('x', 'zh'), 0, 0, tiled=True)  18.8 us
    ppermute x2, waiting for transfers between devices, shards(): fwd = lax.ppermute(slab, 'x', turn(4, 1))  17.6 us
    ppermute x6, starting transfers between devices, shards(): lax.ppermute(own, 'zh', turn(4, s))  14.9 us
    all_to_all x2, waiting for transfers between devices, shards(): lax.all_to_all(diag, ('zl', 'y'), 0, 0, tiled=True)  12.7 us
    all_to_all x2, starting transfers between devices, shards(): parts = lax.all_to_all(sent, ('zl', 'y'), 0, 0, tiled=True)  8.93 us
    ppermute x2, waiting for transfers between devices, shards(): far_a = lax.ppermute(fwd[:half], 'x', turn(4, 1))  8.9 us
  transfers between devices with their start and end apart: 27, of which 12 were waited for; matrix products, arithmetic and copies ran while one was open for 3% of the time, Pallas kernels for 4%

profile of v1, /device:TPU:1, one launch (start us, length us, event | category | flops | bytes accessed | tf_op | source)
XLA Modules:
  0.0 204.8 jit_solution(6696365445844574399)
XLA Ops:
  0.6 3.3 %collective-permute-start.7 = (bf16[512,2048]{1,0:T(8,128)(2,1)}, bf16[512,2048]{1,0:T(8,128)(2,1)}, u32[]{:S(2)}, u32[]{:S(2)}) collective-permute-start(bf16[512,2048]{1,0:T(8,128)(2,1)} %param.4), channel_id=1, source_target_pairs={{0,8},{8,0},{1,9},{9,1},{2,10},{10,2},{3,11},{11,3},{4,12},{12,4},... | collective-permute-start | bytes 6291464 | tf_op jit(solution)/shard_map/ppermute | solution.py:153
  7.2 5.1 %collective-permute-start.11 = (bf16[32,2048]{1,0:T(8,128)(2,1)S(1)}, bf16[32,2048]{1,0:T(8,128)(2,1)S(1)}, u32[]{:S(2)}, u32[]{:S(2)}) collective-permute-start(bf16[32,2048]{1,0:T(8,128)(2,1)S(1)} %get-tuple-element.22), channel_id=1, source_target_pairs={{0,32},{16,48},{32,0},{48,16},{1,33},{17,49},{33,1},{49,17},{2,34}... | collective-permute-start | bytes 393224 | tf_op jit(solution)/shard_map/ppermute | solution.py:151
  14.8 6.7 %collective-permute-done.11 = bf16[32,2048]{1,0:T(8,128)(2,1)S(1)} collective-permute-done((bf16[32,2048]{1,0:T(8,128)(2,1)S(1)}, bf16[32,2048]{1,0:T(8,128)(2,1)S(1)}, u32[]{:S(2)}, u32[]{:S(2)}) %collective-permute-start.11) | collective-permute-done | bytes 131104 | tf_op jit(solution)/shard_map/ppermute | solution.py:151
  21.5 3.8 %collective-permute-done.12 = bf16[32,2048]{1,0:T(8,128)(2,1)S(1)} collective-permute-done((bf16[32,2048]{1,0:T(8,128)(2,1)S(1)}, bf16[32,2048]{1,0:T(8,128)(2,1)S(1)}, u32[]{:S(2)}, u32[]{:S(2)}) %collective-permute-start.12) | collective-permute-done | bytes 131104 | tf_op jit(solution)/shard_map/ppermute | solution.py:151
  28.4 11.3 %collective-permute-done.13.fwd = bf16[128,2048]{1,0:T(8,128)(2,1)S(1)} collective-permute-done((bf16[128,2048]{1,0:T(8,128)(2,1)S(1)}, bf16[128,2048]{1,0:T(8,128)(2,1)S(1)}, u32[]{:S(2)}, u32[]{:S(2)}) %collective-permute-start.13) | collective-permute-done | bytes 524320 | tf_op jit(solution)/shard_map/ppermute | solution.py:165
  44.4 3.0 %collective-permute-done.15.far_a = bf16[64,2048]{1,0:T(8,128)(2,1)S(1)} collective-permute-done((bf16[64,2048]{1,0:T(8,128)(2,1)S(1)}, bf16[64,2048]{1,0:T(8,128)(2,1)S(1)}, u32[]{:S(2)}, u32[]{:S(2)}) %collective-permute-start.15) | collective-permute-done | bytes 262176 | tf_op jit(solution)/shard_map/ppermute | solution.py:167
  47.4 3.5 %shard_map.61 = (f32[8,512,128]{2,1,0:T(8,128)S(1)}, bf16[512,128]{1,0:T(8,128)(2,1)S(1)}) custom-call(s32[3]{0:T(128)S(1)} %pad_add_fusion.ids, bf16[128,2048]{1,0:T(8,128)(2,1)S(1)} %pad_maximum_fusion.2.own, bf16[128,2048]{1,0:T(8,128)(2,1)S(1)} %collective-permute-done.13.fwd, bf16[128,2048]{1,0:T(8,128)(2,1)S(1)} %collective-permute-done.14.bwd, ...), custom_call_target="tpu_custom_call" | custom-call | flops 2415919104 | bytes 12582912 | tf_op jit(solution)/shard_map/pallas_call | solution.py:44
  52.2 4.2 %all-to-all-start.1 = ((f16[8,512,128]{2,1,0:T(8,128)(2,1)}), f16[8,512,128]{2,1,0:T(8,128)(2,1)S(1)}, u32[]{:S(2)}, u32[]{:S(2)}) async-start(f16[8,512,128]{2,1,0:T(8,128)(2,1)} %multiply_convert_fusion), calls=%async_computation.1 | async-start | bytes 2097152 | tf_op jit(solution)/shard_map/all_to_all | solution.py:173
  57.7 4.0 %collective-permute-start.1 = (bf16[32,2048]{1,0:T(8,128)(2,1)S(1)}, bf16[32,2048]{1,0:T(8,128)(2,1)S(1)}, u32[]{:S(2)}, u32[]{:S(2)}) collective-permute-start(bf16[32,2048]{1,0:T(8,128)(2,1)S(1)} %get-tuple-element.23), channel_id=1, source_target_pairs={{0,32},{16,48},{32,0},{48,16},{1,33},{17,49},{33,1},{49,17},{2,34}... | collective-permute-start | bytes 393224 | tf_op jit(solution)/shard_map/ppermute | solution.py:151
  62.5 14.4 %collective-permute-done = bf16[32,2048]{1,0:T(8,128)(2,1)S(1)} collective-permute-done((bf16[32,2048]{1,0:T(8,128)(2,1)S(1)}, bf16[32,2048]{1,0:T(8,128)(2,1)S(1)}, u32[]{:S(2)}, u32[]{:S(2)}) %collective-permute-start) | collective-permute-done | bytes 131104 | tf_op jit(solution)/shard_map/ppermute | solution.py:151
  77.1 2.9 %collective-permute-start.4 = (bf16[128,2048]{1,0:T(8,128)(2,1)S(1)}, bf16[128,2048]{1,0:T(8,128)(2,1)S(1)}, u32[]{:S(2)}, u32[]{:S(2)}) collective-permute-start(bf16[128,2048]{1,0:T(8,128)(2,1)S(1)} %pad_maximum_fusion.1.own), channel_id=1, source_target_pairs={{0,192},{64,0},{128,64},{192,128},{1,193},{65,1},{129,65},{193,129... | collective-permute-start | bytes 1572872 | tf_op jit(solution)/shard_map/ppermute | solution.py:166
  80.0 6.3 %collective-permute-done.3.fwd = bf16[128,2048]{1,0:T(8,128)(2,1)S(1)} collective-permute-done((bf16[128,2048]{1,0:T(8,128)(2,1)S(1)}, bf16[128,2048]{1,0:T(8,128)(2,1)S(1)}, u32[]{:S(2)}, u32[]{:S(2)}) %collective-permute-start.3) | collective-permute-done | bytes 524320 | tf_op jit(solution)/shard_map/ppermute | solution.py:165
  86.5 2.9 %collective-permute-start.6 = (bf16[64,2048]{1,0:T(8,128)(2,1)S(1)}, bf16[64,2048]{1,0:T(8,128)(2,1)S(1)}, u32[]{:S(2)}, u32[]{:S(2)}) collective-permute-start(bf16[64,2048]{1,0:T(8,128)(2,1)S(1)} %slice.35), channel_id=1, source_target_pairs={{0,192},{64,0},{128,64},{192,128},{1,193},{65,1},{129,65},{193,129... | collective-permute-start | bytes 786440 | tf_op jit(solution)/shard_map/ppermute | solution.py:168
  89.4 5.9 %collective-permute-done.5.far_a = bf16[64,2048]{1,0:T(8,128)(2,1)S(1)} collective-permute-done((bf16[64,2048]{1,0:T(8,128)(2,1)S(1)}, bf16[64,2048]{1,0:T(8,128)(2,1)S(1)}, u32[]{:S(2)}, u32[]{:S(2)}) %collective-permute-start.5) | collective-permute-done | bytes 262176 | tf_op jit(solution)/shard_map/ppermute | solution.py:167
  97.5 3.5 %shard_map.59 = (f32[8,512,128]{2,1,0:T(8,128)S(1)}, bf16[512,128]{1,0:T(8,128)(2,1)S(1)}) custom-call(s32[3]{0:T(128)S(1)} %pad_add_fusion.ids, bf16[128,2048]{1,0:T(8,128)(2,1)S(1)} %pad_maximum_fusion.1.own, bf16[128,2048]{1,0:T(8,128)(2,1)S(1)} %collective-permute-done.3.fwd, bf16[128,2048]{1,0:T(8,128)(2,1)S(1)} %collective-permute-done.4.bwd, ...), custom_call_target="tpu_custom_call" | custom-call | flops 2415919104 | bytes 12582912 | tf_op jit(solution)/shard_map/pallas_call | solution.py:44
  102.3 4.7 %all-to-all-start = ((f16[8,512,128]{2,1,0:T(8,128)(2,1)}), f16[8,512,128]{2,1,0:T(8,128)(2,1)S(1)}, u32[]{:S(2)}, u32[]{:S(2)}) async-start(f16[8,512,128]{2,1,0:T(8,128)(2,1)} %multiply_convert_fusion.1), calls=%async_computation | async-start | bytes 2097152 | tf_op jit(solution)/shard_map/all_to_all | solution.py:173
  107.7 7.8 %collective-permute-start.18 = (bf16[512,128]{1,0:T(8,128)(2,1)S(1)}, bf16[512,128]{1,0:T(8,128)(2,1)S(1)}, u32[]{:S(2)}, u32[]{:S(2)}) collective-permute-start(bf16[512,128]{1,0:T(8,128)(2,1)S(1)} %collective-permute-done.17.mine), channel_id=1, source_target_pairs={{0,8},{8,0},{1,9},{9,1},{2,10},{10,2},{3,11},{11,3},{4,12},{12,4},... | collective-permute-start | bytes 393224 | tf_op jit(solution)/shard_map/ppermute | solution.py:171
  117.7 17.1 %all-to-all-start.3 = ((f32[8,64,256]{2,1,0:T(8,128)}), f32[8,64,256]{2,1,0:T(8,128)S(1)}, u32[]{:S(2)}, u32[]{:S(2)}) async-start(f32[8,64,256]{2,1,0:T(8,128)} %get-tuple-element.21), calls=%async_computation.3 | async-start | bytes 1048576 | tf_op jit(solution)/shard_map/all_to_all | solution.py:178
  138.5 4.6 %all-to-all-done.3 = f32[8,64,256]{2,1,0:T(8,128)S(1)} async-done(((f32[8,64,256]{2,1,0:T(8,128)}), f32[8,64,256]{2,1,0:T(8,128)S(1)}, u32[]{:S(2)}, u32[]{:S(2)}) %all-to-all-start.3) | async-done | bytes 524320 | tf_op jit(solution)/shard_map/all_to_all | solution.py:178
  143.0 17.9 %all-to-all-start.2 = ((f32[8,64,256]{2,1,0:T(8,128)}), f32[8,64,256]{2,1,0:T(8,128)S(1)}, u32[]{:S(2)}, u32[]{:S(2)}) async-start(f32[8,64,256]{2,1,0:T(8,128)} %get-tuple-element.20), calls=%async_computation.2 | async-start | bytes 1048576 | tf_op jit(solution)/shard_map/all_to_all | solution.py:178
  161.0 8.2 %all-to-all-done.2 = f32[8,64,256]{2,1,0:T(8,128)S(1)} async-done(((f32[8,64,256]{2,1,0:T(8,128)}), f32[8,64,256]{2,1,0:T(8,128)S(1)}, u32[]{:S(2)}, u32[]{:S(2)}) %all-to-all-start.2) | async-done | bytes 524320 | tf_op jit(solution)/shard_map/all_to_all | solution.py:178
  170.0 18.8 %all-to-all-start.4 = ((f32[16,2,8,128]{3,2,1,0:T(8,128)}), f32[16,2,8,128]{3,2,1,0:T(8,128)S(1)}, u32[]{:S(2)}, u32[]{:S(2)}) async-start(f32[16,2,8,128]{3,2,1,0:T(8,128)} %copy.12), calls=%async_computation.4 | async-start | bytes 262144 | tf_op jit(solution)/shard_map/all_to_all | solution.py:184
  191.2 7.6 %all-to-all-done.4 = f32[16,2,8,128]{3,2,1,0:T(8,128)S(1)} async-done(((f32[16,2,8,128]{3,2,1,0:T(8,128)}), f32[16,2,8,128]{3,2,1,0:T(8,128)S(1)}, u32[]{:S(2)}, u32[]{:S(2)}) %all-to-all-start.4) | async-done | bytes 131104 | tf_op jit(solution)/shard_map/all_to_all | solution.py:184
  198.8 3.1 %collective-permute-start.21 = (f32[8,128]{1,0:T(8,128)S(1)}, f32[8,128]{1,0:T(8,128)S(1)}, u32[]{:S(2)}, u32[]{:S(2)}) collective-permute-start(f32[8,128]{1,0:T(8,128)S(1)} %slice_bitcast_fusion.2), channel_id=1, source_target_pairs={{0,8},{8,0},{1,9},{9,1},{2,10},{10,2},{3,11},{11,3},{4,12},{12,4},... | collective-permute-start | bytes 12296 | tf_op jit(solution)/shard_map/ppermute | solution.py:185
  (80 shorter events, 33.2 us)
Async XLA Ops:
  0.6 41.9 %collective-permute-start.7 = (bf16[512,2048]{1,0:T(8,128)(2,1)}, bf16[512,2048]{1,0:T(8,128)(2,1)}, u32[]{:S(2)}, u32[]{:S(2)}) collective-permute-start(bf16[512,2048]{1,0:T(8,128)(2,1)} %param.4), channel_id=1, source_target_pairs={{0,8},{8,0},{1,9},{9,1},{2,10},{10,2},{3,11},{11,3},{4,12},{12,4},... | collective-permute-start | bytes 6291464 | tf_op jit(solution)/shard_map/ppermute | solution.py:153
  5.9 8.9 %collective-permute-start.10 = (bf16[32,2048]{1,0:T(8,128)(2,1)S(1)}, bf16[32,2048]{1,0:T(8,128)(2,1)S(1)}, u32[]{:S(2)}, u32[]{:S(2)}) collective-permute-start(bf16[32,2048]{1,0:T(8,128)(2,1)S(1)} %get-tuple-element.22), channel_id=1, source_target_pairs={{0,16},{16,32},{32,48},{48,0},{1,17},{17,33},{33,49},{49,1},{2,18}... | collective-permute-start | bytes 393224 | tf_op jit(solution)/shard_map/ppermute | solution.py:151
  7.2 14.3 %collective-permute-start.11 = (bf16[32,2048]{1,0:T(8,128)(2,1)S(1)}, bf16[32,2048]{1,0:T(8,128)(2,1)S(1)}, u32[]{:S(2)}, u32[]{:S(2)}) collective-permute-start(bf16[32,2048]{1,0:T(8,128)(2,1)S(1)} %get-tuple-element.22), channel_id=1, source_target_pairs={{0,32},{16,48},{32,0},{48,16},{1,33},{17,49},{33,1},{49,17},{2,34}... | collective-permute-start | bytes 393224 | tf_op jit(solution)/shard_map/ppermute | solution.py:151
  12.4 12.9 %collective-permute-start.12 = (bf16[32,2048]{1,0:T(8,128)(2,1)S(1)}, bf16[32,2048]{1,0:T(8,128)(2,1)S(1)}, u32[]{:S(2)}, u32[]{:S(2)}) collective-permute-start(bf16[32,2048]{1,0:T(8,128)(2,1)S(1)} %get-tuple-element.22), channel_id=1, source_target_pairs={{0,48},{16,0},{32,16},{48,32},{1,49},{17,1},{33,17},{49,33},{2,50}... | collective-permute-start | bytes 393224 | tf_op jit(solution)/shard_map/ppermute | solution.py:151
  25.3 14.3 %collective-permute-start.13 = (bf16[128,2048]{1,0:T(8,128)(2,1)S(1)}, bf16[128,2048]{1,0:T(8,128)(2,1)S(1)}, u32[]{:S(2)}, u32[]{:S(2)}) collective-permute-start(bf16[128,2048]{1,0:T(8,128)(2,1)S(1)} %pad_maximum_fusion.2.own), channel_id=1, source_target_pairs={{0,64},{64,128},{128,192},{192,0},{1,65},{65,129},{129,193},{193,1... | collective-permute-start | bytes 1572872 | tf_op jit(solution)/shard_map/ppermute | solution.py:165
  26.6 13.1 %collective-permute-start.14 = (bf16[128,2048]{1,0:T(8,128)(2,1)S(1)}, bf16[128,2048]{1,0:T(8,128)(2,1)S(1)}, u32[]{:S(2)}, u32[]{:S(2)}) collective-permute-start(bf16[128,2048]{1,0:T(8,128)(2,1)S(1)} %pad_maximum_fusion.2.own), channel_id=1, source_target_pairs={{0,192},{64,0},{128,64},{192,128},{1,193},{65,1},{129,65},{193,129... | collective-permute-start | bytes 1572872 | tf_op jit(solution)/shard_map/ppermute | solution.py:166
  39.6 7.7 %collective-permute-start.15 = (bf16[64,2048]{1,0:T(8,128)(2,1)S(1)}, bf16[64,2048]{1,0:T(8,128)(2,1)S(1)}, u32[]{:S(2)}, u32[]{:S(2)}) collective-permute-start(bf16[64,2048]{1,0:T(8,128)(2,1)S(1)} %slice.37), channel_id=1, source_target_pairs={{0,64},{64,128},{128,192},{192,0},{1,65},{65,129},{129,193},{193,1... | collective-permute-start | bytes 786440 | tf_op jit(solution)/shard_map/ppermute | solution.py:167
  39.8 7.6 %collective-permute-start.16 = (bf16[64,2048]{1,0:T(8,128)(2,1)S(1)}, bf16[64,2048]{1,0:T(8,128)(2,1)S(1)}, u32[]{:S(2)}, u32[]{:S(2)}) collective-permute-start(bf16[64,2048]{1,0:T(8,128)(2,1)S(1)} %slice.38), channel_id=1, source_target_pairs={{0,192},{64,0},{128,64},{192,128},{1,193},{65,1},{129,65},{193,129... | collective-permute-start | bytes 786440 | tf_op jit(solution)/shard_map/ppermute | solution.py:168
  52.2 50.1 %all-to-all-start.1 = ((f16[8,512,128]{2,1,0:T(8,128)(2,1)}), f16[8,512,128]{2,1,0:T(8,128)(2,1)S(1)}, u32[]{:S(2)}, u32[]{:S(2)}) async-start(f16[8,512,128]{2,1,0:T(8,128)(2,1)} %multiply_convert_fusion), calls=%async_computation.1 | async-start | bytes 2097152 | tf_op jit(solution)/shard_map/all_to_all | solution.py:173
  56.4 20.5 %collective-permute-start = (bf16[32,2048]{1,0:T(8,128)(2,1)S(1)}, bf16[32,2048]{1,0:T(8,128)(2,1)S(1)}, u32[]{:S(2)}, u32[]{:S(2)}) collective-permute-start(bf16[32,2048]{1,0:T(8,128)(2,1)S(1)} %get-tuple-element.23), channel_id=1, source_target_pairs={{0,16},{16,32},{32,48},{48,0},{1,17},{17,33},{33,49},{49,1},{2,18}... | collective-permute-start | bytes 393224 | tf_op jit(solution)/shard_map/ppermute | solution.py:151
  57.7 19.1 %collective-permute-start.1 = (bf16[32,2048]{1,0:T(8,128)(2,1)S(1)}, bf16[32,2048]{1,0:T(8,128)(2,1)S(1)}, u32[]{:S(2)}, u32[]{:S(2)}) collective-permute-start(bf16[32,2048]{1,0:T(8,128)(2,1)S(1)} %get-tuple-element.23), channel_id=1, source_target_pairs={{0,32},{16,48},{32,0},{48,16},{1,33},{17,49},{33,1},{49,17},{2,34}... | collective-permute-start | bytes 393224 | tf_op jit(solution)/shard_map/ppermute | solution.py:151
  61.8 15.1 %collective-permute-start.2 = (bf16[32,2048]{1,0:T(8,128)(2,1)S(1)}, bf16[32,2048]{1,0:T(8,128)(2,1)S(1)}, u32[]{:S(2)}, u32[]{:S(2)}) collective-permute-start(bf16[32,2048]{1,0:T(8,128)(2,1)S(1)} %get-tuple-element.23), channel_id=1, source_target_pairs={{0,48},{16,0},{32,16},{48,32},{1,49},{17,1},{33,17},{49,33},{2,50}... | collective-permute-start | bytes 393224 | tf_op jit(solution)/shard_map/ppermute | solution.py:151
  76.9 9.4 %collective-permute-start.3 = (bf16[128,2048]{1,0:T(8,128)(2,1)S(1)}, bf16[128,2048]{1,0:T(8,128)(2,1)S(1)}, u32[]{:S(2)}, u32[]{:S(2)}) collective-permute-start(bf16[128,2048]{1,0:T(8,128)(2,1)S(1)} %pad_maximum_fusion.1.own), channel_id=1, source_target_pairs={{0,64},{64,128},{128,192},{192,0},{1,65},{65,129},{129,193},{193,1... | collective-permute-start | bytes 1572872 | tf_op jit(solution)/shard_map/ppermute | solution.py:165
  77.1 9.4 %collective-permute-start.4 = (bf16[128,2048]{1,0:T(8,128)(2,1)S(1)}, bf16[128,2048]{1,0:T(8,128)(2,1)S(1)}, u32[]{:S(2)}, u32[]{:S(2)}) collective-permute-start(bf16[128,2048]{1,0:T(8,128)(2,1)S(1)} %pad_maximum_fusion.1.own), channel_id=1, source_target_pairs={{0,192},{64,0},{128,64},{192,128},{1,193},{65,1},{129,65},{193,129... | collective-permute-start | bytes 1572872 | tf_op jit(solution)/shard_map/ppermute | solution.py:166
  86.3 8.9 %collective-permute-start.5 = (bf16[64,2048]{1,0:T(8,128)(2,1)S(1)}, bf16[64,2048]{1,0:T(8,128)(2,1)S(1)}, u32[]{:S(2)}, u32[]{:S(2)}) collective-permute-start(bf16[64,2048]{1,0:T(8,128)(2,1)S(1)} %slice.34), channel_id=1, source_target_pairs={{0,64},{64,128},{128,192},{192,0},{1,65},{65,129},{129,193},{193,1... | collective-permute-start | bytes 786440 | tf_op jit(solution)/shard_map/ppermute | solution.py:167
  86.5 8.8 %collective-permute-start.6 = (bf16[64,2048]{1,0:T(8,128)(2,1)S(1)}, bf16[64,2048]{1,0:T(8,128)(2,1)S(1)}, u32[]{:S(2)}, u32[]{:S(2)}) collective-permute-start(bf16[64,2048]{1,0:T(8,128)(2,1)S(1)} %slice.35), channel_id=1, source_target_pairs={{0,192},{64,0},{128,64},{192,128},{1,193},{65,1},{129,65},{193,129... | collective-permute-start | bytes 786440 | tf_op jit(solution)/shard_map/ppermute | solution.py:168
  102.3 15.4 %all-to-all-start = ((f16[8,512,128]{2,1,0:T(8,128)(2,1)}), f16[8,512,128]{2,1,0:T(8,128)(2,1)S(1)}, u32[]{:S(2)}, u32[]{:S(2)}) async-start(f16[8,512,128]{2,1,0:T(8,128)(2,1)} %multiply_convert_fusion.1), calls=%async_computation | async-start | bytes 2097152 | tf_op jit(solution)/shard_map/all_to_all | solution.py:173
  107.7 8.7 %collective-permute-start.18 = (bf16[512,128]{1,0:T(8,128)(2,1)S(1)}, bf16[512,128]{1,0:T(8,128)(2,1)S(1)}, u32[]{:S(2)}, u32[]{:S(2)}) collective-permute-start(bf16[512,128]{1,0:T(8,128)(2,1)S(1)} %collective-permute-done.17.mine), channel_id=1, source_target_pairs={{0,8},{8,0},{1,9},{9,1},{2,10},{10,2},{3,11},{11,3},{4,12},{12,4},... | collective-permute-start | bytes 393224 | tf_op jit(solution)/shard_map/ppermute | solution.py:171
  117.7 25.3 %all-to-all-start.3 = ((f32[8,64,256]{2,1,0:T(8,128)}), f32[8,64,256]{2,1,0:T(8,128)S(1)}, u32[]{:S(2)}, u32[]{:S(2)}) async-start(f32[8,64,256]{2,1,0:T(8,128)} %get-tuple-element.21), calls=%async_computation.3 | async-start | bytes 1048576 | tf_op jit(solution)/shard_map/all_to_all | solution.py:178
  143.0 26.1 %all-to-all-start.2 = ((f32[8,64,256]{2,1,0:T(8,128)}), f32[8,64,256]{2,1,0:T(8,128)S(1)}, u32[]{:S(2)}, u32[]{:S(2)}) async-start(f32[8,64,256]{2,1,0:T(8,128)} %get-tuple-element.20), calls=%async_computation.2 | async-start | bytes 1048576 | tf_op jit(solution)/shard_map/all_to_all | solution.py:178
  170.0 28.8 %all-to-all-start.4 = ((f32[16,2,8,128]{3,2,1,0:T(8,128)}), f32[16,2,8,128]{3,2,1,0:T(8,128)S(1)}, u32[]{:S(2)}, u32[]{:S(2)}) async-start(f32[16,2,8,128]{3,2,1,0:T(8,128)} %copy.12), calls=%async_computation.4 | async-start | bytes 262144 | tf_op jit(solution)/shard_map/all_to_all | solution.py:184
  188.8 13.1 %collective-permute-start.20 = (f32[2,128,128]{2,1,0:T(8,128)S(1)}, f32[2,128,128]{2,1,0:T(8,128)S(1)}, u32[]{:S(2)}, u32[]{:S(2)}) collective-permute-start(f32[2,128,128]{2,1,0:T(8,128)S(1)} %get-tuple-element.19), channel_id=1, source_target_pairs={{0,8},{8,0},{1,9},{9,1},{2,10},{10,2},{3,11},{11,3},{4,12},{12,4},... | collective-permute-start | bytes 393224 | tf_op jit(solution)/shard_map/ppermute | solution.py:177
  191.1 10.9 %collective-permute-start.19 = (f32[2,128,128]{2,1,0:T(8,128)S(1)}, f32[2,128,128]{2,1,0:T(8,128)S(1)}, u32[]{:S(2)}, u32[]{:S(2)}) collective-permute-start(f32[2,128,128]{2,1,0:T(8,128)S(1)} %get-tuple-element.18), channel_id=1, source_target_pairs={{0,8},{8,0},{1,9},{9,1},{2,10},{10,2},{3,11},{11,3},{4,12},{12,4},... | collective-permute-start | bytes 393224 | tf_op jit(solution)/shard_map/ppermute | solution.py:177
  198.8 4.7 %collective-permute-start.21 = (f32[8,128]{1,0:T(8,128)S(1)}, f32[8,128]{1,0:T(8,128)S(1)}, u32[]{:S(2)}, u32[]{:S(2)}) collective-permute-start(f32[8,128]{1,0:T(8,128)S(1)} %slice_bitcast_fusion.2), channel_id=1, source_target_pairs={{0,8},{8,0},{1,9},{9,1},{2,10},{10,2},{3,11},{11,3},{4,12},{12,4},... | collective-permute-start | bytes 12296 | tf_op jit(solution)/shard_map/ppermute | solution.py:185
  (7 other events, 96.9 us)

commit v2 on v0

v2 whole, which is shorter than its diff:
```python
import functools

import jax
import jax.numpy as jnp
from jax import lax
from jax.experimental import pallas as pl
from jax.experimental.pallas import tpu as pltpu
from jax.sharding import Mesh, PartitionSpec as P

GROUPS = ((0,), (1, 3, 2))
SCALE = 64.0
NT = (((1,), (1,)), ((), ()))
VMEM = pl.BlockSpec(memory_space=pltpu.VMEM)
ANY = pl.BlockSpec(memory_space=pl.ANY)
SMEM = pl.BlockSpec(memory_space=pltpu.SMEM)


def mask_kernel(ids, mask, panel, own, pieces):
    ic, col = ids[2], ids[3]
    upper = lax.broadcasted_iota(jnp.int32, (16, 256), 0) < 8
    low = lax.broadcasted_iota(jnp.int32, (16, 128), 1) < 64
    for t in range(4):
        rows = slice(16 * t, 16 * t + 16)
        blocks = []
        for i in range(8):
            lanes = slice(256 * i, 256 * i + 256)
            here = jnp.where(upper, mask[2 * t, col * 8 + i], mask[2 * t + 1, col * 8 + i]).astype(jnp.float32)
            blocks.append(panel[rows, lanes].astype(jnp.float32) * here)
            own[rows, lanes] = blocks[-1].astype(own.dtype)
        for b in range(2):
            for h in range(2):
                even, odd = blocks[4 * b + h], blocks[4 * b + 2 + h]
                first, second = jnp.where(ic == 0, even, odd), jnp.where(ic == 0, odd, even)
                for u in range(2):
                    p, q = first[:, 128 * u:128 * u + 128], second[:, 128 * u:128 * u + 128]
                    j = 4 * h + 2 * u
                    pieces[j, b, rows, :] = jnp.where(low, p, pltpu.roll(q, 64, 1)).astype(pieces.dtype)
                    pieces[j + 1, b, rows, :] = jnp.where(low, pltpu.roll(p, 64, 1), q).astype(pieces.dtype)


def mask_call(ids, mask, panel):
    return pl.pallas_call(
        mask_kernel,
        out_shape=(
            jax.ShapeDtypeStruct((64, 2048), jnp.bfloat16),
            jax.ShapeDtypeStruct((8, 2, 64, 128), jnp.bfloat16),
        ),
        in_specs=[SMEM, SMEM, VMEM],
        out_specs=(VMEM, VMEM),
        compiler_params=pltpu.CompilerParams(vmem_limit_bytes=16 * 2**20),
        cost_estimate=pl.CostEstimate(flops=1, bytes_accessed=2**20, transcendentals=0),
    )(ids, mask, panel)


def product_kernel(places, size, ids, *refs):
    count = len(places)
    slabs, (root, other_root, out, gathered, pair) = refs[:count], refs[count:]

    @pl.when(pl.program_id(0) == 0)
    def _():
        for slab, (shift, skip) in zip(slabs, places):
            start = pl.multiple_of(lax.rem(ids[0] + shift, 4) * size + skip, 16)
            gathered[pl.ds(start, slab.shape[0]), :] = slab[...]

    for j in range(2):
        pair[128 * j:128 * j + 64, :] = root[64 * j:64 * j + 64, :]
        pair[128 * j + 64:128 * j + 128, :] = other_root[64 * j:64 * j + 64, :]
    prod = lax.dot_general(gathered[...], pair[...], NT, preferred_element_type=jnp.float32)
    out[0] = prod[:, 0:128] * SCALE
    out[1] = prod[:, 128:256] * SCALE


def product_call(ids, slabs, places, size, root, other_root):
    n = 4 * size
    return pl.pallas_call(
        functools.partial(product_kernel, places, size),
        grid=(4,),
        out_shape=jax.ShapeDtypeStruct((8, n, 128), jnp.float32),
        in_specs=[SMEM] + [pl.BlockSpec(slab.shape, lambda t: (0, 0)) for slab in slabs]
        + [pl.BlockSpec((128, 2048), lambda t: (t, 0))] * 2,
        out_specs=pl.BlockSpec((2, n, 128), lambda t: (t, 0, 0)),
        scratch_shapes=[pltpu.VMEM((n, 2048), jnp.bfloat16), pltpu.VMEM((256, 2048), jnp.bfloat16)],
        compiler_params=pltpu.CompilerParams(vmem_limit_bytes=24 * 2**20),
        cost_estimate=pl.CostEstimate(flops=2 * n * 2048 * 1024, bytes_accessed=2 * n * 2048 + 6 * 2**20, transcendentals=0),
    )(ids, *slabs, root, other_root)


def diag_kernel(ids, *refs):
    count = len(GROUPS)
    products, (mine, other, keep, give, diag) = refs[:count], refs[count:]
    iz = ids[1]
    low = lax.broadcasted_iota(jnp.int32, (8, 128), 1) < 64
    left = mine[...].astype(jnp.float32).reshape(16, 8, 8, 128)
    right = pltpu.roll(other[...].astype(jnp.float32), 64, 2).reshape(16, 8, 8, 128)
    totals, places = [], []
    for product, group in zip(products, GROUPS):
        total = product[...].reshape(4, len(group), 8, 8, 128)
        for q, s in enumerate(group):
            z = lax.rem(iz + 4 - s, 4)
            for x in range(4):
                totals.append(total[x, q])
                places.append((x, z))
                for t in range(4):
                    even, odd = total[x, q, 2 * t], total[x, q, 2 * t + 1]
                    keep[t, x, z] = -jnp.where(low, even, pltpu.roll(odd, 64, 1))
                    give[t, x, z] = -jnp.where(low, pltpu.roll(even, 64, 1), odd)
    for k in range(8):
        p = jnp.concatenate([total[k] for total in totals], axis=0)
        hi = p.astype(jnp.bfloat16)
        rest = p - hi.astype(jnp.float32)
        mid = rest.astype(jnp.bfloat16)
        lo = (rest - mid.astype(jnp.float32)).astype(jnp.bfloat16)
        m = jnp.concatenate([left[:, k].reshape(128, 128), right[:, k].reshape(128, 128)], axis=0).astype(jnp.bfloat16)
        d = lax.dot_general(lo, m, NT, preferred_element_type=jnp.float32)
        d += lax.dot_general(mid, m, NT, preferred_element_type=jnp.float32)
        d += lax.dot_general(hi, m, NT, preferred_element_type=jnp.float32)
        for i, (x, z) in enumerate(places):
            diag[2 * x + z // 2, k, lax.rem(z, 2)] = d[i * 8:(i + 1) * 8, :]


def diag_call(ids, products, mine, other):
    return pl.pallas_call(
        diag_kernel,
        out_shape=(
            jax.ShapeDtypeStruct((4, 4, 4, 8, 128), jnp.float32),
            jax.ShapeDtypeStruct((4, 4, 4, 8, 128), jnp.float32),
            jax.ShapeDtypeStruct((8, 8, 2, 8, 256), jnp.float32),
        ),
        in_specs=[SMEM] + [VMEM] * (len(GROUPS) + 2),
        out_specs=(VMEM,) * 3,
        compiler_params=pltpu.CompilerParams(vmem_limit_bytes=16 * 2**20),
        cost_estimate=pl.CostEstimate(flops=2 * 8 * 3 * 128 * 128 * 256, bytes_accessed=2**23, transcendentals=0),
    )(ids, *products, mine, other)


def rows_kernel(ids, keep, got, out):
    first = ids[2] == 0
    for t in range(4):
        a, b = keep[t].reshape(16, 1, 8, 128), got[t].reshape(16, 1, 8, 128)
        even, odd = jnp.where(first, a, b), jnp.where(first, b, a)
        both = jnp.concatenate([even, odd], axis=1).reshape(256, 128).T
        out[:, 2 * t, :] = both[0:64, :]
        out[:, 2 * t + 1, :] = both[64:128, :]


def rows_call(ids, keep, got):
    return pl.pallas_call(
        rows_kernel,
        out_shape=jax.ShapeDtypeStruct((64, 8, 256), jnp.float32),
        in_specs=[SMEM, VMEM, VMEM],
        out_specs=VMEM,
        compiler_params=pltpu.CompilerParams(vmem_limit_bytes=16 * 2**20),
        cost_estimate=pl.CostEstimate(flops=0, bytes_accessed=2**20, transcendentals=0),
    )(ids, keep, got)


def pin(values):
    return lax.optimization_barrier(values)


def turn(size, shift):
    return [(i, (i + shift) % size) for i in range(size)]


def shards(inverse_root, panel, block_mask, diag_inverse):
    ix, iz, ic = lax.axis_index("x"), lax.axis_index("zh"), lax.axis_index("core")
    col = lax.axis_index("zl") * 4 + lax.axis_index("y")
    ids = jnp.stack([ix, iz, ic, col]).astype(jnp.int32)
    swap = [(0, 1), (1, 0)]

    def sum_parts(parts):
        return jnp.sum(parts.astype(jnp.float32), axis=0) * (1.0 / SCALE)

    def send_parts(partial):
        return partial.astype(jnp.float16)

    def around(slab):
        return [lax.ppermute(slab, "x", turn(4, 1)), lax.ppermute(slab, "x", turn(4, -1))]

    def to_columns(value):
        return lax.all_to_all(value, ("zl", "y"), 0, 0, tiled=True)

    def to_rows(value):
        return lax.all_to_all(value, ("x", "zh"), 0, 0, tiled=True)

    other_root = lax.ppermute(inverse_root, "core", swap)
    own, pieces = mask_call(ids, block_mask, jnp.transpose(panel, (1, 2, 0)).reshape(64, 2048))

    z1, z3 = (lax.ppermute(own, "zh", turn(4, s)) for s in (1, 3))
    near0, pieces = pin((around(own), pieces))
    far0 = lax.ppermute(near0[0], "x", turn(4, 1))
    pieces = to_columns(pieces)
    z1, z3, near0, far0, own, other_root = pin((z1, z3, near0, far0, own, other_root))

    z2 = lax.ppermute(own, "zh", turn(4, 2))
    near1, near3 = around(z1), around(z3)
    sent0 = send_parts(
        product_call(ids, [own, *near0, far0], [(0, 0), (3, 0), (1, 0), (2, 0)], 64, inverse_root, other_root)
    )
    z2, near1, near3, pieces, sent0 = pin((z2, near1, near3, pieces, sent0))

    far1, far3 = lax.ppermute(near1[0], "x", turn(4, 1)), lax.ppermute(near3[1], "x", turn(4, -1))
    near2 = around(z2)
    far1, sent0 = pin((far1, sent0))
    parts0 = to_columns(sent0)
    far1, far3, near2 = pin((far1, far3, near2))

    far2 = [lax.ppermute(near2[0][:32], "x", turn(4, 1)), lax.ppermute(near2[1][32:], "x", turn(4, -1))]
    far2, pieces, parts0 = pin((far2, pieces, parts0))

    sent1 = send_parts(product_call(
        ids,
        [z1, *near1, far1, z3, *near3, far3, z2, *near2, *far2],
        [(0, 0), (3, 0), (1, 0), (2, 0), (0, 64), (3, 64), (1, 64), (2, 64), (0, 128), (3, 128), (1, 128), (2, 128), (2, 160)],
        192, inverse_root, other_root,
    ))
    parts1 = to_columns(sent1)
    mine = to_rows(pieces.reshape(16, 64, 128))
    other = lax.ppermute(mine, "core", swap)
    products = [sum_parts(parts0), sum_parts(parts1)]

    keep, give, diag = diag_call(ids, products, mine, other)
    got = lax.ppermute(give, "core", swap)
    here = jnp.sum(to_columns(diag), axis=0)
    panel_inverse = rows_call(ids, keep, got)
    here, panel_inverse = lax.optimization_barrier((here, panel_inverse))
    across = here.reshape(128, 256).T.reshape(2, 16, 8, 128)
    across = jnp.transpose(across, (1, 0, 2, 3))
    here = jnp.sum(to_rows(across), axis=0)
    came = lax.ppermute(here[1], "core", swap)
    even, odd = jnp.where(ic == 0, here[0], came), jnp.where(ic == 0, came, here[0])
    both = jnp.stack([even.reshape(8, 8, 2, 8), odd.reshape(8, 8, 2, 8)], axis=3)
    block = jnp.transpose(both, (1, 0, 2, 3, 4)).reshape(8, 8, 32)
    return panel_inverse, diag_inverse + block


def solution(mesh):
    wide = Mesh(mesh.devices.reshape(4, 4, 2, 2, 4), ("x", "zh", "core", "zl", "y"))
    prow, pcol = ("x", "zh", "core"), ("zl", "y")
    in_specs = (P(prow, pcol), P(pcol, None, prow), P(), P(None, prow, pcol))
    out_specs = (P(prow + pcol, None, None), P(None, prow, pcol))
    return jax.shard_map(shards, mesh=wide, in_specs=in_specs, out_specs=out_specs, check_vma=False)
```

time: 409 us -> 162 us (0.40)
  waiting for transfers between devices: 332 us -> 44.7 us
  starting transfers between devices: 0.21 us -> 66.7 us
  local copies, waits for them, and re-layouts: 38.8 us -> 9.34 us
  blocking collectives: 0 us -> 20.1 us
  Pallas kernels: 0 us -> 13.6 us
  matrix products: 13.3 us -> 0 us
  between operations: 13.9 us -> 0.85 us
    reduce_scatter x3 -> x0, waiting for transfers between devices: 193 us -> none  [the longest x1 91.7 us: shards(): summed = lax.psum_scatter(by_cols, 'prow', scatter_dimension=1, tiled=True)]
    all_gather x1 -> x0, waiting for transfers between devices: 81.3 us -> none  [shards(): column_panel = lax.all_gather(panel, 'prow', axis=2, tiled=True)]
    psum x1 -> x0, waiting for transfers between devices: 57.8 us -> none  [spread(): return lax.psum(block, axis)]
    ppermute x0 -> x20, starting transfers between devices: none -> 37.2 us  [the longest x4 9.32 us: around(): lax.ppermute(slab, 'x', turn(4, -1))]
    all_to_all x0 -> x5, starting transfers between devices: none -> 29.5 us  [the longest x4 22.9 us: to_columns(): return lax.all_to_all(value, ('zl', 'y'), 0, 0, tiled=True)]
    ppermute x0 -> x20, waiting for transfers between devices: none -> 29.2 us  [the longest x1 6.64 us: shards(): lax.ppermute(near1[0], 'x', turn(4, 1))]
    all_to_all x0 -> x1, blocking collectives: none -> 20.1 us  [to_rows(): return lax.all_to_all(value, ('x', 'zh'), 0, 0, tiled=True)]
    all_to_all x0 -> x5, waiting for transfers between devices: none -> 15.6 us  [the longest x4 15 us: to_columns(): return lax.all_to_all(value, ('zl', 'y'), 0, 0, tiled=True)]
  transfers between devices with their start and end apart: 5 -> 25, of which waited for: 5 -> 14; matrix products, arithmetic and copies ran while one was open for 7% -> 3% of each run, Pallas kernels for 0% -> 7%
where the time goes in v2:
time: 162 us; the launch traced here: 161 us
  starting transfers between devices  66.7 us (41%)
  waiting for transfers between devices  44.7 us (28%)
  blocking collectives  20.1 us (12%)
  Pallas kernels  13.6 us (8%)
  local copies, waits for them, and re-layouts  9.34 us (6%)
  other arithmetic  5.96 us (4%)
    all_to_all x4, starting transfers between devices, to_columns(): return lax.all_to_all(value, ('zl', 'y'), 0, 0, tiled=True)  22.9 us
    all_to_all x1, blocking collectives, to_rows(): return lax.all_to_all(value, ('x', 'zh'), 0, 0, tiled=True)  20.1 us
    all_to_all x4, waiting for transfers between devices, to_columns(): return lax.all_to_all(value, ('zl', 'y'), 0, 0, tiled=True)  15 us
    ppermute x4, starting transfers between devices, around(): lax.ppermute(slab, 'x', turn(4, -1))  9.32 us
    unnamed x22, local copies, waits for them, and re-layouts  8.68 us
    pallas_call x2, Pallas kernels, product_call(): pl.pallas_call(functools.partial(product_kernel, places, size), grid=(4,)...  8.33 us
    all_to_all x1, starting transfers between devices, to_rows(): return lax.all_to_all(value, ('x', 'zh'), 0, 0, tiled=True)  6.67 us
    ppermute x1, waiting for transfers between devices, shards(): lax.ppermute(near1[0], 'x', turn(4, 1))  6.64 us
  transfers between devices with their start and end apart: 25, of which 14 were waited for; matrix products, arithmetic and copies ran while one was open for 3% of the time, Pallas kernels for 7%

profile of v2, /device:TPU:1, one launch (start us, length us, event | category | flops | bytes accessed | tf_op | source)
XLA Modules:
  0.0 161.3 jit_solution(7710150228836852712)
XLA Ops:
  0.6 3.3 %collective-permute-start.5 = (bf16[512,2048]{1,0:T(8,128)(2,1)}, bf16[512,2048]{1,0:T(8,128)(2,1)S(1)}, u32[]{:S(2)}, u32[]{:S(2)}) collective-permute-start(bf16[512,2048]{1,0:T(8,128)(2,1)} %refs_13_.1), channel_id=1, source_target_pairs={{0,8},{8,0},{1,9},{9,1},{2,10},{10,2},{3,11},{11,3},{4,12},{12,4},... | collective-permute-start | bytes 6291464 | tf_op jit(solution)/shard_map/ppermute | solution.py:186
  7.1 2.7 %collective-permute-start.3 = (bf16[64,2048]{1,0:T(8,128)(2,1)S(1)}, bf16[64,2048]{1,0:T(8,128)(2,1)S(1)}, u32[]{:S(2)}, u32[]{:S(2)}) collective-permute-start(bf16[64,2048]{1,0:T(8,128)(2,1)S(1)} %get-tuple-element.40.refs_0_), channel_id=1, source_target_pairs={{0,192},{64,0},{128,64},{192,128},{1,193},{65,1},{129,65},{193,129... | collective-permute-start | bytes 786440 | tf_op jit(solution)/shard_map/ppermute | solution.py:178
  11.1 3.0 %collective-permute-start.1 = (bf16[64,2048]{1,0:T(8,128)(2,1)S(1)}, bf16[64,2048]{1,0:T(8,128)(2,1)}, u32[]{:S(2)}, u32[]{:S(2)}) collective-permute-start(bf16[64,2048]{1,0:T(8,128)(2,1)S(1)} %get-tuple-element.40.refs_0_), channel_id=1, source_target_pairs={{0,48},{16,0},{32,16},{48,32},{1,49},{17,1},{33,17},{49,33},{2,50}... | collective-permute-start | bytes 786440 | tf_op jit(solution)/shard_map/ppermute | solution.py:189
  16.3 4.7 %all-to-all-start = ((bf16[8,2,64,128]{3,2,1,0:T(8,128)(2,1)}), bf16[8,2,64,128]{3,2,1,0:T(8,128)(2,1)}, u32[]{:S(2)}, u32[]{:S(2)}) async-start(bf16[8,2,64,128]{3,2,1,0:T(8,128)(2,1)} %get-tuple-element.43), calls=%async_computation | async-start | bytes 524288 | tf_op jit(solution)/shard_map/all_to_all | solution.py:181
  21.8 5.5 %collective-permute-done.1.refs_4_ = bf16[64,2048]{1,0:T(8,128)(2,1)} collective-permute-done((bf16[64,2048]{1,0:T(8,128)(2,1)S(1)}, bf16[64,2048]{1,0:T(8,128)(2,1)}, u32[]{:S(2)}, u32[]{:S(2)}) %collective-permute-start.1) | collective-permute-done | bytes 262176 | tf_op jit(solution)/shard_map/ppermute | solution.py:189
  27.4 3.2 %collective-permute-start.6 = (bf16[64,2048]{1,0:T(8,128)(2,1)S(1)}, bf16[64,2048]{1,0:T(8,128)(2,1)}, u32[]{:S(2)}, u32[]{:S(2)}) collective-permute-start(bf16[64,2048]{1,0:T(8,128)(2,1)S(1)} %get-tuple-element.40.refs_0_), channel_id=1, source_target_pairs={{0,32},{16,48},{32,0},{48,16},{1,33},{17,49},{33,1},{49,17},{2,34}... | collective-permute-start | bytes 786440 | tf_op jit(solution)/shard_map/ppermute | solution.py:195
  30.6 2.7 %collective-permute-start.8 = (bf16[64,2048]{1,0:T(8,128)(2,1)S(1)}, bf16[64,2048]{1,0:T(8,128)(2,1)}, u32[]{:S(2)}, u32[]{:S(2)}) collective-permute-start(bf16[64,2048]{1,0:T(8,128)(2,1)S(1)} %collective-permute-done.refs_0_), channel_id=1, source_target_pairs={{0,192},{64,0},{128,64},{192,128},{1,193},{65,1},{129,65},{193,129... | collective-permute-start | bytes 786440 | tf_op jit(solution)/shard_map/ppermute | solution.py:178
  33.3 2.7 %collective-permute-start.10 = (bf16[64,2048]{1,0:T(8,128)(2,1)}, bf16[64,2048]{1,0:T(8,128)(2,1)}, u32[]{:S(2)}, u32[]{:S(2)}) collective-permute-start(bf16[64,2048]{1,0:T(8,128)(2,1)} %collective-permute-done.1.refs_4_), channel_id=1, source_target_pairs={{0,192},{64,0},{128,64},{192,128},{1,193},{65,1},{129,65},{193,129... | collective-permute-start | bytes 786440 | tf_op jit(solution)/shard_map/ppermute | solution.py:178
  37.5 2.6 %shard_map.60 = f32[8,256,128]{2,1,0:T(8,128)S(1)} custom-call(s32[4]{0:T(128)S(1)} %pad_add_fusion.ids, bf16[64,2048]{1,0:T(8,128)(2,1)S(1)} %get-tuple-element.40.refs_0_, bf16[64,2048]{1,0:T(8,128)(2,1)S(1)} %collective-permute-done.2.refs_1_, bf16[64,2048]{1,0:T(8,128)(2,1)S(1)} %collective-permute-done.3.refs_2_, ...), custom_call_target="tpu_custom_call" | custom-call | flops 1073741824 | bytes 7340032 | tf_op jit(solution)/shard_map/pallas_call | solution.py:75
  43.7 6.6 %collective-permute-done.11.refs_3_ = bf16[64,2048]{1,0:T(8,128)(2,1)S(1)} collective-permute-done((bf16[64,2048]{1,0:T(8,128)(2,1)}, bf16[64,2048]{1,0:T(8,128)(2,1)S(1)}, u32[]{:S(2)}, u32[]{:S(2)}) %collective-permute-start.11) | collective-permute-done | bytes 262176 | tf_op jit(solution)/shard_map/ppermute | solution.py:202
  50.4 6.2 %all-to-all-start.1 = ((f16[8,256,128]{2,1,0:T(8,128)(2,1)}), f16[8,256,128]{2,1,0:T(8,128)(2,1)}, u32[]{:S(2)}, u32[]{:S(2)}) async-start(f16[8,256,128]{2,1,0:T(8,128)(2,1)} %convert_element_type.12), calls=%async_computation.1 | async-start | bytes 1048576 | tf_op jit(solution)/shard_map/all_to_all | solution.py:181
  59.4 2.7 %collective-permute-done.12.refs_7_ = bf16[64,2048]{1,0:T(8,128)(2,1)S(1)} collective-permute-done((bf16[64,2048]{1,0:T(8,128)(2,1)}, bf16[64,2048]{1,0:T(8,128)(2,1)S(1)}, u32[]{:S(2)}, u32[]{:S(2)}) %collective-permute-start.12) | collective-permute-done | bytes 262176 | tf_op jit(solution)/shard_map/ppermute | solution.py:202
  63.6 4.1 %collective-permute-done.14.refs_10_ = bf16[64,2048]{1,0:T(8,128)(2,1)S(1)} collective-permute-done((bf16[64,2048]{1,0:T(8,128)(2,1)}, bf16[64,2048]{1,0:T(8,128)(2,1)S(1)}, u32[]{:S(2)}, u32[]{:S(2)}) %collective-permute-start.14) | collective-permute-done | bytes 262176 | tf_op jit(solution)/shard_map/ppermute | solution.py:178
  68.0 2.7 %collective-permute-start.16 = (bf16[32,2048]{1,0:T(8,128)(2,1)S(1)}, bf16[32,2048]{1,0:T(8,128)(2,1)S(1)}, u32[]{:S(2)}, u32[]{:S(2)}) collective-permute-start(bf16[32,2048]{1,0:T(8,128)(2,1)S(1)} %slice.14), channel_id=1, source_target_pairs={{0,192},{64,0},{128,64},{192,128},{1,193},{65,1},{129,65},{193,129... | collective-permute-start | bytes 393224 | tf_op jit(solution)/shard_map/ppermute | solution.py:208
  70.8 2.3 %collective-permute-done.15.refs_11_ = bf16[32,2048]{1,0:T(8,128)(2,1)S(1)} collective-permute-done((bf16[32,2048]{1,0:T(8,128)(2,1)S(1)}, bf16[32,2048]{1,0:T(8,128)(2,1)S(1)}, u32[]{:S(2)}, u32[]{:S(2)}) %collective-permute-start.15) | collective-permute-done | bytes 131104 | tf_op jit(solution)/shard_map/ppermute | solution.py:208
  73.7 6.7 %all-to-all-start.3 = ((bf16[16,64,128]{2,1,0:T(8,128)(2,1)}), bf16[16,64,128]{2,1,0:T(8,128)(2,1)S(1)}, u32[]{:S(2)}, u32[]{:S(2)}) async-start(bf16[16,64,128]{2,1,0:T(8,128)(2,1)} %bitcast.6), calls=%async_computation.3 | async-start | bytes 524288 | tf_op jit(solution)/shard_map/all_to_all | solution.py:184
  83.8 5.8 %shard_map.61 = f32[8,768,128]{2,1,0:T(8,128)S(1)} custom-call(s32[4]{0:T(128)S(1)} %pad_add_fusion.ids, bf16[64,2048]{1,0:T(8,128)(2,1)S(1)} %collective-permute-done.refs_0_, bf16[64,2048]{1,0:T(8,128)(2,1)} %collective-permute-done.7.refs_1_, bf16[64,2048]{1,0:T(8,128)(2,1)} %collective-permute-done.8.refs_2_, ...), custom_call_target="tpu_custom_call" | custom-call | flops 3221225472 | bytes 9437184 | tf_op jit(solution)/shard_map/pallas_call | solution.py:75
  91.5 4.3 %all-to-all-start.2 = ((f16[8,768,128]{2,1,0:T(8,128)(2,1)}), f16[8,768,128]{2,1,0:T(8,128)(2,1)}, u32[]{:S(2)}, u32[]{:S(2)}) async-start(f16[8,768,128]{2,1,0:T(8,128)(2,1)} %convert_element_type.14), calls=%async_computation.2 | async-start | bytes 3145728 | tf_op jit(solution)/shard_map/all_to_all | solution.py:181
  97.0 6.6 %collective-permute-start.17 = (bf16[16,64,128]{2,1,0:T(8,128)(2,1)S(1)}, bf16[16,64,128]{2,1,0:T(8,128)(2,1)S(1)}, u32[]{:S(2)}, u32[]{:S(2)}) collective-permute-start(bf16[16,64,128]{2,1,0:T(8,128)(2,1)S(1)} %all-to-all-done.3.refs_2_), channel_id=1, source_target_pairs={{0,8},{8,0},{1,9},{9,1},{2,10},{10,2},{3,11},{11,3},{4,12},{12,4},... | collective-permute-start | bytes 786440 | tf_op jit(solution)/shard_map/ppermute | solution.py:219
  103.6 7.5 %all-to-all-done.2 = f16[8,768,128]{2,1,0:T(8,128)(2,1)} async-done(((f16[8,768,128]{2,1,0:T(8,128)(2,1)}), f16[8,768,128]{2,1,0:T(8,128)(2,1)}, u32[]{:S(2)}, u32[]{:S(2)}) %all-to-all-start.2) | async-done | bytes 1572896 | tf_op jit(solution)/shard_map/all_to_all | solution.py:181
  115.1 7.6 %all-to-all-start.4 = ((f32[8,8,2,8,256]{4,3,2,1,0:T(8,128)}), f32[8,8,2,8,256]{4,3,2,1,0:T(8,128)S(1)}, u32[]{:S(2)}, u32[]{:S(2)}) async-start(f32[8,8,2,8,256]{4,3,2,1,0:T(8,128)} %get-tuple-element.65), calls=%async_computation.4 | async-start | bytes 2097152 | tf_op jit(solution)/shard_map/all_to_all | solution.py:181
  127.6 7.5 %all-to-all-done.4 = f32[8,8,2,8,256]{4,3,2,1,0:T(8,128)S(1)} async-done(((f32[8,8,2,8,256]{4,3,2,1,0:T(8,128)}), f32[8,8,2,8,256]{4,3,2,1,0:T(8,128)S(1)}, u32[]{:S(2)}, u32[]{:S(2)}) %all-to-all-start.4) | async-done | bytes 1048608 | tf_op jit(solution)/shard_map/all_to_all | solution.py:181
  135.3 20.1 %all_to_all.30 = f32[16,2,8,128]{3,2,1,0:T(8,128)S(1)} all-to-all(f32[16,2,8,128]{3,2,1,0:T(8,128)S(1)} %copy.9), channel_id=1, replica_groups=mesh['x'=4,'zh'=4,'core'=2,'zl'=2,'y'=4] {'x','zh'}, dimensions={0} | all-to-all | bytes 262144 | tf_op jit(solution)/shard_map/all_to_all | solution.py:184
  155.4 3.8 %collective-permute-start.19 = (f32[8,128]{1,0:T(8,128)S(1)}, f32[8,128]{1,0:T(8,128)S(1)}, u32[]{:S(2)}, u32[]{:S(2)}) collective-permute-start(f32[8,128]{1,0:T(8,128)S(1)} %slice_bitcast_fusion), channel_id=1, source_target_pairs={{0,8},{8,0},{1,9},{9,1},{2,10},{10,2},{3,11},{11,3},{4,12},{12,4},... | collective-permute-start | bytes 12296 | tf_op jit(solution)/shard_map/ppermute | solution.py:230
  (75 shorter events, 35.5 us)
Async XLA Ops:
  0.6 26.7 %collective-permute-start.5 = (bf16[512,2048]{1,0:T(8,128)(2,1)}, bf16[512,2048]{1,0:T(8,128)(2,1)S(1)}, u32[]{:S(2)}, u32[]{:S(2)}) collective-permute-start(bf16[512,2048]{1,0:T(8,128)(2,1)} %refs_13_.1), channel_id=1, source_target_pairs={{0,8},{8,0},{1,9},{9,1},{2,10},{10,2},{3,11},{11,3},{4,12},{12,4},... | collective-permute-start | bytes 6291464 | tf_op jit(solution)/shard_map/ppermute | solution.py:186
  7.1 9.1 %collective-permute-start.2 = (bf16[64,2048]{1,0:T(8,128)(2,1)S(1)}, bf16[64,2048]{1,0:T(8,128)(2,1)S(1)}, u32[]{:S(2)}, u32[]{:S(2)}) collective-permute-start(bf16[64,2048]{1,0:T(8,128)(2,1)S(1)} %get-tuple-element.40.refs_0_), channel_id=1, source_target_pairs={{0,64},{64,128},{128,192},{192,0},{1,65},{65,129},{129,193},{193,1... | collective-permute-start | bytes 786440 | tf_op jit(solution)/shard_map/ppermute | solution.py:178
  7.1 9.1 %collective-permute-start.3 = (bf16[64,2048]{1,0:T(8,128)(2,1)S(1)}, bf16[64,2048]{1,0:T(8,128)(2,1)S(1)}, u32[]{:S(2)}, u32[]{:S(2)}) collective-permute-start(bf16[64,2048]{1,0:T(8,128)(2,1)S(1)} %get-tuple-element.40.refs_0_), channel_id=1, source_target_pairs={{0,192},{64,0},{128,64},{192,128},{1,193},{65,1},{129,65},{193,129... | collective-permute-start | bytes 786440 | tf_op jit(solution)/shard_map/ppermute | solution.py:178
  9.8 12.0 %collective-permute-start = (bf16[64,2048]{1,0:T(8,128)(2,1)S(1)}, bf16[64,2048]{1,0:T(8,128)(2,1)S(1)}, u32[]{:S(2)}, u32[]{:S(2)}) collective-permute-start(bf16[64,2048]{1,0:T(8,128)(2,1)S(1)} %get-tuple-element.40.refs_0_), channel_id=1, source_target_pairs={{0,16},{16,32},{32,48},{48,0},{1,17},{17,33},{33,49},{49,1},{2,18}... | collective-permute-start | bytes 786440 | tf_op jit(solution)/shard_map/ppermute | solution.py:189
  11.1 16.3 %collective-permute-start.1 = (bf16[64,2048]{1,0:T(8,128)(2,1)S(1)}, bf16[64,2048]{1,0:T(8,128)(2,1)}, u32[]{:S(2)}, u32[]{:S(2)}) collective-permute-start(bf16[64,2048]{1,0:T(8,128)(2,1)S(1)} %get-tuple-element.40.refs_0_), channel_id=1, source_target_pairs={{0,48},{16,0},{32,16},{48,32},{1,49},{17,1},{33,17},{49,33},{2,50}... | collective-permute-start | bytes 786440 | tf_op jit(solution)/shard_map/ppermute | solution.py:189
  16.3 11.1 %collective-permute-start.4 = (bf16[64,2048]{1,0:T(8,128)(2,1)S(1)}, bf16[64,2048]{1,0:T(8,128)(2,1)S(1)}, u32[]{:S(2)}, u32[]{:S(2)}) collective-permute-start(bf16[64,2048]{1,0:T(8,128)(2,1)S(1)} %collective-permute-done.2.refs_1_), channel_id=1, source_target_pairs={{0,64},{64,128},{128,192},{192,0},{1,65},{65,129},{129,193},{193,1... | collective-permute-start | bytes 786440 | tf_op jit(solution)/shard_map/ppermute | solution.py:191
  16.3 26.1 %all-to-all-start = ((bf16[8,2,64,128]{3,2,1,0:T(8,128)(2,1)}), bf16[8,2,64,128]{3,2,1,0:T(8,128)(2,1)}, u32[]{:S(2)}, u32[]{:S(2)}) async-start(bf16[8,2,64,128]{3,2,1,0:T(8,128)(2,1)} %get-tuple-element.43), calls=%async_computation | async-start | bytes 524288 | tf_op jit(solution)/shard_map/all_to_all | solution.py:181
  27.4 15.0 %collective-permute-start.6 = (bf16[64,2048]{1,0:T(8,128)(2,1)S(1)}, bf16[64,2048]{1,0:T(8,128)(2,1)}, u32[]{:S(2)}, u32[]{:S(2)}) collective-permute-start(bf16[64,2048]{1,0:T(8,128)(2,1)S(1)} %get-tuple-element.40.refs_0_), channel_id=1, source_target_pairs={{0,32},{16,48},{32,0},{48,16},{1,33},{17,49},{33,1},{49,17},{2,34}... | collective-permute-start | bytes 786440 | tf_op jit(solution)/shard_map/ppermute | solution.py:195
  30.6 11.8 %collective-permute-start.7 = (bf16[64,2048]{1,0:T(8,128)(2,1)S(1)}, bf16[64,2048]{1,0:T(8,128)(2,1)}, u32[]{:S(2)}, u32[]{:S(2)}) collective-permute-start(bf16[64,2048]{1,0:T(8,128)(2,1)S(1)} %collective-permute-done.refs_0_), channel_id=1, source_target_pairs={{0,64},{64,128},{128,192},{192,0},{1,65},{65,129},{129,193},{193,1... | collective-permute-start | bytes 786440 | tf_op jit(solution)/shard_map/ppermute | solution.py:178
  30.6 11.8 %collective-permute-start.8 = (bf16[64,2048]{1,0:T(8,128)(2,1)S(1)}, bf16[64,2048]{1,0:T(8,128)(2,1)}, u32[]{:S(2)}, u32[]{:S(2)}) collective-permute-start(bf16[64,2048]{1,0:T(8,128)(2,1)S(1)} %collective-permute-done.refs_0_), channel_id=1, source_target_pairs={{0,192},{64,0},{128,64},{192,128},{1,193},{65,1},{129,65},{193,129... | collective-permute-start | bytes 786440 | tf_op jit(solution)/shard_map/ppermute | solution.py:178
  33.3 10.5 %collective-permute-start.9 = (bf16[64,2048]{1,0:T(8,128)(2,1)}, bf16[64,2048]{1,0:T(8,128)(2,1)}, u32[]{:S(2)}, u32[]{:S(2)}) collective-permute-start(bf16[64,2048]{1,0:T(8,128)(2,1)} %collective-permute-done.1.refs_4_), channel_id=1, source_target_pairs={{0,64},{64,128},{128,192},{192,0},{1,65},{65,129},{129,193},{193,1... | collective-permute-start | bytes 786440 | tf_op jit(solution)/shard_map/ppermute | solution.py:178
  33.3 10.5 %collective-permute-start.10 = (bf16[64,2048]{1,0:T(8,128)(2,1)}, bf16[64,2048]{1,0:T(8,128)(2,1)}, u32[]{:S(2)}, u32[]{:S(2)}) collective-permute-start(bf16[64,2048]{1,0:T(8,128)(2,1)} %collective-permute-done.1.refs_4_), channel_id=1, source_target_pairs={{0,192},{64,0},{128,64},{192,128},{1,193},{65,1},{129,65},{193,129... | collective-permute-start | bytes 786440 | tf_op jit(solution)/shard_map/ppermute | solution.py:178
  43.7 6.6 %collective-permute-start.11 = (bf16[64,2048]{1,0:T(8,128)(2,1)}, bf16[64,2048]{1,0:T(8,128)(2,1)S(1)}, u32[]{:S(2)}, u32[]{:S(2)}) collective-permute-start(bf16[64,2048]{1,0:T(8,128)(2,1)} %collective-permute-done.7.refs_1_), channel_id=1, source_target_pairs={{0,64},{64,128},{128,192},{192,0},{1,65},{65,129},{129,193},{193,1... | collective-permute-start | bytes 786440 | tf_op jit(solution)/shard_map/ppermute | solution.py:202
  50.4 23.3 %all-to-all-start.1 = ((f16[8,256,128]{2,1,0:T(8,128)(2,1)}), f16[8,256,128]{2,1,0:T(8,128)(2,1)}, u32[]{:S(2)}, u32[]{:S(2)}) async-start(f16[8,256,128]{2,1,0:T(8,128)(2,1)} %convert_element_type.12), calls=%async_computation.1 | async-start | bytes 1048576 | tf_op jit(solution)/shard_map/all_to_all | solution.py:181
  56.6 5.4 %collective-permute-start.12 = (bf16[64,2048]{1,0:T(8,128)(2,1)}, bf16[64,2048]{1,0:T(8,128)(2,1)S(1)}, u32[]{:S(2)}, u32[]{:S(2)}) collective-permute-start(bf16[64,2048]{1,0:T(8,128)(2,1)} %collective-permute-done.10.refs_6_), channel_id=1, source_target_pairs={{0,192},{64,0},{128,64},{192,128},{1,193},{65,1},{129,65},{193,129... | collective-permute-start | bytes 786440 | tf_op jit(solution)/shard_map/ppermute | solution.py:202
  56.6 7.0 %collective-permute-start.13 = (bf16[64,2048]{1,0:T(8,128)(2,1)}, bf16[64,2048]{1,0:T(8,128)(2,1)S(1)}, u32[]{:S(2)}, u32[]{:S(2)}) collective-permute-start(bf16[64,2048]{1,0:T(8,128)(2,1)} %collective-permute-done.6.refs_8_), channel_id=1, source_target_pairs={{0,64},{64,128},{128,192},{192,0},{1,65},{65,129},{129,193},{193,1... | collective-permute-start | bytes 786440 | tf_op jit(solution)/shard_map/ppermute | solution.py:178
  58.1 9.7 %collective-permute-start.14 = (bf16[64,2048]{1,0:T(8,128)(2,1)}, bf16[64,2048]{1,0:T(8,128)(2,1)S(1)}, u32[]{:S(2)}, u32[]{:S(2)}) collective-permute-start(bf16[64,2048]{1,0:T(8,128)(2,1)} %collective-permute-done.6.refs_8_), channel_id=1, source_target_pairs={{0,192},{64,0},{128,64},{192,128},{1,193},{65,1},{129,65},{193,129... | collective-permute-start | bytes 786440 | tf_op jit(solution)/shard_map/ppermute | solution.py:178
  67.7 5.3 %collective-permute-start.15 = (bf16[32,2048]{1,0:T(8,128)(2,1)S(1)}, bf16[32,2048]{1,0:T(8,128)(2,1)S(1)}, u32[]{:S(2)}, u32[]{:S(2)}) collective-permute-start(bf16[32,2048]{1,0:T(8,128)(2,1)S(1)} %slice.13), channel_id=1, source_target_pairs={{0,64},{64,128},{128,192},{192,0},{1,65},{65,129},{129,193},{193,1... | collective-permute-start | bytes 393224 | tf_op jit(solution)/shard_map/ppermute | solution.py:208
  68.0 5.0 %collective-permute-start.16 = (bf16[32,2048]{1,0:T(8,128)(2,1)S(1)}, bf16[32,2048]{1,0:T(8,128)(2,1)S(1)}, u32[]{:S(2)}, u32[]{:S(2)}) collective-permute-start(bf16[32,2048]{1,0:T(8,128)(2,1)S(1)} %slice.14), channel_id=1, source_target_pairs={{0,192},{64,0},{128,64},{192,128},{1,193},{65,1},{129,65},{193,129... | collective-permute-start | bytes 393224 | tf_op jit(solution)/shard_map/ppermute | solution.py:208
  73.7 17.9 %all-to-all-start.3 = ((bf16[16,64,128]{2,1,0:T(8,128)(2,1)}), bf16[16,64,128]{2,1,0:T(8,128)(2,1)S(1)}, u32[]{:S(2)}, u32[]{:S(2)}) async-start(bf16[16,64,128]{2,1,0:T(8,128)(2,1)} %bitcast.6), calls=%async_computation.3 | async-start | bytes 524288 | tf_op jit(solution)/shard_map/all_to_all | solution.py:184
  91.5 19.6 %all-to-all-start.2 = ((f16[8,768,128]{2,1,0:T(8,128)(2,1)}), f16[8,768,128]{2,1,0:T(8,128)(2,1)}, u32[]{:S(2)}, u32[]{:S(2)}) async-start(f16[8,768,128]{2,1,0:T(8,128)(2,1)} %convert_element_type.14), calls=%async_computation.2 | async-start | bytes 3145728 | tf_op jit(solution)/shard_map/all_to_all | solution.py:181
  97.0 15.8 %collective-permute-start.17 = (bf16[16,64,128]{2,1,0:T(8,128)(2,1)S(1)}, bf16[16,64,128]{2,1,0:T(8,128)(2,1)S(1)}, u32[]{:S(2)}, u32[]{:S(2)}) collective-permute-start(bf16[16,64,128]{2,1,0:T(8,128)(2,1)S(1)} %all-to-all-done.3.refs_2_), channel_id=1, source_target_pairs={{0,8},{8,0},{1,9},{9,1},{2,10},{10,2},{3,11},{11,3},{4,12},{12,4},... | collective-permute-start | bytes 786440 | tf_op jit(solution)/shard_map/ppermute | solution.py:219
  115.1 20.1 %all-to-all-start.4 = ((f32[8,8,2,8,256]{4,3,2,1,0:T(8,128)}), f32[8,8,2,8,256]{4,3,2,1,0:T(8,128)S(1)}, u32[]{:S(2)}, u32[]{:S(2)}) async-start(f32[8,8,2,8,256]{4,3,2,1,0:T(8,128)} %get-tuple-element.65), calls=%async_computation.4 | async-start | bytes 2097152 | tf_op jit(solution)/shard_map/all_to_all | solution.py:181
  155.4 4.6 %collective-permute-start.19 = (f32[8,128]{1,0:T(8,128)S(1)}, f32[8,128]{1,0:T(8,128)S(1)}, u32[]{:S(2)}, u32[]{:S(2)}) collective-permute-start(f32[8,128]{1,0:T(8,128)S(1)} %slice_bitcast_fusion), channel_id=1, source_target_pairs={{0,8},{8,0},{1,9},{9,1},{2,10},{10,2},{3,11},{11,3},{4,12},{12,4},... | collective-permute-start | bytes 12296 | tf_op jit(solution)/shard_map/ppermute | solution.py:230
  (12 other events, 100.6 us)

commit v3 on v2

--- a/solution.py
+++ b/solution.py
@@ -7,7 +7,8 @@
 from jax.experimental.pallas import tpu as pltpu
 from jax.sharding import Mesh, PartitionSpec as P
 
-GROUPS = ((0,), (1, 3, 2))
+EARLY = ((0, 0), (3, 0), (1, 0), (2, 0), (0, 1), (3, 1), (1, 1), (0, 3), (3, 3), (1, 3))
+LATE = ((2, 1), (2, 3), (0, 2), (3, 2), (1, 2), (2, 2))
 SCALE = 64.0
 NT = (((1,), (1,)), ((), ()))
 VMEM = pl.BlockSpec(memory_space=pltpu.VMEM)
@@ -52,15 +53,15 @@
     )(ids, mask, panel)
 
 
-def product_kernel(places, size, ids, *refs):
-    count = len(places)
-    slabs, (root, other_root, out, gathered, pair) = refs[:count], refs[count:]
+def product_kernel(ids, *refs):
+    slabs, (root, other_root, out, gathered, pair) = refs[:-5], refs[-5:]
 
     @pl.when(pl.program_id(0) == 0)
     def _():
-        for slab, (shift, skip) in zip(slabs, places):
-            start = pl.multiple_of(lax.rem(ids[0] + shift, 4) * size + skip, 16)
-            gathered[pl.ds(start, slab.shape[0]), :] = slab[...]
+        start = 0
+        for slab in slabs:
+            gathered[start:start + slab.shape[0], :] = slab[...]
+            start += slab.shape[0]
 
     for j in range(2):
         pair[128 * j:128 * j + 64, :] = root[64 * j:64 * j + 64, :]
@@ -70,40 +71,65 @@
     out[1] = prod[:, 128:256] * SCALE
 
 
-def product_call(ids, slabs, places, size, root, other_root):
-    n = 4 * size
-    return pl.pallas_call(
-        functools.partial(product_kernel, places, size),
+def product_call(ids, slabs, root, other_root, vmem):
+    n = sum(slab.shape[0] for slab in slabs)
+    return pl.pallas_call(
+        product_kernel,
         grid=(4,),
         out_shape=jax.ShapeDtypeStruct((8, n, 128), jnp.float32),
         in_specs=[SMEM] + [pl.BlockSpec(slab.shape, lambda t: (0, 0)) for slab in slabs]
         + [pl.BlockSpec((128, 2048), lambda t: (t, 0))] * 2,
         out_specs=pl.BlockSpec((2, n, 128), lambda t: (t, 0, 0)),
         scratch_shapes=[pltpu.VMEM((n, 2048), jnp.bfloat16), pltpu.VMEM((256, 2048), jnp.bfloat16)],
-        compiler_params=pltpu.CompilerParams(vmem_limit_bytes=24 * 2**20),
+        compiler_params=pltpu.CompilerParams(vmem_limit_bytes=vmem * 2**20),
         cost_estimate=pl.CostEstimate(flops=2 * n * 2048 * 1024, bytes_accessed=2 * n * 2048 + 6 * 2**20, transcendentals=0),
     )(ids, *slabs, root, other_root)
 
 
-def diag_kernel(ids, *refs):
-    count = len(GROUPS)
-    products, (mine, other, keep, give, diag) = refs[:count], refs[count:]
-    iz = ids[1]
+def mark_kernel(source, out):
+    out[...] = jnp.zeros_like(out)
+
+
+def mark_call(value):
+    return pl.pallas_call(
+        mark_kernel,
+        out_shape=jax.ShapeDtypeStruct((8, 128), jnp.float32),
+        in_specs=[ANY],
+        out_specs=VMEM,
+        cost_estimate=pl.CostEstimate(flops=2**34, bytes_accessed=2**12, transcendentals=0),
+    )(value)
+
+
+def hold_kernel(after, source, out):
+    out[...] = source[...]
+
+
+def hold_call(after, value):
+    return pl.pallas_call(
+        hold_kernel,
+        out_shape=jax.ShapeDtypeStruct(value.shape, value.dtype),
+        in_specs=[ANY, VMEM],
+        out_specs=VMEM,
+        cost_estimate=pl.CostEstimate(flops=2**34, bytes_accessed=2**19, transcendentals=0),
+    )(after, value)
+
+
+def diag_kernel(ids, early, late, mine, other, keep, give, diag):
+    ix, iz = ids[0], ids[1]
     low = lax.broadcasted_iota(jnp.int32, (8, 128), 1) < 64
     left = mine[...].astype(jnp.float32).reshape(16, 8, 8, 128)
     right = pltpu.roll(other[...].astype(jnp.float32), 64, 2).reshape(16, 8, 8, 128)
     totals, places = [], []
-    for product, group in zip(products, GROUPS):
-        total = product[...].reshape(4, len(group), 8, 8, 128)
-        for q, s in enumerate(group):
-            z = lax.rem(iz + 4 - s, 4)
-            for x in range(4):
-                totals.append(total[x, q])
-                places.append((x, z))
-                for t in range(4):
-                    even, odd = total[x, q, 2 * t], total[x, q, 2 * t + 1]
-                    keep[t, x, z] = -jnp.where(low, even, pltpu.roll(odd, 64, 1))
-                    give[t, x, z] = -jnp.where(low, pltpu.roll(even, 64, 1), odd)
+    slabs = [early[64 * i:64 * i + 64, :] for i in range(len(EARLY))] + [late[64 * i:64 * i + 64, :] for i in range(len(LATE))]
+    for slab, (dx, dz) in zip(slabs, EARLY + LATE):
+        total = slab.reshape(8, 8, 128)
+        x, z = lax.rem(ix + dx, 4), lax.rem(iz + 4 - dz, 4)
+        totals.append(total)
+        places.append((2 * x + lax.div(z, 2), lax.rem(z, 2)))
+        for t in range(4):
+            even, odd = total[2 * t], total[2 * t + 1]
+            keep[t, x, z] = -jnp.where(low, even, pltpu.roll(odd, 64, 1))
+            give[t, x, z] = -jnp.where(low, pltpu.roll(even, 64, 1), odd)
     for k in range(8):
         p = jnp.concatenate([total[k] for total in totals], axis=0)
         hi = p.astype(jnp.bfloat16)
@@ -114,11 +140,11 @@
         d = lax.dot_general(lo, m, NT, preferred_element_type=jnp.float32)
         d += lax.dot_general(mid, m, NT, preferred_element_type=jnp.float32)
         d += lax.dot_general(hi, m, NT, preferred_element_type=jnp.float32)
-        for i, (x, z) in enumerate(places):
-            diag[2 * x + z // 2, k, lax.rem(z, 2)] = d[i * 8:(i + 1) * 8, :]
-
-
-def diag_call(ids, products, mine, other):
+        for i, (column, z) in enumerate(places):
+            diag[column, k, z] = d[i * 8:(i + 1) * 8, :]
+
+
+def diag_call(ids, early, late, mine, other):
     return pl.pallas_call(
         diag_kernel,
         out_shape=(
@@ -126,11 +152,11 @@
             jax.ShapeDtypeStruct((4, 4, 4, 8, 128), jnp.float32),
             jax.ShapeDtypeStruct((8, 8, 2, 8, 256), jnp.float32),
         ),
-        in_specs=[SMEM] + [VMEM] * (len(GROUPS) + 2),
+        in_specs=[SMEM] + [VMEM] * 4,
         out_specs=(VMEM,) * 3,
         compiler_params=pltpu.CompilerParams(vmem_limit_bytes=16 * 2**20),
         cost_estimate=pl.CostEstimate(flops=2 * 8 * 3 * 128 * 128 * 256, bytes_accessed=2**23, transcendentals=0),
-    )(ids, *products, mine, other)
+    )(ids, early, late, mine, other)
 
 
 def rows_kernel(ids, keep, got, out):
@@ -194,32 +220,22 @@
 
     z2 = lax.ppermute(own, "zh", turn(4, 2))
     near1, near3 = around(z1), around(z3)
-    sent0 = send_parts(
-        product_call(ids, [own, *near0, far0], [(0, 0), (3, 0), (1, 0), (2, 0)], 64, inverse_root, other_root)
-    )
-    z2, near1, near3, pieces, sent0 = pin((z2, near1, near3, pieces, sent0))
+    mine = to_rows(hold_call(mark_call(own), pieces.reshape(16, 64, 128)))
+    z2, near1, near3 = pin((z2, near1, near3))
 
     far1, far3 = lax.ppermute(near1[0], "x", turn(4, 1)), lax.ppermute(near3[1], "x", turn(4, -1))
     near2 = around(z2)
-    far1, sent0 = pin((far1, sent0))
-    parts0 = to_columns(sent0)
-    far1, far3, near2 = pin((far1, far3, near2))
-
-    far2 = [lax.ppermute(near2[0][:32], "x", turn(4, 1)), lax.ppermute(near2[1][32:], "x", turn(4, -1))]
-    far2, pieces, parts0 = pin((far2, pieces, parts0))
-
-    sent1 = send_parts(product_call(
-        ids,
-        [z1, *near1, far1, z3, *near3, far3, z2, *near2, *far2],
-        [(0, 0), (3, 0), (1, 0), (2, 0), (0, 64), (3, 64), (1, 64), (2, 64), (0, 128), (3, 128), (1, 128), (2, 128), (2, 160)],
-        192, inverse_root, other_root,
-    ))
-    parts1 = to_columns(sent1)
-    mine = to_rows(pieces.reshape(16, 64, 128))
+    early = send_parts(product_call(ids, [own, *near0, far0, z1, *near1, z3, *near3], inverse_root, other_root, 58))
+    far1, far3, near2, early, mine = pin((far1, far3, near2, early, mine))
+
+    parts = to_columns(early)
+    far2 = lax.ppermute(near2[0], "x", turn(4, 1))
+    far2 = pin((far2,))[0]
+
+    late = send_parts(product_call(ids, [far1, far3, z2, *near2, far2], inverse_root, other_root, 24))
+    late, parts = pin((late, parts))
     other = lax.ppermute(mine, "core", swap)
-    products = [sum_parts(parts0), sum_parts(parts1)]
-
-    keep, give, diag = diag_call(ids, products, mine, other)
+    keep, give, diag = diag_call(ids, sum_parts(parts), sum_parts(to_columns(late)), mine, other)
     got = lax.ppermute(give, "core", swap)
     here = jnp.sum(to_columns(diag), axis=0)
     panel_inverse = rows_call(ids, keep, got)

time: 162 us -> 142 us (0.88)
  starting transfers between devices: 66.7 us -> 57.8 us
  waiting for transfers between devices: 44.7 us -> 37.5 us
  blocking collectives: 20.1 us -> 14.9 us
  Pallas kernels: 13.6 us -> 18.3 us
  local copies, waits for them, and re-layouts: 9.34 us -> 5.34 us
    ppermute x1, waiting for transfers between devices: 6.64 us -> 0.01 us  [shards(): lax.ppermute(near1[0], 'x', turn(4, 1))]
    all_to_all x4, waiting for transfers between devices: 15 us -> 20.7 us  [to_columns(): return lax.all_to_all(value, ('zl', 'y'), 0, 0, tiled=True)]
    ppermute x1, starting transfers between devices: 6.61 us -> 1.07 us  [shards(): other = lax.ppermute(mine, 'core', swap)]
    all_to_all x1, blocking collectives: 20.1 us -> 14.9 us  [to_rows(): return lax.all_to_all(value, ('x', 'zh'), 0, 0, tiled=True)]
    pallas_call x2 -> x4, Pallas kernels: 8.33 us -> 13.1 us  [the longest x2 10.8 us: product_call(): pl.pallas_call(product_kernel, grid=(4,), out_shape=jax.ShapeDtypeStruct(...]
    ppermute x2 -> x1, waiting for transfers between devices: 2.26 us -> 6.42 us  [shards(): far2 = lax.ppermute(near2[0], 'x', turn(4, 1))]
    ppermute x4, waiting for transfers between devices: 4.15 us -> 0.01 us  [around(): lax.ppermute(slab, 'x', turn(4, -1))]
    unnamed x22 -> x28, local copies, waits for them, and re-layouts: 8.68 us -> 4.7 us
  transfers between devices with their start and end apart: 25 -> 24, of which waited for: 14 -> 9; matrix products, arithmetic and copies ran while one was open for 3% -> 4% of each run, Pallas kernels for 7% -> 11%
where the time goes in v3:
time: 142 us; the launch traced here: 141 us
  starting transfers between devices  57.8 us (41%)
  waiting for transfers between devices  37.5 us (26%)
  Pallas kernels  18.3 us (13%)
  blocking collectives  14.9 us (10%)
  other arithmetic  6.6 us (5%)
  local copies, waits for them, and re-layouts  5.34 us (4%)
    all_to_all x4, starting transfers between devices, to_columns(): return lax.all_to_all(value, ('zl', 'y'), 0, 0, tiled=True)  24.8 us
    all_to_all x4, waiting for transfers between devices, to_columns(): return lax.all_to_all(value, ('zl', 'y'), 0, 0, tiled=True)  20.7 us
    all_to_all x1, blocking collectives, to_rows(): return lax.all_to_all(value, ('x', 'zh'), 0, 0, tiled=True)  14.9 us
    pallas_call x2, Pallas kernels, product_call(): pl.pallas_call(product_kernel, grid=(4,), out_shape=jax.ShapeDtypeStruct(...  10.8 us
    ppermute x4, starting transfers between devices, around(): lax.ppermute(slab, 'x', turn(4, -1))  7.91 us
    ppermute x1, waiting for transfers between devices, shards(): far2 = lax.ppermute(near2[0], 'x', turn(4, 1))  6.42 us
    ppermute x2, waiting for transfers between devices, shards(): z1, z3 = (lax.ppermute(own, 'zh', turn(4, s)) for s in (1, 3))  6.27 us
    all_to_all x1, starting transfers between devices, to_rows(): return lax.all_to_all(value, ('x', 'zh'), 0, 0, tiled=True)  5.5 us
  transfers between devices with their start and end apart: 24, of which 9 were waited for; matrix products, arithmetic and copies ran while one was open for 4% of the time, Pallas kernels for 11%

profile of v3, /device:TPU:1, one launch (start us, length us, event | category | flops | bytes accessed | tf_op | source)
XLA Modules:
  0.0 141.3 jit_solution(4961484498334714182)
XLA Ops:
  0.6 3.3 %collective-permute-start.5 = (bf16[512,2048]{1,0:T(8,128)(2,1)}, bf16[512,2048]{1,0:T(8,128)(2,1)S(1)}, u32[]{:S(2)}, u32[]{:S(2)}) collective-permute-start(bf16[512,2048]{1,0:T(8,128)(2,1)} %refs_6_.1), channel_id=1, source_target_pairs={{0,8},{8,0},{1,9},{9,1},{2,10},{10,2},{3,11},{11,3},{4,12},{12,4},... | collective-permute-start | bytes 6291464 | tf_op jit(solution)/shard_map/ppermute | solution.py:212
  7.2 2.7 %collective-permute-start.3 = (bf16[64,2048]{1,0:T(8,128)(2,1)S(1)}, bf16[64,2048]{1,0:T(8,128)(2,1)S(1)}, u32[]{:S(2)}, u32[]{:S(2)}) collective-permute-start(bf16[64,2048]{1,0:T(8,128)(2,1)S(1)} %get-tuple-element.36.refs_0_.source), channel_id=1, source_target_pairs={{0,192},{64,0},{128,64},{192,128},{1,193},{65,1},{129,65},{193,129... | collective-permute-start | bytes 786440 | tf_op jit(solution)/shard_map/ppermute | solution.py:204
  11.1 3.0 %collective-permute-start.1 = (bf16[64,2048]{1,0:T(8,128)(2,1)S(1)}, bf16[64,2048]{1,0:T(8,128)(2,1)S(1)}, u32[]{:S(2)}, u32[]{:S(2)}) collective-permute-start(bf16[64,2048]{1,0:T(8,128)(2,1)S(1)} %get-tuple-element.36.refs_0_.source), channel_id=1, source_target_pairs={{0,48},{16,0},{32,16},{48,32},{1,49},{17,1},{33,17},{49,33},{2,50}... | collective-permute-start | bytes 786440 | tf_op jit(solution)/shard_map/ppermute | solution.py:215
  14.1 2.2 %collective-permute-done.2.refs_1_ = bf16[64,2048]{1,0:T(8,128)(2,1)S(1)} collective-permute-done((bf16[64,2048]{1,0:T(8,128)(2,1)S(1)}, bf16[64,2048]{1,0:T(8,128)(2,1)S(1)}, u32[]{:S(2)}, u32[]{:S(2)}) %collective-permute-start.2) | collective-permute-done | bytes 262176 | tf_op jit(solution)/shard_map/ppermute | solution.py:204
  17.1 3.9 %all-to-all-start = ((bf16[8,2,64,128]{3,2,1,0:T(8,128)(2,1)}), bf16[8,2,64,128]{3,2,1,0:T(8,128)(2,1)S(1)}, u32[]{:S(2)}, u32[]{:S(2)}) async-start(bf16[8,2,64,128]{3,2,1,0:T(8,128)(2,1)} %get-tuple-element.48), calls=%async_computation | async-start | bytes 524288 | tf_op jit(solution)/shard_map/all_to_all | solution.py:207
  21.8 5.4 %collective-permute-done.1.refs_7_ = bf16[64,2048]{1,0:T(8,128)(2,1)S(1)} collective-permute-done((bf16[64,2048]{1,0:T(8,128)(2,1)S(1)}, bf16[64,2048]{1,0:T(8,128)(2,1)S(1)}, u32[]{:S(2)}, u32[]{:S(2)}) %collective-permute-start.1) | collective-permute-done | bytes 262176 | tf_op jit(solution)/shard_map/ppermute | solution.py:215
  27.4 2.7 %collective-permute-start.8 = (bf16[64,2048]{1,0:T(8,128)(2,1)S(1)}, bf16[64,2048]{1,0:T(8,128)(2,1)}, u32[]{:S(2)}, u32[]{:S(2)}) collective-permute-start(bf16[64,2048]{1,0:T(8,128)(2,1)S(1)} %collective-permute-done.refs_4_), channel_id=1, source_target_pairs={{0,192},{64,0},{128,64},{192,128},{1,193},{65,1},{129,65},{193,129... | collective-permute-start | bytes 786440 | tf_op jit(solution)/shard_map/ppermute | solution.py:204
  31.5 3.2 %collective-permute-start.6 = (bf16[64,2048]{1,0:T(8,128)(2,1)S(1)}, bf16[64,2048]{1,0:T(8,128)(2,1)S(1)}, u32[]{:S(2)}, u32[]{:S(2)}) collective-permute-start(bf16[64,2048]{1,0:T(8,128)(2,1)S(1)} %get-tuple-element.36.refs_0_.source), channel_id=1, source_target_pairs={{0,32},{16,48},{32,0},{48,16},{1,33},{17,49},{33,1},{49,17},{2,34}... | collective-permute-start | bytes 786440 | tf_op jit(solution)/shard_map/ppermute | solution.py:221
  36.1 1.7 %shard_map.62 = bf16[16,64,128]{2,1,0:T(8,128)(2,1)} custom-call(f32[8,128]{1,0:T(8,128)} %shard_map.61.after, bf16[16,64,128]{2,1,0:T(8,128)(2,1)} %bitcast.27), custom_call_target="tpu_custom_call" | custom-call | flops 17179869184 | bytes 524288 | tf_op jit(solution)/shard_map/pallas_call | solution.py:108
  37.7 5.5 %all-to-all-start.1 = ((bf16[16,64,128]{2,1,0:T(8,128)(2,1)}), bf16[16,64,128]{2,1,0:T(8,128)(2,1)S(1)}, u32[]{:S(2)}, u32[]{:S(2)}) async-start(bf16[16,64,128]{2,1,0:T(8,128)(2,1)} %shard_map.62), calls=%async_computation.1 | async-start | bytes 524288 | tf_op jit(solution)/shard_map/all_to_all | solution.py:210
  46.2 2.5 %collective-permute-start.14 = (bf16[64,2048]{1,0:T(8,128)(2,1)S(1)}, bf16[64,2048]{1,0:T(8,128)(2,1)}, u32[]{:S(2)}, u32[]{:S(2)}) collective-permute-start(bf16[64,2048]{1,0:T(8,128)(2,1)S(1)} %collective-permute-done.6.refs_2_), channel_id=1, source_target_pairs={{0,192},{64,0},{128,64},{192,128},{1,193},{65,1},{129,65},{193,129... | collective-permute-start | bytes 786440 | tf_op jit(solution)/shard_map/ppermute | solution.py:204
  48.7 7.2 %shard_map.60 = f32[8,640,128]{2,1,0:T(8,128)} custom-call(s32[4]{0:T(128)} %copy-done.4, bf16[64,2048]{1,0:T(8,128)(2,1)} %copy-done.7, bf16[64,2048]{1,0:T(8,128)(2,1)} %copy-done.10, bf16[64,2048]{1,0:T(8,128)(2,1)} %copy-done.11, bf16[64,2048]{1,0:T(8,128)(2,1)} %collective-permute-done.4.refs_3_, bf16[64,2048]{1,0:T(8,128)(2,1)} %copy-done.12, ...), custom_call_target="tpu_custom_call" | custom-call | flops 2684354560 | bytes 8912896 | tf_op jit(solution)/shard_map/pallas_call | solution.py:76
  56.0 3.1 %convert_element_type.12 = f16[8,640,128]{2,1,0:T(8,128)(2,1)} convert(f32[8,640,128]{2,1,0:T(8,128)} %shard_map.60) | non-fusion elementwise | flops 655360 | bytes 3932160 | tf_op jit(solution)/shard_map/convert_element_type | solution.py:201
  59.1 8.3 %all-to-all-start.2 = ((f16[8,640,128]{2,1,0:T(8,128)(2,1)}), f16[8,640,128]{2,1,0:T(8,128)(2,1)}, u32[]{:S(2)}, u32[]{:S(2)}) async-start(f16[8,640,128]{2,1,0:T(8,128)(2,1)} %convert_element_type.12), calls=%async_computation.2 | async-start | bytes 2621440 | tf_op jit(solution)/shard_map/all_to_all | solution.py:207
  67.4 6.4 %collective-permute-done.15.refs_5_ = bf16[64,2048]{1,0:T(8,128)(2,1)S(1)} collective-permute-done((bf16[64,2048]{1,0:T(8,128)(2,1)S(1)}, bf16[64,2048]{1,0:T(8,128)(2,1)S(1)}, u32[]{:S(2)}, u32[]{:S(2)}) %collective-permute-start.15) | collective-permute-done | bytes 262176 | tf_op jit(solution)/shard_map/ppermute | solution.py:232
  73.8 1.6 %copy-done.2 = bf16[512,2048]{1,0:T(8,128)(2,1)S(1)} copy-done((bf16[512,2048]{1,0:T(8,128)(2,1)S(1)}, bf16[512,2048]{1,0:T(8,128)(2,1)}, u32[]{:S(2)}) %copy-start.2) | copy-done | bytes 2097176
  75.4 3.6 %shard_map.63 = f32[8,384,128]{2,1,0:T(8,128)S(1)} custom-call(s32[4]{0:T(128)S(1)} %copy-done.5, bf16[64,2048]{1,0:T(8,128)(2,1)S(1)} %collective-permute-done.11.refs_0_, bf16[64,2048]{1,0:T(8,128)(2,1)S(1)} %collective-permute-done.12.refs_1_, bf16[64,2048]{1,0:T(8,128)(2,1)S(1)} %collective-permute-done.6.refs_2_, ...), custom_call_target="tpu_custom_call" | custom-call | flops 1610612736 | bytes 7864320 | tf_op jit(solution)/shard_map/pallas_call | solution.py:76
  81.1 7.6 %all-to-all-start.3 = ((f16[8,384,128]{2,1,0:T(8,128)(2,1)}), f16[8,384,128]{2,1,0:T(8,128)(2,1)S(1)}, u32[]{:S(2)}, u32[]{:S(2)}) async-start(f16[8,384,128]{2,1,0:T(8,128)(2,1)} %convert_element_type.13), calls=%async_computation.3 | async-start | bytes 1572864 | tf_op jit(solution)/shard_map/all_to_all | solution.py:207
  91.4 8.2 %all-to-all-done.3 = f16[8,384,128]{2,1,0:T(8,128)(2,1)S(1)} async-done(((f16[8,384,128]{2,1,0:T(8,128)(2,1)}), f16[8,384,128]{2,1,0:T(8,128)(2,1)S(1)}, u32[]{:S(2)}, u32[]{:S(2)}) %all-to-all-start.3) | async-done | bytes 786464 | tf_op jit(solution)/shard_map/all_to_all | solution.py:207
  99.7 2.2 %shard_map.64 = (f32[4,4,4,8,128]{4,3,2,1,0:T(8,128)S(1)}, f32[4,4,4,8,128]{4,3,2,1,0:T(8,128)S(1)}, f32[8,8,2,8,256]{4,3,2,1,0:T(8,128)}) custom-call(s32[4]{0:T(128)S(1)} %copy-done.5, f32[640,128]{1,0:T(8,128)S(1)} %broadcast_multiply_fusion.early, f32[384,128]{1,0:T(8,128)S(1)} %broadcast_multiply_fusion.1.late, ...), custom_call_target="tpu_custom_call" | custom-call | flops 201326592 | bytes 8388608 | tf_op jit(solution)/shard_map/pallas_call | solution.py:148
  101.8 5.0 %all-to-all-start.4 = ((f32[8,8,2,8,256]{4,3,2,1,0:T(8,128)}), f32[8,8,2,8,256]{4,3,2,1,0:T(8,128)S(1)}, u32[]{:S(2)}, u32[]{:S(2)}) async-start(f32[8,8,2,8,256]{4,3,2,1,0:T(8,128)} %get-tuple-element.57), calls=%async_computation.4 | async-start | bytes 2097152 | tf_op jit(solution)/shard_map/all_to_all | solution.py:207
  110.4 11.4 %all-to-all-done.4 = f32[8,8,2,8,256]{4,3,2,1,0:T(8,128)S(1)} async-done(((f32[8,8,2,8,256]{4,3,2,1,0:T(8,128)}), f32[8,8,2,8,256]{4,3,2,1,0:T(8,128)S(1)}, u32[]{:S(2)}, u32[]{:S(2)}) %all-to-all-start.4) | async-done | bytes 1048608 | tf_op jit(solution)/shard_map/all_to_all | solution.py:207
  122.0 14.9 %all_to_all.30 = f32[16,2,8,128]{3,2,1,0:T(8,128)S(1)} all-to-all(f32[16,2,8,128]{3,2,1,0:T(8,128)S(1)} %copy.9), channel_id=1, replica_groups=mesh['x'=4,'zh'=4,'core'=2,'zl'=2,'y'=4] {'x','zh'}, dimensions={0} | all-to-all | bytes 262144 | tf_op jit(solution)/shard_map/all_to_all | solution.py:210
  136.9 2.3 %collective-permute-start.18 = (f32[8,128]{1,0:T(8,128)S(1)}, f32[8,128]{1,0:T(8,128)S(1)}, u32[]{:S(2)}, u32[]{:S(2)}) collective-permute-start(f32[8,128]{1,0:T(8,128)S(1)} %slice_bitcast_fusion), channel_id=1, source_target_pairs={{0,8},{8,0},{1,9},{9,1},{2,10},{10,2},{3,11},{11,3},{4,12},{12,4},... | collective-permute-start | bytes 12296 | tf_op jit(solution)/shard_map/ppermute | solution.py:246
  (79 shorter events, 22.6 us)
Async XLA Ops:
  0.6 26.6 %collective-permute-start.5 = (bf16[512,2048]{1,0:T(8,128)(2,1)}, bf16[512,2048]{1,0:T(8,128)(2,1)S(1)}, u32[]{:S(2)}, u32[]{:S(2)}) collective-permute-start(bf16[512,2048]{1,0:T(8,128)(2,1)} %refs_6_.1), channel_id=1, source_target_pairs={{0,8},{8,0},{1,9},{9,1},{2,10},{10,2},{3,11},{11,3},{4,12},{12,4},... | collective-permute-start | bytes 6291464 | tf_op jit(solution)/shard_map/ppermute | solution.py:212
  7.2 9.1 %collective-permute-start.2 = (bf16[64,2048]{1,0:T(8,128)(2,1)S(1)}, bf16[64,2048]{1,0:T(8,128)(2,1)S(1)}, u32[]{:S(2)}, u32[]{:S(2)}) collective-permute-start(bf16[64,2048]{1,0:T(8,128)(2,1)S(1)} %get-tuple-element.36.refs_0_.source), channel_id=1, source_target_pairs={{0,64},{64,128},{128,192},{192,0},{1,65},{65,129},{129,193},{193,1... | collective-permute-start | bytes 786440 | tf_op jit(solution)/shard_map/ppermute | solution.py:204
  7.2 9.1 %collective-permute-start.3 = (bf16[64,2048]{1,0:T(8,128)(2,1)S(1)}, bf16[64,2048]{1,0:T(8,128)(2,1)S(1)}, u32[]{:S(2)}, u32[]{:S(2)}) collective-permute-start(bf16[64,2048]{1,0:T(8,128)(2,1)S(1)} %get-tuple-element.36.refs_0_.source), channel_id=1, source_target_pairs={{0,192},{64,0},{128,64},{192,128},{1,193},{65,1},{129,65},{193,129... | collective-permute-start | bytes 786440 | tf_op jit(solution)/shard_map/ppermute | solution.py:204
  9.8 12.0 %collective-permute-start = (bf16[64,2048]{1,0:T(8,128)(2,1)S(1)}, bf16[64,2048]{1,0:T(8,128)(2,1)S(1)}, u32[]{:S(2)}, u32[]{:S(2)}) collective-permute-start(bf16[64,2048]{1,0:T(8,128)(2,1)S(1)} %get-tuple-element.36.refs_0_.source), channel_id=1, source_target_pairs={{0,16},{16,32},{32,48},{48,0},{1,17},{17,33},{33,49},{49,1},{2,18}... | collective-permute-start | bytes 786440 | tf_op jit(solution)/shard_map/ppermute | solution.py:215
  11.1 16.2 %collective-permute-start.1 = (bf16[64,2048]{1,0:T(8,128)(2,1)S(1)}, bf16[64,2048]{1,0:T(8,128)(2,1)S(1)}, u32[]{:S(2)}, u32[]{:S(2)}) collective-permute-start(bf16[64,2048]{1,0:T(8,128)(2,1)S(1)} %get-tuple-element.36.refs_0_.source), channel_id=1, source_target_pairs={{0,48},{16,0},{32,16},{48,32},{1,49},{17,1},{33,17},{49,33},{2,50}... | collective-permute-start | bytes 786440 | tf_op jit(solution)/shard_map/ppermute | solution.py:215
  16.3 11.0 %collective-permute-start.4 = (bf16[64,2048]{1,0:T(8,128)(2,1)S(1)}, bf16[64,2048]{1,0:T(8,128)(2,1)}, u32[]{:S(2)}, u32[]{:S(2)}) collective-permute-start(bf16[64,2048]{1,0:T(8,128)(2,1)S(1)} %collective-permute-done.2.refs_1_), channel_id=1, source_target_pairs={{0,64},{64,128},{128,192},{192,0},{1,65},{65,129},{129,193},{193,1... | collective-permute-start | bytes 786440 | tf_op jit(solution)/shard_map/ppermute | solution.py:217
  17.1 18.3 %all-to-all-start = ((bf16[8,2,64,128]{3,2,1,0:T(8,128)(2,1)}), bf16[8,2,64,128]{3,2,1,0:T(8,128)(2,1)S(1)}, u32[]{:S(2)}, u32[]{:S(2)}) async-start(bf16[8,2,64,128]{3,2,1,0:T(8,128)(2,1)} %get-tuple-element.48), calls=%async_computation | async-start | bytes 524288 | tf_op jit(solution)/shard_map/all_to_all | solution.py:207
  27.3 16.0 %collective-permute-start.7 = (bf16[64,2048]{1,0:T(8,128)(2,1)S(1)}, bf16[64,2048]{1,0:T(8,128)(2,1)}, u32[]{:S(2)}, u32[]{:S(2)}) collective-permute-start(bf16[64,2048]{1,0:T(8,128)(2,1)S(1)} %collective-permute-done.refs_4_), channel_id=1, source_target_pairs={{0,64},{64,128},{128,192},{192,0},{1,65},{65,129},{129,193},{193,1... | collective-permute-start | bytes 786440 | tf_op jit(solution)/shard_map/ppermute | solution.py:204
  27.4 15.9 %collective-permute-start.8 = (bf16[64,2048]{1,0:T(8,128)(2,1)S(1)}, bf16[64,2048]{1,0:T(8,128)(2,1)}, u32[]{:S(2)}, u32[]{:S(2)}) collective-permute-start(bf16[64,2048]{1,0:T(8,128)(2,1)S(1)} %collective-permute-done.refs_4_), channel_id=1, source_target_pairs={{0,192},{64,0},{128,64},{192,128},{1,193},{65,1},{129,65},{193,129... | collective-permute-start | bytes 786440 | tf_op jit(solution)/shard_map/ppermute | solution.py:204
  30.0 13.2 %collective-permute-start.10 = (bf16[64,2048]{1,0:T(8,128)(2,1)S(1)}, bf16[64,2048]{1,0:T(8,128)(2,1)}, u32[]{:S(2)}, u32[]{:S(2)}) collective-permute-start(bf16[64,2048]{1,0:T(8,128)(2,1)S(1)} %collective-permute-done.1.refs_7_), channel_id=1, source_target_pairs={{0,192},{64,0},{128,64},{192,128},{1,193},{65,1},{129,65},{193,129... | collective-permute-start | bytes 786440 | tf_op jit(solution)/shard_map/ppermute | solution.py:204
  30.1 13.2 %collective-permute-start.9 = (bf16[64,2048]{1,0:T(8,128)(2,1)S(1)}, bf16[64,2048]{1,0:T(8,128)(2,1)}, u32[]{:S(2)}, u32[]{:S(2)}) collective-permute-start(bf16[64,2048]{1,0:T(8,128)(2,1)S(1)} %collective-permute-done.1.refs_7_), channel_id=1, source_target_pairs={{0,64},{64,128},{128,192},{192,0},{1,65},{65,129},{129,193},{193,1... | collective-permute-start | bytes 786440 | tf_op jit(solution)/shard_map/ppermute | solution.py:204
  31.5 11.8 %collective-permute-start.6 = (bf16[64,2048]{1,0:T(8,128)(2,1)S(1)}, bf16[64,2048]{1,0:T(8,128)(2,1)S(1)}, u32[]{:S(2)}, u32[]{:S(2)}) collective-permute-start(bf16[64,2048]{1,0:T(8,128)(2,1)S(1)} %get-tuple-element.36.refs_0_.source), channel_id=1, source_target_pairs={{0,32},{16,48},{32,0},{48,16},{1,33},{17,49},{33,1},{49,17},{2,34}... | collective-permute-start | bytes 786440 | tf_op jit(solution)/shard_map/ppermute | solution.py:221
  37.7 21.3 %all-to-all-start.1 = ((bf16[16,64,128]{2,1,0:T(8,128)(2,1)}), bf16[16,64,128]{2,1,0:T(8,128)(2,1)S(1)}, u32[]{:S(2)}, u32[]{:S(2)}) async-start(bf16[16,64,128]{2,1,0:T(8,128)(2,1)} %shard_map.62), calls=%async_computation.1 | async-start | bytes 524288 | tf_op jit(solution)/shard_map/all_to_all | solution.py:210
  43.3 15.8 %collective-permute-start.11 = (bf16[64,2048]{1,0:T(8,128)(2,1)}, bf16[64,2048]{1,0:T(8,128)(2,1)S(1)}, u32[]{:S(2)}, u32[]{:S(2)}) collective-permute-start(bf16[64,2048]{1,0:T(8,128)(2,1)} %collective-permute-done.7.refs_5_), channel_id=1, source_target_pairs={{0,64},{64,128},{128,192},{192,0},{1,65},{65,129},{129,193},{193,1... | collective-permute-start | bytes 786440 | tf_op jit(solution)/shard_map/ppermute | solution.py:226
  44.7 14.3 %collective-permute-start.12 = (bf16[64,2048]{1,0:T(8,128)(2,1)}, bf16[64,2048]{1,0:T(8,128)(2,1)S(1)}, u32[]{:S(2)}, u32[]{:S(2)}) collective-permute-start(bf16[64,2048]{1,0:T(8,128)(2,1)} %collective-permute-done.10.refs_9_), channel_id=1, source_target_pairs={{0,192},{64,0},{128,64},{192,128},{1,193},{65,1},{129,65},{193,129... | collective-permute-start | bytes 786440 | tf_op jit(solution)/shard_map/ppermute | solution.py:226
  46.1 13.0 %collective-permute-start.13 = (bf16[64,2048]{1,0:T(8,128)(2,1)S(1)}, bf16[64,2048]{1,0:T(8,128)(2,1)S(1)}, u32[]{:S(2)}, u32[]{:S(2)}) collective-permute-start(bf16[64,2048]{1,0:T(8,128)(2,1)S(1)} %collective-permute-done.6.refs_2_), channel_id=1, source_target_pairs={{0,64},{64,128},{128,192},{192,0},{1,65},{65,129},{129,193},{193,1... | collective-permute-start | bytes 786440 | tf_op jit(solution)/shard_map/ppermute | solution.py:204
  46.2 12.9 %collective-permute-start.14 = (bf16[64,2048]{1,0:T(8,128)(2,1)S(1)}, bf16[64,2048]{1,0:T(8,128)(2,1)}, u32[]{:S(2)}, u32[]{:S(2)}) collective-permute-start(bf16[64,2048]{1,0:T(8,128)(2,1)S(1)} %collective-permute-done.6.refs_2_), channel_id=1, source_target_pairs={{0,192},{64,0},{128,64},{192,128},{1,193},{65,1},{129,65},{193,129... | collective-permute-start | bytes 786440 | tf_op jit(solution)/shard_map/ppermute | solution.py:204
  59.1 22.0 %all-to-all-start.2 = ((f16[8,640,128]{2,1,0:T(8,128)(2,1)}), f16[8,640,128]{2,1,0:T(8,128)(2,1)}, u32[]{:S(2)}, u32[]{:S(2)}) async-start(f16[8,640,128]{2,1,0:T(8,128)(2,1)} %convert_element_type.12), calls=%async_computation.2 | async-start | bytes 2621440 | tf_op jit(solution)/shard_map/all_to_all | solution.py:207
  67.4 6.4 %collective-permute-start.15 = (bf16[64,2048]{1,0:T(8,128)(2,1)S(1)}, bf16[64,2048]{1,0:T(8,128)(2,1)S(1)}, u32[]{:S(2)}, u32[]{:S(2)}) collective-permute-start(bf16[64,2048]{1,0:T(8,128)(2,1)S(1)} %collective-permute-done.13.refs_3_), channel_id=1, source_target_pairs={{0,64},{64,128},{128,192},{192,0},{1,65},{65,129},{129,193},{193,1... | collective-permute-start | bytes 786440 | tf_op jit(solution)/shard_map/ppermute | solution.py:232
  81.1 18.4 %all-to-all-start.3 = ((f16[8,384,128]{2,1,0:T(8,128)(2,1)}), f16[8,384,128]{2,1,0:T(8,128)(2,1)S(1)}, u32[]{:S(2)}, u32[]{:S(2)}) async-start(f16[8,384,128]{2,1,0:T(8,128)(2,1)} %convert_element_type.13), calls=%async_computation.3 | async-start | bytes 1572864 | tf_op jit(solution)/shard_map/all_to_all | solution.py:207
  88.7 10.9 %collective-permute-start.16 = (bf16[16,64,128]{2,1,0:T(8,128)(2,1)S(1)}, bf16[16,64,128]{2,1,0:T(8,128)(2,1)S(1)}, u32[]{:S(2)}, u32[]{:S(2)}) collective-permute-start(bf16[16,64,128]{2,1,0:T(8,128)(2,1)S(1)} %all-to-all-done.1.mine), channel_id=1, source_target_pairs={{0,8},{8,0},{1,9},{9,1},{2,10},{10,2},{3,11},{11,3},{4,12},{12,4},... | collective-permute-start | bytes 786440 | tf_op jit(solution)/shard_map/ppermute | solution.py:237
  101.8 20.0 %all-to-all-start.4 = ((f32[8,8,2,8,256]{4,3,2,1,0:T(8,128)}), f32[8,8,2,8,256]{4,3,2,1,0:T(8,128)S(1)}, u32[]{:S(2)}, u32[]{:S(2)}) async-start(f32[8,8,2,8,256]{4,3,2,1,0:T(8,128)} %get-tuple-element.57), calls=%async_computation.4 | async-start | bytes 2097152 | tf_op jit(solution)/shard_map/all_to_all | solution.py:207
  106.9 2.0 %collective-permute-start.17 = (f32[4,4,4,8,128]{4,3,2,1,0:T(8,128)S(1)}, f32[4,4,4,8,128]{4,3,2,1,0:T(8,128)S(1)}, u32[]{:S(2)}, u32[]{:S(2)}) collective-permute-start(f32[4,4,4,8,128]{4,3,2,1,0:T(8,128)S(1)} %get-tuple-element.59), channel_id=1, source_target_pairs={{0,8},{8,0},{1,9},{9,1},{2,10},{10,2},{3,11},{11,3},{4,12},{12,4},... | collective-permute-start | bytes 786440 | tf_op jit(solution)/shard_map/ppermute | solution.py:239
  136.9 3.2 %collective-permute-start.18 = (f32[8,128]{1,0:T(8,128)S(1)}, f32[8,128]{1,0:T(8,128)S(1)}, u32[]{:S(2)}, u32[]{:S(2)}) collective-permute-start(f32[8,128]{1,0:T(8,128)S(1)} %slice_bitcast_fusion), channel_id=1, source_target_pairs={{0,8},{8,0},{1,9},{9,1},{2,10},{10,2},{3,11},{11,3},{4,12},{12,4},... | collective-permute-start | bytes 12296 | tf_op jit(solution)/shard_map/ppermute | solution.py:246
  (14 other events, 167.0 us)

commit v4 on v3

--- a/solution.py
+++ b/solution.py
@@ -17,38 +17,40 @@
 
 
 def mask_kernel(ids, mask, panel, own, pieces):
-    ic, col = ids[2], ids[3]
+    ic, col, t = ids[2], ids[3], pl.program_id(0)
     upper = lax.broadcasted_iota(jnp.int32, (16, 256), 0) < 8
     low = lax.broadcasted_iota(jnp.int32, (16, 128), 1) < 64
-    for t in range(4):
-        rows = slice(16 * t, 16 * t + 16)
-        blocks = []
-        for i in range(8):
-            lanes = slice(256 * i, 256 * i + 256)
-            here = jnp.where(upper, mask[2 * t, col * 8 + i], mask[2 * t + 1, col * 8 + i]).astype(jnp.float32)
-            blocks.append(panel[rows, lanes].astype(jnp.float32) * here)
-            own[rows, lanes] = blocks[-1].astype(own.dtype)
-        for b in range(2):
-            for h in range(2):
-                even, odd = blocks[4 * b + h], blocks[4 * b + 2 + h]
-                first, second = jnp.where(ic == 0, even, odd), jnp.where(ic == 0, odd, even)
-                for u in range(2):
-                    p, q = first[:, 128 * u:128 * u + 128], second[:, 128 * u:128 * u + 128]
-                    j = 4 * h + 2 * u
-                    pieces[j, b, rows, :] = jnp.where(low, p, pltpu.roll(q, 64, 1)).astype(pieces.dtype)
-                    pieces[j + 1, b, rows, :] = jnp.where(low, pltpu.roll(p, 64, 1), q).astype(pieces.dtype)
+    blocks = []
+    for i in range(8):
+        lanes = slice(256 * i, 256 * i + 256)
+        here = jnp.where(upper, mask[2 * t, col * 8 + i], mask[2 * t + 1, col * 8 + i]).astype(jnp.float32)
+        blocks.append(panel[:, lanes].astype(jnp.float32) * here)
+        own[:, lanes] = blocks[-1].astype(own.dtype)
+    for b in range(2):
+        for h in range(2):
+            even, odd = blocks[4 * b + h], blocks[4 * b + 2 + h]
+            first, second = jnp.where(ic == 0, even, odd), jnp.where(ic == 0, odd, even)
+            for u in range(2):
+                p, q = first[:, 128 * u:128 * u + 128], second[:, 128 * u:128 * u + 128]
+                j = 4 * h + 2 * u
+                pieces[j, b] = jnp.where(low, p, pltpu.roll(q, 64, 1)).astype(pieces.dtype)
+                pieces[j + 1, b] = jnp.where(low, pltpu.roll(p, 64, 1), q).astype(pieces.dtype)
 
 
 def mask_call(ids, mask, panel):
     return pl.pallas_call(
         mask_kernel,
+        grid=(4,),
         out_shape=(
             jax.ShapeDtypeStruct((64, 2048), jnp.bfloat16),
             jax.ShapeDtypeStruct((8, 2, 64, 128), jnp.bfloat16),
         ),
-        in_specs=[SMEM, SMEM, VMEM],
-        out_specs=(VMEM, VMEM),
-        compiler_params=pltpu.CompilerParams(vmem_limit_bytes=16 * 2**20),
+        in_specs=[SMEM, SMEM, pl.BlockSpec((16, 2048), lambda t: (t, 0))],
+        out_specs=(
+            pl.BlockSpec((16, 2048), lambda t: (t, 0)),
+            pl.BlockSpec((8, 2, 16, 128), lambda t: (0, 0, t, 0)),
+        ),
+        compiler_params=pltpu.CompilerParams(vmem_limit_bytes=60 * 2**20),
         cost_estimate=pl.CostEstimate(flops=1, bytes_accessed=2**20, transcendentals=0),
     )(ids, mask, panel)
 
@@ -101,16 +103,17 @@
 
 
 def hold_kernel(after, source, out):
-    out[...] = source[...]
+    pass
 
 
 def hold_call(after, value):
     return pl.pallas_call(
         hold_kernel,
         out_shape=jax.ShapeDtypeStruct(value.shape, value.dtype),
-        in_specs=[ANY, VMEM],
-        out_specs=VMEM,
-        cost_estimate=pl.CostEstimate(flops=2**34, bytes_accessed=2**19, transcendentals=0),
+        in_specs=[ANY, ANY],
+        out_specs=ANY,
+        input_output_aliases={1: 0},
+        cost_estimate=pl.CostEstimate(flops=2**34, bytes_accessed=2**12, transcendentals=0),
     )(after, value)
 
 
@@ -237,7 +240,7 @@
     other = lax.ppermute(mine, "core", swap)
     keep, give, diag = diag_call(ids, sum_parts(parts), sum_parts(to_columns(late)), mine, other)
     got = lax.ppermute(give, "core", swap)
-    here = jnp.sum(to_columns(diag), axis=0)
+    here = jnp.sum(to_columns(diag.astype(jnp.float16)).astype(jnp.float32), axis=0)
     panel_inverse = rows_call(ids, keep, got)
     here, panel_inverse = lax.optimization_barrier((here, panel_inverse))
     across = here.reshape(128, 256).T.reshape(2, 16, 8, 128)

time: 142 us -> 138 us (0.972)
  waiting for transfers between devices: 37.5 us -> 21.3 us
  starting transfers between devices: 57.8 us -> 66.2 us
  blocking collectives: 14.9 us -> 19.4 us
  local copies, waits for them, and re-layouts: 5.34 us -> 3.61 us
  other arithmetic: 6.6 us -> 8.02 us
    all_to_all x4, waiting for transfers between devices: 20.7 us -> 3.06 us  [to_columns(): return lax.all_to_all(value, ('zl', 'y'), 0, 0, tiled=True)]
    all_to_all x1, blocking collectives: 14.9 us -> 19.4 us  [to_rows(): return lax.all_to_all(value, ('x', 'zh'), 0, 0, tiled=True)]
    ppermute x1, starting transfers between devices: 0.82 us -> 4.49 us  [shards(): got = lax.ppermute(give, 'core', swap)]
    ppermute x1, starting transfers between devices: 1.07 us -> 3.73 us  [shards(): other = lax.ppermute(mine, 'core', swap)]
    ppermute x1, waiting for transfers between devices: 0.01 us -> 1.84 us  [shards(): z2 = lax.ppermute(own, 'zh', turn(4, 2))]
    unnamed x28 -> x22, local copies, waits for them, and re-layouts: 4.7 us -> 2.96 us
    pallas_call x1, Pallas kernels: 1.47 us -> 3.2 us  [mask_call(): pl.pallas_call(mask_kernel, grid=(4,), out_shape=(jax.ShapeDtypeStruct((6...]
    ppermute x1, starting transfers between devices: 2.34 us -> 4.03 us  [shards(): came = lax.ppermute(here[1], 'core', swap)]
  transfers between devices with their start and end apart: 24 -> 24, of which waited for: 9 -> 8; matrix products, arithmetic and copies ran while one was open for 4% -> 5% of each run, Pallas kernels for 11% -> 12%
where the time goes in v4:
time: 138 us; the launch traced here: 137 us
  starting transfers between devices  66.2 us (48%)
  waiting for transfers between devices  21.3 us (15%)
  blocking collectives  19.4 us (14%)
  Pallas kernels  17.4 us (13%)
  other arithmetic  8.02 us (6%)
  local copies, waits for them, and re-layouts  3.61 us (3%)
    all_to_all x4, starting transfers between devices, to_columns(): return lax.all_to_all(value, ('zl', 'y'), 0, 0, tiled=True)  25.9 us
    all_to_all x1, blocking collectives, to_rows(): return lax.all_to_all(value, ('x', 'zh'), 0, 0, tiled=True)  19.4 us
    pallas_call x2, Pallas kernels, product_call(): pl.pallas_call(product_kernel, grid=(4,), out_shape=jax.ShapeDtypeStruct(...  10.9 us
    ppermute x4, starting transfers between devices, around(): lax.ppermute(slab, 'x', turn(4, -1))  8.07 us
    ppermute x1, waiting for transfers between devices, shards(): far2 = lax.ppermute(near2[0], 'x', turn(4, 1))  6.42 us
    ppermute x2, waiting for transfers between devices, shards(): z1, z3 = (lax.ppermute(own, 'zh', turn(4, s)) for s in (1, 3))  5.59 us
    all_to_all x1, starting transfers between devices, to_rows(): return lax.all_to_all(value, ('x', 'zh'), 0, 0, tiled=True)  5.53 us
    ppermute x1, starting transfers between devices, shards(): got = lax.ppermute(give, 'core', swap)  4.49 us
  transfers between devices with their start and end apart: 24, of which 8 were waited for; matrix products, arithmetic and copies ran while one was open for 5% of the time, Pallas kernels for 12%

profile of v4, /device:TPU:1, one launch (start us, length us, event | category | flops | bytes accessed | tf_op | source)
XLA Modules:
  0.0 136.9 jit_solution(3755373090306087557)
XLA Ops:
  0.6 3.3 %collective-permute-start.5 = (bf16[512,2048]{1,0:T(8,128)(2,1)}, bf16[512,2048]{1,0:T(8,128)(2,1)S(1)}, u32[]{:S(2)}, u32[]{:S(2)}) collective-permute-start(bf16[512,2048]{1,0:T(8,128)(2,1)} %refs_6_.1), channel_id=1, source_target_pairs={{0,8},{8,0},{1,9},{9,1},{2,10},{10,2},{3,11},{11,3},{4,12},{12,4},... | collective-permute-start | bytes 6291464 | tf_op jit(solution)/shard_map/ppermute | solution.py:215
  4.5 3.2 %shard_map.59 = (bf16[64,2048]{1,0:T(8,128)(2,1)}, bf16[8,2,64,128]{3,2,1,0:T(8,128)(2,1)}) custom-call(s32[4]{0:T(128)} %pad_add_fusion.ids, s32[8,64]{1,0:T(8,128)} %mask.1, bf16[64,2048]{1,0:T(8,128)(2,1)} %bitcast.26), custom_call_target="tpu_custom_call" | custom-call | flops 1 | bytes 1048576 | tf_op jit(solution)/shard_map/pallas_call | solution.py:41
  7.7 2.7 %collective-permute-start.3 = (bf16[64,2048]{1,0:T(8,128)(2,1)}, bf16[64,2048]{1,0:T(8,128)(2,1)S(1)}, u32[]{:S(2)}, u32[]{:S(2)}) collective-permute-start(bf16[64,2048]{1,0:T(8,128)(2,1)} %get-tuple-element.36.refs_0_.source), channel_id=1, source_target_pairs={{0,192},{64,0},{128,64},{192,128},{1,193},{65,1},{129,65},{193,129... | collective-permute-start | bytes 786440 | tf_op jit(solution)/shard_map/ppermute | solution.py:207
  11.7 3.0 %collective-permute-start.1 = (bf16[64,2048]{1,0:T(8,128)(2,1)}, bf16[64,2048]{1,0:T(8,128)(2,1)S(1)}, u32[]{:S(2)}, u32[]{:S(2)}) collective-permute-start(bf16[64,2048]{1,0:T(8,128)(2,1)} %get-tuple-element.36.refs_0_.source), channel_id=1, source_target_pairs={{0,48},{16,0},{32,16},{48,32},{1,49},{17,1},{33,17},{49,33},{2,50}... | collective-permute-start | bytes 786440 | tf_op jit(solution)/shard_map/ppermute | solution.py:218
  14.7 2.4 %collective-permute-done.2.refs_1_ = bf16[64,2048]{1,0:T(8,128)(2,1)S(1)} collective-permute-done((bf16[64,2048]{1,0:T(8,128)(2,1)}, bf16[64,2048]{1,0:T(8,128)(2,1)S(1)}, u32[]{:S(2)}, u32[]{:S(2)}) %collective-permute-start.2) | collective-permute-done | bytes 262176 | tf_op jit(solution)/shard_map/ppermute | solution.py:207
  17.8 4.7 %all-to-all-start = ((bf16[8,2,64,128]{3,2,1,0:T(8,128)(2,1)}), bf16[8,2,64,128]{3,2,1,0:T(8,128)(2,1)}, u32[]{:S(2)}, u32[]{:S(2)}) async-start(bf16[8,2,64,128]{3,2,1,0:T(8,128)(2,1)} %get-tuple-element.48), calls=%async_computation | async-start | bytes 524288 | tf_op jit(solution)/shard_map/all_to_all | solution.py:210
  22.7 5.4 %collective-permute-done.1.refs_7_ = bf16[64,2048]{1,0:T(8,128)(2,1)S(1)} collective-permute-done((bf16[64,2048]{1,0:T(8,128)(2,1)}, bf16[64,2048]{1,0:T(8,128)(2,1)S(1)}, u32[]{:S(2)}, u32[]{:S(2)}) %collective-permute-start.1) | collective-permute-done | bytes 262176 | tf_op jit(solution)/shard_map/ppermute | solution.py:218
  28.2 2.7 %collective-permute-start.8 = (bf16[64,2048]{1,0:T(8,128)(2,1)S(1)}, bf16[64,2048]{1,0:T(8,128)(2,1)S(1)}, u32[]{:S(2)}, u32[]{:S(2)}) collective-permute-start(bf16[64,2048]{1,0:T(8,128)(2,1)S(1)} %collective-permute-done.refs_4_), channel_id=1, source_target_pairs={{0,192},{64,0},{128,64},{192,128},{1,193},{65,1},{129,65},{193,129... | collective-permute-start | bytes 786440 | tf_op jit(solution)/shard_map/ppermute | solution.py:207
  32.3 3.2 %collective-permute-start.6 = (bf16[64,2048]{1,0:T(8,128)(2,1)}, bf16[64,2048]{1,0:T(8,128)(2,1)S(1)}, u32[]{:S(2)}, u32[]{:S(2)}) collective-permute-start(bf16[64,2048]{1,0:T(8,128)(2,1)} %get-tuple-element.36.refs_0_.source), channel_id=1, source_target_pairs={{0,32},{16,48},{32,0},{48,16},{1,33},{17,49},{33,1},{49,17},{2,34}... | collective-permute-start | bytes 786440 | tf_op jit(solution)/shard_map/ppermute | solution.py:224
  36.2 5.5 %all-to-all-start.1 = ((bf16[16,64,128]{2,1,0:T(8,128)(2,1)}), bf16[16,64,128]{2,1,0:T(8,128)(2,1)S(1)}, u32[]{:S(2)}, u32[]{:S(2)}) async-start(bf16[16,64,128]{2,1,0:T(8,128)(2,1)} %shard_map.62), calls=%async_computation.1 | async-start | bytes 524288 | tf_op jit(solution)/shard_map/all_to_all | solution.py:213
  44.3 2.1 %collective-permute-start.12 = (bf16[64,2048]{1,0:T(8,128)(2,1)}, bf16[64,2048]{1,0:T(8,128)(2,1)S(1)}, u32[]{:S(2)}, u32[]{:S(2)}) collective-permute-start(bf16[64,2048]{1,0:T(8,128)(2,1)} %collective-permute-done.10.refs_9_), channel_id=1, source_target_pairs={{0,192},{64,0},{128,64},{192,128},{1,193},{65,1},{129,65},{193,129... | collective-permute-start | bytes 786440 | tf_op jit(solution)/shard_map/ppermute | solution.py:229
  46.3 2.7 %collective-permute-start.14 = (bf16[64,2048]{1,0:T(8,128)(2,1)S(1)}, bf16[64,2048]{1,0:T(8,128)(2,1)}, u32[]{:S(2)}, u32[]{:S(2)}) collective-permute-start(bf16[64,2048]{1,0:T(8,128)(2,1)S(1)} %collective-permute-done.6.refs_2_), channel_id=1, source_target_pairs={{0,192},{64,0},{128,64},{192,128},{1,193},{65,1},{129,65},{193,129... | collective-permute-start | bytes 786440 | tf_op jit(solution)/shard_map/ppermute | solution.py:207
  49.0 7.3 %shard_map.60 = f32[8,640,128]{2,1,0:T(8,128)} custom-call(s32[4]{0:T(128)} %pad_add_fusion.ids, bf16[64,2048]{1,0:T(8,128)(2,1)} %get-tuple-element.36.refs_0_.source, bf16[64,2048]{1,0:T(8,128)(2,1)} %copy-done.5, bf16[64,2048]{1,0:T(8,128)(2,1)} %copy-done.6, bf16[64,2048]{1,0:T(8,128)(2,1)} %copy-done.9, bf16[64,2048]{1,0:T(8,128)(2,1)} %copy-done.7, ...), custom_call_target="tpu_custom_call" | custom-call | flops 2684354560 | bytes 8912896 | tf_op jit(solution)/shard_map/pallas_call | solution.py:78
  56.3 3.0 %convert_element_type.18 = f16[8,640,128]{2,1,0:T(8,128)(2,1)} convert(f32[8,640,128]{2,1,0:T(8,128)} %shard_map.60) | non-fusion elementwise | flops 655360 | bytes 3932160 | tf_op jit(solution)/shard_map/convert_element_type | solution.py:204
  59.4 9.1 %all-to-all-start.2 = ((f16[8,640,128]{2,1,0:T(8,128)(2,1)}), f16[8,640,128]{2,1,0:T(8,128)(2,1)}, u32[]{:S(2)}, u32[]{:S(2)}) async-start(f16[8,640,128]{2,1,0:T(8,128)(2,1)} %convert_element_type.18), calls=%async_computation.2 | async-start | bytes 2621440 | tf_op jit(solution)/shard_map/all_to_all | solution.py:210
  68.5 6.4 %collective-permute-done.15.refs_5_ = bf16[64,2048]{1,0:T(8,128)(2,1)S(1)} collective-permute-done((bf16[64,2048]{1,0:T(8,128)(2,1)S(1)}, bf16[64,2048]{1,0:T(8,128)(2,1)S(1)}, u32[]{:S(2)}, u32[]{:S(2)}) %collective-permute-start.15) | collective-permute-done | bytes 262176 | tf_op jit(solution)/shard_map/ppermute | solution.py:235
  76.5 3.6 %shard_map.63 = f32[8,384,128]{2,1,0:T(8,128)S(1)} custom-call(s32[4]{0:T(128)S(1)} %copy-done.3, bf16[64,2048]{1,0:T(8,128)(2,1)S(1)} %collective-permute-done.11.refs_0_, bf16[64,2048]{1,0:T(8,128)(2,1)S(1)} %collective-permute-done.12.refs_1_, bf16[64,2048]{1,0:T(8,128)(2,1)S(1)} %collective-permute-done.6.refs_2_, ...), custom_call_target="tpu_custom_call" | custom-call | flops 1610612736 | bytes 7864320 | tf_op jit(solution)/shard_map/pallas_call | solution.py:78
  81.1 8.1 %all-to-all-start.3 = ((f16[8,384,128]{2,1,0:T(8,128)(2,1)}), f16[8,384,128]{2,1,0:T(8,128)(2,1)S(1)}, u32[]{:S(2)}, u32[]{:S(2)}) async-start(f16[8,384,128]{2,1,0:T(8,128)(2,1)} %convert_element_type.19), calls=%async_computation.3 | async-start | bytes 1572864 | tf_op jit(solution)/shard_map/all_to_all | solution.py:210
  89.2 3.7 %collective-permute-start.16 = (bf16[16,64,128]{2,1,0:T(8,128)(2,1)S(1)}, bf16[16,64,128]{2,1,0:T(8,128)(2,1)S(1)}, u32[]{:S(2)}, u32[]{:S(2)}) collective-permute-start(bf16[16,64,128]{2,1,0:T(8,128)(2,1)S(1)} %all-to-all-done.1.mine), channel_id=1, source_target_pairs={{0,8},{8,0},{1,9},{9,1},{2,10},{10,2},{3,11},{11,3},{4,12},{12,4},... | collective-permute-start | bytes 786440 | tf_op jit(solution)/shard_map/ppermute | solution.py:240
  94.5 3.1 %all-to-all-done.3 = f16[8,384,128]{2,1,0:T(8,128)(2,1)S(1)} async-done(((f16[8,384,128]{2,1,0:T(8,128)(2,1)}), f16[8,384,128]{2,1,0:T(8,128)(2,1)S(1)}, u32[]{:S(2)}, u32[]{:S(2)}) %all-to-all-start.3) | async-done | bytes 786464 | tf_op jit(solution)/shard_map/all_to_all | solution.py:210
  99.8 4.0 %all-to-all-start.4 = ((f16[8,8,2,8,256]{4,3,2,1,0:T(8,128)(2,1)}), f16[8,8,2,8,256]{4,3,2,1,0:T(8,128)(2,1)S(1)}, u32[]{:S(2)}, u32[]{:S(2)}) async-start(f16[8,8,2,8,256]{4,3,2,1,0:T(8,128)(2,1)} %convert_element_type.22), calls=%async_computation.4 | async-start | bytes 1048576 | tf_op jit(solution)/shard_map/all_to_all | solution.py:210
  103.9 4.5 %collective-permute-start.17 = (f32[4,4,4,8,128]{4,3,2,1,0:T(8,128)S(1)}, f32[4,4,4,8,128]{4,3,2,1,0:T(8,128)S(1)}, u32[]{:S(2)}, u32[]{:S(2)}) collective-permute-start(f32[4,4,4,8,128]{4,3,2,1,0:T(8,128)S(1)} %get-tuple-element.59), channel_id=1, source_target_pairs={{0,8},{8,0},{1,9},{9,1},{2,10},{10,2},{3,11},{11,3},{4,12},{12,4},... | collective-permute-start | bytes 786440 | tf_op jit(solution)/shard_map/ppermute | solution.py:242
  111.3 19.4 %all_to_all.30 = f32[16,2,8,128]{3,2,1,0:T(8,128)S(1)} all-to-all(f32[16,2,8,128]{3,2,1,0:T(8,128)S(1)} %copy.10), channel_id=1, replica_groups=mesh['x'=4,'zh'=4,'core'=2,'zl'=2,'y'=4] {'x','zh'}, dimensions={0} | all-to-all | bytes 262144 | tf_op jit(solution)/shard_map/all_to_all | solution.py:213
  130.8 4.0 %collective-permute-start.18 = (f32[8,128]{1,0:T(8,128)S(1)}, f32[8,128]{1,0:T(8,128)S(1)}, u32[]{:S(2)}, u32[]{:S(2)}) collective-permute-start(f32[8,128]{1,0:T(8,128)S(1)} %slice_bitcast_fusion), channel_id=1, source_target_pairs={{0,8},{8,0},{1,9},{9,1},{2,10},{10,2},{3,11},{11,3},{4,12},{12,4},... | collective-permute-start | bytes 12296 | tf_op jit(solution)/shard_map/ppermute | solution.py:249
  (74 shorter events, 18.9 us)
Async XLA Ops:
  0.6 27.5 %collective-permute-start.5 = (bf16[512,2048]{1,0:T(8,128)(2,1)}, bf16[512,2048]{1,0:T(8,128)(2,1)S(1)}, u32[]{:S(2)}, u32[]{:S(2)}) collective-permute-start(bf16[512,2048]{1,0:T(8,128)(2,1)} %refs_6_.1), channel_id=1, source_target_pairs={{0,8},{8,0},{1,9},{9,1},{2,10},{10,2},{3,11},{11,3},{4,12},{12,4},... | collective-permute-start | bytes 6291464 | tf_op jit(solution)/shard_map/ppermute | solution.py:215
  7.7 9.3 %collective-permute-start.2 = (bf16[64,2048]{1,0:T(8,128)(2,1)}, bf16[64,2048]{1,0:T(8,128)(2,1)S(1)}, u32[]{:S(2)}, u32[]{:S(2)}) collective-permute-start(bf16[64,2048]{1,0:T(8,128)(2,1)} %get-tuple-element.36.refs_0_.source), channel_id=1, source_target_pairs={{0,64},{64,128},{128,192},{192,0},{1,65},{65,129},{129,193},{193,1... | collective-permute-start | bytes 786440 | tf_op jit(solution)/shard_map/ppermute | solution.py:207
  7.7 9.3 %collective-permute-start.3 = (bf16[64,2048]{1,0:T(8,128)(2,1)}, bf16[64,2048]{1,0:T(8,128)(2,1)S(1)}, u32[]{:S(2)}, u32[]{:S(2)}) collective-permute-start(bf16[64,2048]{1,0:T(8,128)(2,1)} %get-tuple-element.36.refs_0_.source), channel_id=1, source_target_pairs={{0,192},{64,0},{128,64},{192,128},{1,193},{65,1},{129,65},{193,129... | collective-permute-start | bytes 786440 | tf_op jit(solution)/shard_map/ppermute | solution.py:207
  10.4 12.2 %collective-permute-start = (bf16[64,2048]{1,0:T(8,128)(2,1)}, bf16[64,2048]{1,0:T(8,128)(2,1)S(1)}, u32[]{:S(2)}, u32[]{:S(2)}) collective-permute-start(bf16[64,2048]{1,0:T(8,128)(2,1)} %get-tuple-element.36.refs_0_.source), channel_id=1, source_target_pairs={{0,16},{16,32},{32,48},{48,0},{1,17},{17,33},{33,49},{49,1},{2,18}... | collective-permute-start | bytes 786440 | tf_op jit(solution)/shard_map/ppermute | solution.py:218
  11.7 16.4 %collective-permute-start.1 = (bf16[64,2048]{1,0:T(8,128)(2,1)}, bf16[64,2048]{1,0:T(8,128)(2,1)S(1)}, u32[]{:S(2)}, u32[]{:S(2)}) collective-permute-start(bf16[64,2048]{1,0:T(8,128)(2,1)} %get-tuple-element.36.refs_0_.source), channel_id=1, source_target_pairs={{0,48},{16,0},{32,16},{48,32},{1,49},{17,1},{33,17},{49,33},{2,50}... | collective-permute-start | bytes 786440 | tf_op jit(solution)/shard_map/ppermute | solution.py:218
  17.8 10.3 %collective-permute-start.4 = (bf16[64,2048]{1,0:T(8,128)(2,1)S(1)}, bf16[64,2048]{1,0:T(8,128)(2,1)S(1)}, u32[]{:S(2)}, u32[]{:S(2)}) collective-permute-start(bf16[64,2048]{1,0:T(8,128)(2,1)S(1)} %collective-permute-done.2.refs_1_), channel_id=1, source_target_pairs={{0,64},{64,128},{128,192},{192,0},{1,65},{65,129},{129,193},{193,1... | collective-permute-start | bytes 786440 | tf_op jit(solution)/shard_map/ppermute | solution.py:220
  17.8 18.3 %all-to-all-start = ((bf16[8,2,64,128]{3,2,1,0:T(8,128)(2,1)}), bf16[8,2,64,128]{3,2,1,0:T(8,128)(2,1)}, u32[]{:S(2)}, u32[]{:S(2)}) async-start(bf16[8,2,64,128]{3,2,1,0:T(8,128)(2,1)} %get-tuple-element.48), calls=%async_computation | async-start | bytes 524288 | tf_op jit(solution)/shard_map/all_to_all | solution.py:210
  28.1 15.4 %collective-permute-start.7 = (bf16[64,2048]{1,0:T(8,128)(2,1)S(1)}, bf16[64,2048]{1,0:T(8,128)(2,1)}, u32[]{:S(2)}, u32[]{:S(2)}) collective-permute-start(bf16[64,2048]{1,0:T(8,128)(2,1)S(1)} %collective-permute-done.refs_4_), channel_id=1, source_target_pairs={{0,64},{64,128},{128,192},{192,0},{1,65},{65,129},{129,193},{193,1... | collective-permute-start | bytes 786440 | tf_op jit(solution)/shard_map/ppermute | solution.py:207
  28.2 15.4 %collective-permute-start.8 = (bf16[64,2048]{1,0:T(8,128)(2,1)S(1)}, bf16[64,2048]{1,0:T(8,128)(2,1)S(1)}, u32[]{:S(2)}, u32[]{:S(2)}) collective-permute-start(bf16[64,2048]{1,0:T(8,128)(2,1)S(1)} %collective-permute-done.refs_4_), channel_id=1, source_target_pairs={{0,192},{64,0},{128,64},{192,128},{1,193},{65,1},{129,65},{193,129... | collective-permute-start | bytes 786440 | tf_op jit(solution)/shard_map/ppermute | solution.py:207
  30.9 10.8 %collective-permute-start.10 = (bf16[64,2048]{1,0:T(8,128)(2,1)S(1)}, bf16[64,2048]{1,0:T(8,128)(2,1)}, u32[]{:S(2)}, u32[]{:S(2)}) collective-permute-start(bf16[64,2048]{1,0:T(8,128)(2,1)S(1)} %collective-permute-done.1.refs_7_), channel_id=1, source_target_pairs={{0,192},{64,0},{128,64},{192,128},{1,193},{65,1},{129,65},{193,129... | collective-permute-start | bytes 786440 | tf_op jit(solution)/shard_map/ppermute | solution.py:207
  30.9 12.6 %collective-permute-start.9 = (bf16[64,2048]{1,0:T(8,128)(2,1)S(1)}, bf16[64,2048]{1,0:T(8,128)(2,1)}, u32[]{:S(2)}, u32[]{:S(2)}) collective-permute-start(bf16[64,2048]{1,0:T(8,128)(2,1)S(1)} %collective-permute-done.1.refs_7_), channel_id=1, source_target_pairs={{0,64},{64,128},{128,192},{192,0},{1,65},{65,129},{129,193},{193,1... | collective-permute-start | bytes 786440 | tf_op jit(solution)/shard_map/ppermute | solution.py:207
  32.3 11.2 %collective-permute-start.6 = (bf16[64,2048]{1,0:T(8,128)(2,1)}, bf16[64,2048]{1,0:T(8,128)(2,1)S(1)}, u32[]{:S(2)}, u32[]{:S(2)}) collective-permute-start(bf16[64,2048]{1,0:T(8,128)(2,1)} %get-tuple-element.36.refs_0_.source), channel_id=1, source_target_pairs={{0,32},{16,48},{32,0},{48,16},{1,33},{17,49},{33,1},{49,17},{2,34}... | collective-permute-start | bytes 786440 | tf_op jit(solution)/shard_map/ppermute | solution.py:224
  36.2 23.2 %all-to-all-start.1 = ((bf16[16,64,128]{2,1,0:T(8,128)(2,1)}), bf16[16,64,128]{2,1,0:T(8,128)(2,1)S(1)}, u32[]{:S(2)}, u32[]{:S(2)}) async-start(bf16[16,64,128]{2,1,0:T(8,128)(2,1)} %shard_map.62), calls=%async_computation.1 | async-start | bytes 524288 | tf_op jit(solution)/shard_map/all_to_all | solution.py:213
  43.6 15.8 %collective-permute-start.11 = (bf16[64,2048]{1,0:T(8,128)(2,1)}, bf16[64,2048]{1,0:T(8,128)(2,1)S(1)}, u32[]{:S(2)}, u32[]{:S(2)}) collective-permute-start(bf16[64,2048]{1,0:T(8,128)(2,1)} %collective-permute-done.7.refs_5_), channel_id=1, source_target_pairs={{0,64},{64,128},{128,192},{192,0},{1,65},{65,129},{129,193},{193,1... | collective-permute-start | bytes 786440 | tf_op jit(solution)/shard_map/ppermute | solution.py:229
  44.3 15.1 %collective-permute-start.12 = (bf16[64,2048]{1,0:T(8,128)(2,1)}, bf16[64,2048]{1,0:T(8,128)(2,1)S(1)}, u32[]{:S(2)}, u32[]{:S(2)}) collective-permute-start(bf16[64,2048]{1,0:T(8,128)(2,1)} %collective-permute-done.10.refs_9_), channel_id=1, source_target_pairs={{0,192},{64,0},{128,64},{192,128},{1,193},{65,1},{129,65},{193,129... | collective-permute-start | bytes 786440 | tf_op jit(solution)/shard_map/ppermute | solution.py:229
  46.3 13.0 %collective-permute-start.13 = (bf16[64,2048]{1,0:T(8,128)(2,1)S(1)}, bf16[64,2048]{1,0:T(8,128)(2,1)S(1)}, u32[]{:S(2)}, u32[]{:S(2)}) collective-permute-start(bf16[64,2048]{1,0:T(8,128)(2,1)S(1)} %collective-permute-done.6.refs_2_), channel_id=1, source_target_pairs={{0,64},{64,128},{128,192},{192,0},{1,65},{65,129},{129,193},{193,1... | collective-permute-start | bytes 786440 | tf_op jit(solution)/shard_map/ppermute | solution.py:207
  46.3 13.0 %collective-permute-start.14 = (bf16[64,2048]{1,0:T(8,128)(2,1)S(1)}, bf16[64,2048]{1,0:T(8,128)(2,1)}, u32[]{:S(2)}, u32[]{:S(2)}) collective-permute-start(bf16[64,2048]{1,0:T(8,128)(2,1)S(1)} %collective-permute-done.6.refs_2_), channel_id=1, source_target_pairs={{0,192},{64,0},{128,64},{192,128},{1,193},{65,1},{129,65},{193,129... | collective-permute-start | bytes 786440 | tf_op jit(solution)/shard_map/ppermute | solution.py:207
  59.4 21.7 %all-to-all-start.2 = ((f16[8,640,128]{2,1,0:T(8,128)(2,1)}), f16[8,640,128]{2,1,0:T(8,128)(2,1)}, u32[]{:S(2)}, u32[]{:S(2)}) async-start(f16[8,640,128]{2,1,0:T(8,128)(2,1)} %convert_element_type.18), calls=%async_computation.2 | async-start | bytes 2621440 | tf_op jit(solution)/shard_map/all_to_all | solution.py:210
  68.4 6.4 %collective-permute-start.15 = (bf16[64,2048]{1,0:T(8,128)(2,1)S(1)}, bf16[64,2048]{1,0:T(8,128)(2,1)S(1)}, u32[]{:S(2)}, u32[]{:S(2)}) collective-permute-start(bf16[64,2048]{1,0:T(8,128)(2,1)S(1)} %collective-permute-done.13.refs_3_), channel_id=1, source_target_pairs={{0,64},{64,128},{128,192},{192,0},{1,65},{65,129},{129,193},{193,1... | collective-permute-start | bytes 786440 | tf_op jit(solution)/shard_map/ppermute | solution.py:235
  81.1 16.5 %all-to-all-start.3 = ((f16[8,384,128]{2,1,0:T(8,128)(2,1)}), f16[8,384,128]{2,1,0:T(8,128)(2,1)S(1)}, u32[]{:S(2)}, u32[]{:S(2)}) async-start(f16[8,384,128]{2,1,0:T(8,128)(2,1)} %convert_element_type.19), calls=%async_computation.3 | async-start | bytes 1572864 | tf_op jit(solution)/shard_map/all_to_all | solution.py:210
  89.2 8.5 %collective-permute-start.16 = (bf16[16,64,128]{2,1,0:T(8,128)(2,1)S(1)}, bf16[16,64,128]{2,1,0:T(8,128)(2,1)S(1)}, u32[]{:S(2)}, u32[]{:S(2)}) collective-permute-start(bf16[16,64,128]{2,1,0:T(8,128)(2,1)S(1)} %all-to-all-done.1.mine), channel_id=1, source_target_pairs={{0,8},{8,0},{1,9},{9,1},{2,10},{10,2},{3,11},{11,3},{4,12},{12,4},... | collective-permute-start | bytes 786440 | tf_op jit(solution)/shard_map/ppermute | solution.py:240
  99.8 11.3 %all-to-all-start.4 = ((f16[8,8,2,8,256]{4,3,2,1,0:T(8,128)(2,1)}), f16[8,8,2,8,256]{4,3,2,1,0:T(8,128)(2,1)S(1)}, u32[]{:S(2)}, u32[]{:S(2)}) async-start(f16[8,8,2,8,256]{4,3,2,1,0:T(8,128)(2,1)} %convert_element_type.22), calls=%async_computation.4 | async-start | bytes 1048576 | tf_op jit(solution)/shard_map/all_to_all | solution.py:210
  103.9 5.7 %collective-permute-start.17 = (f32[4,4,4,8,128]{4,3,2,1,0:T(8,128)S(1)}, f32[4,4,4,8,128]{4,3,2,1,0:T(8,128)S(1)}, u32[]{:S(2)}, u32[]{:S(2)}) collective-permute-start(f32[4,4,4,8,128]{4,3,2,1,0:T(8,128)S(1)} %get-tuple-element.59), channel_id=1, source_target_pairs={{0,8},{8,0},{1,9},{9,1},{2,10},{10,2},{3,11},{11,3},{4,12},{12,4},... | collective-permute-start | bytes 786440 | tf_op jit(solution)/shard_map/ppermute | solution.py:242
  130.8 4.8 %collective-permute-start.18 = (f32[8,128]{1,0:T(8,128)S(1)}, f32[8,128]{1,0:T(8,128)S(1)}, u32[]{:S(2)}, u32[]{:S(2)}) collective-permute-start(f32[8,128]{1,0:T(8,128)S(1)} %slice_bitcast_fusion), channel_id=1, source_target_pairs={{0,8},{8,0},{1,9},{9,1},{2,10},{10,2},{3,11},{11,3},{4,12},{12,4},... | collective-permute-start | bytes 12296 | tf_op jit(solution)/shard_map/ppermute | solution.py:249
  (11 other events, 112.4 us)

commit v5 on v4

--- a/solution.py
+++ b/solution.py
@@ -221,7 +221,7 @@
     pieces = to_columns(pieces)
     z1, z3, near0, far0, own, other_root = pin((z1, z3, near0, far0, own, other_root))
 
-    z2 = lax.ppermute(own, "zh", turn(4, 2))
+    z2 = lax.ppermute(z1, "zh", turn(4, 1))
     near1, near3 = around(z1), around(z3)
     mine = to_rows(hold_call(mark_call(own), pieces.reshape(16, 64, 128)))
     z2, near1, near3 = pin((z2, near1, near3))

time: 138 us -> 132 us (0.957)
  starting transfers between devices: 66.2 us -> 60.6 us
  waiting for transfers between devices: 21.3 us -> 24.3 us
  blocking collectives: 19.4 us -> 16.5 us
    all_to_all x4, starting transfers between devices: 25.9 us -> 20.4 us  [to_columns(): return lax.all_to_all(value, ('zl', 'y'), 0, 0, tiled=True)]
    ppermute x4, waiting for transfers between devices: 0.01 us -> 3.66 us  [around(): lax.ppermute(slab, 'x', turn(4, -1))]
    all_to_all x1, blocking collectives: 19.4 us -> 16.5 us  [to_rows(): return lax.all_to_all(value, ('x', 'zh'), 0, 0, tiled=True)]
    ppermute x1, waiting for transfers between devices: 1.84 us -> 0.01 us  [shards(): z2 = lax.ppermute(z1, 'zh', turn(4, 1))]
    all_to_all x1, starting transfers between devices: 5.53 us -> 3.72 us  [to_rows(): return lax.all_to_all(value, ('x', 'zh'), 0, 0, tiled=True)]
  transfers between devices with their start and end apart: 24 -> 24, of which waited for: 8 -> 10; matrix products, arithmetic and copies ran while one was open for 5% -> 5% of each run, Pallas kernels for 12% -> 12%
where the time goes in v5:
time: 132 us; the launch traced here: 131 us
  starting transfers between devices  60.6 us (46%)
  waiting for transfers between devices  24.3 us (18%)
  Pallas kernels  17.4 us (13%)
  blocking collectives  16.5 us (12%)
  other arithmetic  8.02 us (6%)
  local copies, waits for them, and re-layouts  3.74 us (3%)
    all_to_all x4, starting transfers between devices, to_columns(): return lax.all_to_all(value, ('zl', 'y'), 0, 0, tiled=True)  20.4 us
    all_to_all x1, blocking collectives, to_rows(): return lax.all_to_all(value, ('x', 'zh'), 0, 0, tiled=True)  16.5 us
    pallas_call x2, Pallas kernels, product_call(): pl.pallas_call(product_kernel, grid=(4,), out_shape=jax.ShapeDtypeStruct(...  10.8 us
    ppermute x4, starting transfers between devices, around(): lax.ppermute(slab, 'x', turn(4, -1))  8.08 us
    ppermute x1, waiting for transfers between devices, shards(): far2 = lax.ppermute(near2[0], 'x', turn(4, 1))  6.42 us
    ppermute x2, waiting for transfers between devices, shards(): z1, z3 = (lax.ppermute(own, 'zh', turn(4, s)) for s in (1, 3))  5.59 us
    ppermute x1, starting transfers between devices, shards(): got = lax.ppermute(give, 'core', swap)  4.67 us
    ppermute x2, starting transfers between devices, shards(): z1, z3 = (lax.ppermute(own, 'zh', turn(4, s)) for s in (1, 3))  4.29 us
  transfers between devices with their start and end apart: 24, of which 10 were waited for; matrix products, arithmetic and copies ran while one was open for 5% of the time, Pallas kernels for 12%

profile of v5, /device:TPU:1, one launch (start us, length us, event | category | flops | bytes accessed | tf_op | source)
XLA Modules:
  0.0 131.4 jit_solution(1138609710844946585)
XLA Ops:
  0.6 3.3 %collective-permute-start.5 = (bf16[512,2048]{1,0:T(8,128)(2,1)}, bf16[512,2048]{1,0:T(8,128)(2,1)S(1)}, u32[]{:S(2)}, u32[]{:S(2)}) collective-permute-start(bf16[512,2048]{1,0:T(8,128)(2,1)} %refs_6_.1), channel_id=1, source_target_pairs={{0,8},{8,0},{1,9},{9,1},{2,10},{10,2},{3,11},{11,3},{4,12},{12,4},... | collective-permute-start | bytes 6291464 | tf_op jit(solution)/shard_map/ppermute | solution.py:215
  4.5 3.2 %shard_map.59 = (bf16[64,2048]{1,0:T(8,128)(2,1)}, bf16[8,2,64,128]{3,2,1,0:T(8,128)(2,1)}) custom-call(s32[4]{0:T(128)} %pad_add_fusion.ids, s32[8,64]{1,0:T(8,128)} %mask.1, bf16[64,2048]{1,0:T(8,128)(2,1)} %bitcast.26), custom_call_target="tpu_custom_call" | custom-call | flops 1 | bytes 1048576 | tf_op jit(solution)/shard_map/pallas_call | solution.py:41
  7.7 2.7 %collective-permute-start.3 = (bf16[64,2048]{1,0:T(8,128)(2,1)}, bf16[64,2048]{1,0:T(8,128)(2,1)S(1)}, u32[]{:S(2)}, u32[]{:S(2)}) collective-permute-start(bf16[64,2048]{1,0:T(8,128)(2,1)} %get-tuple-element.41.refs_0_.source), channel_id=1, source_target_pairs={{0,192},{64,0},{128,64},{192,128},{1,193},{65,1},{129,65},{193,129... | collective-permute-start | bytes 786440 | tf_op jit(solution)/shard_map/ppermute | solution.py:207
  11.7 3.0 %collective-permute-start.1 = (bf16[64,2048]{1,0:T(8,128)(2,1)}, bf16[64,2048]{1,0:T(8,128)(2,1)S(1)}, u32[]{:S(2)}, u32[]{:S(2)}) collective-permute-start(bf16[64,2048]{1,0:T(8,128)(2,1)} %get-tuple-element.41.refs_0_.source), channel_id=1, source_target_pairs={{0,48},{16,0},{32,16},{48,32},{1,49},{17,1},{33,17},{49,33},{2,50}... | collective-permute-start | bytes 786440 | tf_op jit(solution)/shard_map/ppermute | solution.py:218
  17.8 4.7 %all-to-all-start = ((bf16[8,2,64,128]{3,2,1,0:T(8,128)(2,1)}), bf16[8,2,64,128]{3,2,1,0:T(8,128)(2,1)}, u32[]{:S(2)}, u32[]{:S(2)}) async-start(bf16[8,2,64,128]{3,2,1,0:T(8,128)(2,1)} %get-tuple-element.48), calls=%async_computation | async-start | bytes 524288 | tf_op jit(solution)/shard_map/all_to_all | solution.py:210
  22.7 5.4 %collective-permute-done.1.refs_7_ = bf16[64,2048]{1,0:T(8,128)(2,1)S(1)} collective-permute-done((bf16[64,2048]{1,0:T(8,128)(2,1)}, bf16[64,2048]{1,0:T(8,128)(2,1)S(1)}, u32[]{:S(2)}, u32[]{:S(2)}) %collective-permute-start.1) | collective-permute-done | bytes 262176 | tf_op jit(solution)/shard_map/ppermute | solution.py:218
  28.8 3.1 %collective-permute-start.6 = (bf16[64,2048]{1,0:T(8,128)(2,1)S(1)}, bf16[64,2048]{1,0:T(8,128)(2,1)S(1)}, u32[]{:S(2)}, u32[]{:S(2)}) collective-permute-start(bf16[64,2048]{1,0:T(8,128)(2,1)S(1)} %collective-permute-done.refs_4_), channel_id=1, source_target_pairs={{0,16},{16,32},{32,48},{48,0},{1,17},{17,33},{33,49},{49,1},{2,18}... | collective-permute-start | bytes 786440 | tf_op jit(solution)/shard_map/ppermute | solution.py:224
  31.9 2.7 %collective-permute-start.8 = (bf16[64,2048]{1,0:T(8,128)(2,1)S(1)}, bf16[64,2048]{1,0:T(8,128)(2,1)S(1)}, u32[]{:S(2)}, u32[]{:S(2)}) collective-permute-start(bf16[64,2048]{1,0:T(8,128)(2,1)S(1)} %collective-permute-done.refs_4_), channel_id=1, source_target_pairs={{0,192},{64,0},{128,64},{192,128},{1,193},{65,1},{129,65},{193,129... | collective-permute-start | bytes 786440 | tf_op jit(solution)/shard_map/ppermute | solution.py:207
  36.7 3.7 %all-to-all-start.1 = ((bf16[16,64,128]{2,1,0:T(8,128)(2,1)}), bf16[16,64,128]{2,1,0:T(8,128)(2,1)S(1)}, u32[]{:S(2)}, u32[]{:S(2)}) async-start(bf16[16,64,128]{2,1,0:T(8,128)(2,1)} %shard_map.62), calls=%async_computation.1 | async-start | bytes 524288 | tf_op jit(solution)/shard_map/all_to_all | solution.py:213
  40.4 3.6 %collective-permute-done.10.refs_9_ = bf16[64,2048]{1,0:T(8,128)(2,1)} collective-permute-done((bf16[64,2048]{1,0:T(8,128)(2,1)S(1)}, bf16[64,2048]{1,0:T(8,128)(2,1)}, u32[]{:S(2)}, u32[]{:S(2)}) %collective-permute-start.10) | collective-permute-done | bytes 262176 | tf_op jit(solution)/shard_map/ppermute | solution.py:207
  45.0 3.4 %collective-permute-start.12 = (bf16[64,2048]{1,0:T(8,128)(2,1)}, bf16[64,2048]{1,0:T(8,128)(2,1)S(1)}, u32[]{:S(2)}, u32[]{:S(2)}) collective-permute-start(bf16[64,2048]{1,0:T(8,128)(2,1)} %collective-permute-done.10.refs_9_), channel_id=1, source_target_pairs={{0,192},{64,0},{128,64},{192,128},{1,193},{65,1},{129,65},{193,129... | collective-permute-start | bytes 786440 | tf_op jit(solution)/shard_map/ppermute | solution.py:229
  48.4 2.7 %collective-permute-start.14 = (bf16[64,2048]{1,0:T(8,128)(2,1)S(1)}, bf16[64,2048]{1,0:T(8,128)(2,1)}, u32[]{:S(2)}, u32[]{:S(2)}) collective-permute-start(bf16[64,2048]{1,0:T(8,128)(2,1)S(1)} %collective-permute-done.6.refs_2_), channel_id=1, source_target_pairs={{0,192},{64,0},{128,64},{192,128},{1,193},{65,1},{129,65},{193,129... | collective-permute-start | bytes 786440 | tf_op jit(solution)/shard_map/ppermute | solution.py:207
  51.1 7.3 %shard_map.60 = f32[8,640,128]{2,1,0:T(8,128)} custom-call(s32[4]{0:T(128)} %pad_add_fusion.ids, bf16[64,2048]{1,0:T(8,128)(2,1)} %get-tuple-element.41.refs_0_.source, bf16[64,2048]{1,0:T(8,128)(2,1)} %copy-done.5, bf16[64,2048]{1,0:T(8,128)(2,1)} %copy-done.6, bf16[64,2048]{1,0:T(8,128)(2,1)} %copy-done.9, bf16[64,2048]{1,0:T(8,128)(2,1)} %copy-done.7, ...), custom_call_target="tpu_custom_call" | custom-call | flops 2684354560 | bytes 8912896 | tf_op jit(solution)/shard_map/pallas_call | solution.py:78
  58.4 3.0 %convert_element_type.18 = f16[8,640,128]{2,1,0:T(8,128)(2,1)} convert(f32[8,640,128]{2,1,0:T(8,128)} %shard_map.60) | non-fusion elementwise | flops 655360 | bytes 3932160 | tf_op jit(solution)/shard_map/convert_element_type | solution.py:204
  61.5 4.4 %all-to-all-start.2 = ((f16[8,640,128]{2,1,0:T(8,128)(2,1)}), f16[8,640,128]{2,1,0:T(8,128)(2,1)}, u32[]{:S(2)}, u32[]{:S(2)}) async-start(f16[8,640,128]{2,1,0:T(8,128)(2,1)} %convert_element_type.18), calls=%async_computation.2 | async-start | bytes 2621440 | tf_op jit(solution)/shard_map/all_to_all | solution.py:210
  66.0 6.4 %collective-permute-done.15.refs_5_ = bf16[64,2048]{1,0:T(8,128)(2,1)S(1)} collective-permute-done((bf16[64,2048]{1,0:T(8,128)(2,1)S(1)}, bf16[64,2048]{1,0:T(8,128)(2,1)S(1)}, u32[]{:S(2)}, u32[]{:S(2)}) %collective-permute-start.15) | collective-permute-done | bytes 262176 | tf_op jit(solution)/shard_map/ppermute | solution.py:235
  74.0 3.6 %shard_map.63 = f32[8,384,128]{2,1,0:T(8,128)S(1)} custom-call(s32[4]{0:T(128)S(1)} %copy-done.3, bf16[64,2048]{1,0:T(8,128)(2,1)S(1)} %collective-permute-done.11.refs_0_, bf16[64,2048]{1,0:T(8,128)(2,1)S(1)} %collective-permute-done.12.refs_1_, bf16[64,2048]{1,0:T(8,128)(2,1)S(1)} %collective-permute-done.6.refs_2_, ...), custom_call_target="tpu_custom_call" | custom-call | flops 1610612736 | bytes 7864320 | tf_op jit(solution)/shard_map/pallas_call | solution.py:78
  79.2 7.1 %all-to-all-start.3 = ((f16[8,384,128]{2,1,0:T(8,128)(2,1)}), f16[8,384,128]{2,1,0:T(8,128)(2,1)S(1)}, u32[]{:S(2)}, u32[]{:S(2)}) async-start(f16[8,384,128]{2,1,0:T(8,128)(2,1)} %convert_element_type.19), calls=%async_computation.3 | async-start | bytes 1572864 | tf_op jit(solution)/shard_map/all_to_all | solution.py:210
  86.3 4.1 %collective-permute-start.16 = (bf16[16,64,128]{2,1,0:T(8,128)(2,1)S(1)}, bf16[16,64,128]{2,1,0:T(8,128)(2,1)S(1)}, u32[]{:S(2)}, u32[]{:S(2)}) collective-permute-start(bf16[16,64,128]{2,1,0:T(8,128)(2,1)S(1)} %all-to-all-done.1.mine), channel_id=1, source_target_pairs={{0,8},{8,0},{1,9},{9,1},{2,10},{10,2},{3,11},{11,3},{4,12},{12,4},... | collective-permute-start | bytes 786440 | tf_op jit(solution)/shard_map/ppermute | solution.py:240
  92.0 2.6 %all-to-all-done.3 = f16[8,384,128]{2,1,0:T(8,128)(2,1)S(1)} async-done(((f16[8,384,128]{2,1,0:T(8,128)(2,1)}), f16[8,384,128]{2,1,0:T(8,128)(2,1)S(1)}, u32[]{:S(2)}, u32[]{:S(2)}) %all-to-all-start.3) | async-done | bytes 786464 | tf_op jit(solution)/shard_map/all_to_all | solution.py:210
  97.0 4.2 %all-to-all-start.4 = ((f16[8,8,2,8,256]{4,3,2,1,0:T(8,128)(2,1)}), f16[8,8,2,8,256]{4,3,2,1,0:T(8,128)(2,1)S(1)}, u32[]{:S(2)}, u32[]{:S(2)}) async-start(f16[8,8,2,8,256]{4,3,2,1,0:T(8,128)(2,1)} %convert_element_type.22), calls=%async_computation.4 | async-start | bytes 1048576 | tf_op jit(solution)/shard_map/all_to_all | solution.py:210
  101.2 4.7 %collective-permute-start.17 = (f32[4,4,4,8,128]{4,3,2,1,0:T(8,128)S(1)}, f32[4,4,4,8,128]{4,3,2,1,0:T(8,128)S(1)}, u32[]{:S(2)}, u32[]{:S(2)}) collective-permute-start(f32[4,4,4,8,128]{4,3,2,1,0:T(8,128)S(1)} %get-tuple-element.59), channel_id=1, source_target_pairs={{0,8},{8,0},{1,9},{9,1},{2,10},{10,2},{3,11},{11,3},{4,12},{12,4},... | collective-permute-start | bytes 786440 | tf_op jit(solution)/shard_map/ppermute | solution.py:242
  108.8 16.5 %all_to_all.30 = f32[16,2,8,128]{3,2,1,0:T(8,128)S(1)} all-to-all(f32[16,2,8,128]{3,2,1,0:T(8,128)S(1)} %copy.10), channel_id=1, replica_groups=mesh['x'=4,'zh'=4,'core'=2,'zl'=2,'y'=4] {'x','zh'}, dimensions={0} | all-to-all | bytes 262144 | tf_op jit(solution)/shard_map/all_to_all | solution.py:213
  125.3 4.0 %collective-permute-start.18 = (f32[8,128]{1,0:T(8,128)S(1)}, f32[8,128]{1,0:T(8,128)S(1)}, u32[]{:S(2)}, u32[]{:S(2)}) collective-permute-start(f32[8,128]{1,0:T(8,128)S(1)} %slice_bitcast_fusion), channel_id=1, source_target_pairs={{0,8},{8,0},{1,9},{9,1},{2,10},{10,2},{3,11},{11,3},{4,12},{12,4},... | collective-permute-start | bytes 12296 | tf_op jit(solution)/shard_map/ppermute | solution.py:249
  (74 shorter events, 21.1 us)
Async XLA Ops:
  0.6 28.2 %collective-permute-start.5 = (bf16[512,2048]{1,0:T(8,128)(2,1)}, bf16[512,2048]{1,0:T(8,128)(2,1)S(1)}, u32[]{:S(2)}, u32[]{:S(2)}) collective-permute-start(bf16[512,2048]{1,0:T(8,128)(2,1)} %refs_6_.1), channel_id=1, source_target_pairs={{0,8},{8,0},{1,9},{9,1},{2,10},{10,2},{3,11},{11,3},{4,12},{12,4},... | collective-permute-start | bytes 6291464 | tf_op jit(solution)/shard_map/ppermute | solution.py:215
  7.7 9.3 %collective-permute-start.2 = (bf16[64,2048]{1,0:T(8,128)(2,1)}, bf16[64,2048]{1,0:T(8,128)(2,1)S(1)}, u32[]{:S(2)}, u32[]{:S(2)}) collective-permute-start(bf16[64,2048]{1,0:T(8,128)(2,1)} %get-tuple-element.41.refs_0_.source), channel_id=1, source_target_pairs={{0,64},{64,128},{128,192},{192,0},{1,65},{65,129},{129,193},{193,1... | collective-permute-start | bytes 786440 | tf_op jit(solution)/shard_map/ppermute | solution.py:207
  7.7 9.3 %collective-permute-start.3 = (bf16[64,2048]{1,0:T(8,128)(2,1)}, bf16[64,2048]{1,0:T(8,128)(2,1)S(1)}, u32[]{:S(2)}, u32[]{:S(2)}) collective-permute-start(bf16[64,2048]{1,0:T(8,128)(2,1)} %get-tuple-element.41.refs_0_.source), channel_id=1, source_target_pairs={{0,192},{64,0},{128,64},{192,128},{1,193},{65,1},{129,65},{193,129... | collective-permute-start | bytes 786440 | tf_op jit(solution)/shard_map/ppermute | solution.py:207
  10.4 12.2 %collective-permute-start = (bf16[64,2048]{1,0:T(8,128)(2,1)}, bf16[64,2048]{1,0:T(8,128)(2,1)S(1)}, u32[]{:S(2)}, u32[]{:S(2)}) collective-permute-start(bf16[64,2048]{1,0:T(8,128)(2,1)} %get-tuple-element.41.refs_0_.source), channel_id=1, source_target_pairs={{0,16},{16,32},{32,48},{48,0},{1,17},{17,33},{33,49},{49,1},{2,18}... | collective-permute-start | bytes 786440 | tf_op jit(solution)/shard_map/ppermute | solution.py:218
  11.7 16.4 %collective-permute-start.1 = (bf16[64,2048]{1,0:T(8,128)(2,1)}, bf16[64,2048]{1,0:T(8,128)(2,1)S(1)}, u32[]{:S(2)}, u32[]{:S(2)}) collective-permute-start(bf16[64,2048]{1,0:T(8,128)(2,1)} %get-tuple-element.41.refs_0_.source), channel_id=1, source_target_pairs={{0,48},{16,0},{32,16},{48,32},{1,49},{17,1},{33,17},{49,33},{2,50}... | collective-permute-start | bytes 786440 | tf_op jit(solution)/shard_map/ppermute | solution.py:218
  17.8 10.3 %collective-permute-start.4 = (bf16[64,2048]{1,0:T(8,128)(2,1)S(1)}, bf16[64,2048]{1,0:T(8,128)(2,1)S(1)}, u32[]{:S(2)}, u32[]{:S(2)}) collective-permute-start(bf16[64,2048]{1,0:T(8,128)(2,1)S(1)} %collective-permute-done.2.refs_1_), channel_id=1, source_target_pairs={{0,64},{64,128},{128,192},{192,0},{1,65},{65,129},{129,193},{193,1... | collective-permute-start | bytes 786440 | tf_op jit(solution)/shard_map/ppermute | solution.py:220
  17.8 18.8 %all-to-all-start = ((bf16[8,2,64,128]{3,2,1,0:T(8,128)(2,1)}), bf16[8,2,64,128]{3,2,1,0:T(8,128)(2,1)}, u32[]{:S(2)}, u32[]{:S(2)}) async-start(bf16[8,2,64,128]{3,2,1,0:T(8,128)(2,1)} %get-tuple-element.48), calls=%async_computation | async-start | bytes 524288 | tf_op jit(solution)/shard_map/all_to_all | solution.py:210
  28.8 15.2 %collective-permute-start.6 = (bf16[64,2048]{1,0:T(8,128)(2,1)S(1)}, bf16[64,2048]{1,0:T(8,128)(2,1)S(1)}, u32[]{:S(2)}, u32[]{:S(2)}) collective-permute-start(bf16[64,2048]{1,0:T(8,128)(2,1)S(1)} %collective-permute-done.refs_4_), channel_id=1, source_target_pairs={{0,16},{16,32},{32,48},{48,0},{1,17},{17,33},{33,49},{49,1},{2,18}... | collective-permute-start | bytes 786440 | tf_op jit(solution)/shard_map/ppermute | solution.py:224
  31.9 12.2 %collective-permute-start.7 = (bf16[64,2048]{1,0:T(8,128)(2,1)S(1)}, bf16[64,2048]{1,0:T(8,128)(2,1)}, u32[]{:S(2)}, u32[]{:S(2)}) collective-permute-start(bf16[64,2048]{1,0:T(8,128)(2,1)S(1)} %collective-permute-done.refs_4_), channel_id=1, source_target_pairs={{0,64},{64,128},{128,192},{192,0},{1,65},{65,129},{129,193},{193,1... | collective-permute-start | bytes 786440 | tf_op jit(solution)/shard_map/ppermute | solution.py:207
  31.9 12.2 %collective-permute-start.8 = (bf16[64,2048]{1,0:T(8,128)(2,1)S(1)}, bf16[64,2048]{1,0:T(8,128)(2,1)S(1)}, u32[]{:S(2)}, u32[]{:S(2)}) collective-permute-start(bf16[64,2048]{1,0:T(8,128)(2,1)S(1)} %collective-permute-done.refs_4_), channel_id=1, source_target_pairs={{0,192},{64,0},{128,64},{192,128},{1,193},{65,1},{129,65},{193,129... | collective-permute-start | bytes 786440 | tf_op jit(solution)/shard_map/ppermute | solution.py:207
  34.6 9.5 %collective-permute-start.10 = (bf16[64,2048]{1,0:T(8,128)(2,1)S(1)}, bf16[64,2048]{1,0:T(8,128)(2,1)}, u32[]{:S(2)}, u32[]{:S(2)}) collective-permute-start(bf16[64,2048]{1,0:T(8,128)(2,1)S(1)} %collective-permute-done.1.refs_7_), channel_id=1, source_target_pairs={{0,192},{64,0},{128,64},{192,128},{1,193},{65,1},{129,65},{193,129... | collective-permute-start | bytes 786440 | tf_op jit(solution)/shard_map/ppermute | solution.py:207
  34.6 10.4 %collective-permute-start.9 = (bf16[64,2048]{1,0:T(8,128)(2,1)S(1)}, bf16[64,2048]{1,0:T(8,128)(2,1)}, u32[]{:S(2)}, u32[]{:S(2)}) collective-permute-start(bf16[64,2048]{1,0:T(8,128)(2,1)S(1)} %collective-permute-done.1.refs_7_), channel_id=1, source_target_pairs={{0,64},{64,128},{128,192},{192,0},{1,65},{65,129},{129,193},{193,1... | collective-permute-start | bytes 786440 | tf_op jit(solution)/shard_map/ppermute | solution.py:207
  36.7 24.8 %all-to-all-start.1 = ((bf16[16,64,128]{2,1,0:T(8,128)(2,1)}), bf16[16,64,128]{2,1,0:T(8,128)(2,1)S(1)}, u32[]{:S(2)}, u32[]{:S(2)}) async-start(bf16[16,64,128]{2,1,0:T(8,128)(2,1)} %shard_map.62), calls=%async_computation.1 | async-start | bytes 524288 | tf_op jit(solution)/shard_map/all_to_all | solution.py:213
  45.0 16.4 %collective-permute-start.11 = (bf16[64,2048]{1,0:T(8,128)(2,1)}, bf16[64,2048]{1,0:T(8,128)(2,1)S(1)}, u32[]{:S(2)}, u32[]{:S(2)}) collective-permute-start(bf16[64,2048]{1,0:T(8,128)(2,1)} %collective-permute-done.7.refs_5_), channel_id=1, source_target_pairs={{0,64},{64,128},{128,192},{192,0},{1,65},{65,129},{129,193},{193,1... | collective-permute-start | bytes 786440 | tf_op jit(solution)/shard_map/ppermute | solution.py:229
  45.0 16.4 %collective-permute-start.12 = (bf16[64,2048]{1,0:T(8,128)(2,1)}, bf16[64,2048]{1,0:T(8,128)(2,1)S(1)}, u32[]{:S(2)}, u32[]{:S(2)}) collective-permute-start(bf16[64,2048]{1,0:T(8,128)(2,1)} %collective-permute-done.10.refs_9_), channel_id=1, source_target_pairs={{0,192},{64,0},{128,64},{192,128},{1,193},{65,1},{129,65},{193,129... | collective-permute-start | bytes 786440 | tf_op jit(solution)/shard_map/ppermute | solution.py:229
  48.4 13.0 %collective-permute-start.13 = (bf16[64,2048]{1,0:T(8,128)(2,1)S(1)}, bf16[64,2048]{1,0:T(8,128)(2,1)S(1)}, u32[]{:S(2)}, u32[]{:S(2)}) collective-permute-start(bf16[64,2048]{1,0:T(8,128)(2,1)S(1)} %collective-permute-done.6.refs_2_), channel_id=1, source_target_pairs={{0,64},{64,128},{128,192},{192,0},{1,65},{65,129},{129,193},{193,1... | collective-permute-start | bytes 786440 | tf_op jit(solution)/shard_map/ppermute | solution.py:207
  48.4 13.0 %collective-permute-start.14 = (bf16[64,2048]{1,0:T(8,128)(2,1)S(1)}, bf16[64,2048]{1,0:T(8,128)(2,1)}, u32[]{:S(2)}, u32[]{:S(2)}) collective-permute-start(bf16[64,2048]{1,0:T(8,128)(2,1)S(1)} %collective-permute-done.6.refs_2_), channel_id=1, source_target_pairs={{0,192},{64,0},{128,64},{192,128},{1,193},{65,1},{129,65},{193,129... | collective-permute-start | bytes 786440 | tf_op jit(solution)/shard_map/ppermute | solution.py:207
  61.5 17.8 %all-to-all-start.2 = ((f16[8,640,128]{2,1,0:T(8,128)(2,1)}), f16[8,640,128]{2,1,0:T(8,128)(2,1)}, u32[]{:S(2)}, u32[]{:S(2)}) async-start(f16[8,640,128]{2,1,0:T(8,128)(2,1)} %convert_element_type.18), calls=%async_computation.2 | async-start | bytes 2621440 | tf_op jit(solution)/shard_map/all_to_all | solution.py:210
  65.9 6.5 %collective-permute-start.15 = (bf16[64,2048]{1,0:T(8,128)(2,1)S(1)}, bf16[64,2048]{1,0:T(8,128)(2,1)S(1)}, u32[]{:S(2)}, u32[]{:S(2)}) collective-permute-start(bf16[64,2048]{1,0:T(8,128)(2,1)S(1)} %collective-permute-done.13.refs_3_), channel_id=1, source_target_pairs={{0,64},{64,128},{128,192},{192,0},{1,65},{65,129},{129,193},{193,1... | collective-permute-start | bytes 786440 | tf_op jit(solution)/shard_map/ppermute | solution.py:235
  79.2 15.4 %all-to-all-start.3 = ((f16[8,384,128]{2,1,0:T(8,128)(2,1)}), f16[8,384,128]{2,1,0:T(8,128)(2,1)S(1)}, u32[]{:S(2)}, u32[]{:S(2)}) async-start(f16[8,384,128]{2,1,0:T(8,128)(2,1)} %convert_element_type.19), calls=%async_computation.3 | async-start | bytes 1572864 | tf_op jit(solution)/shard_map/all_to_all | solution.py:210
  86.3 8.5 %collective-permute-start.16 = (bf16[16,64,128]{2,1,0:T(8,128)(2,1)S(1)}, bf16[16,64,128]{2,1,0:T(8,128)(2,1)S(1)}, u32[]{:S(2)}, u32[]{:S(2)}) collective-permute-start(bf16[16,64,128]{2,1,0:T(8,128)(2,1)S(1)} %all-to-all-done.1.mine), channel_id=1, source_target_pairs={{0,8},{8,0},{1,9},{9,1},{2,10},{10,2},{3,11},{11,3},{4,12},{12,4},... | collective-permute-start | bytes 786440 | tf_op jit(solution)/shard_map/ppermute | solution.py:240
  97.0 11.6 %all-to-all-start.4 = ((f16[8,8,2,8,256]{4,3,2,1,0:T(8,128)(2,1)}), f16[8,8,2,8,256]{4,3,2,1,0:T(8,128)(2,1)S(1)}, u32[]{:S(2)}, u32[]{:S(2)}) async-start(f16[8,8,2,8,256]{4,3,2,1,0:T(8,128)(2,1)} %convert_element_type.22), calls=%async_computation.4 | async-start | bytes 1048576 | tf_op jit(solution)/shard_map/all_to_all | solution.py:210
  101.2 5.8 %collective-permute-start.17 = (f32[4,4,4,8,128]{4,3,2,1,0:T(8,128)S(1)}, f32[4,4,4,8,128]{4,3,2,1,0:T(8,128)S(1)}, u32[]{:S(2)}, u32[]{:S(2)}) collective-permute-start(f32[4,4,4,8,128]{4,3,2,1,0:T(8,128)S(1)} %get-tuple-element.59), channel_id=1, source_target_pairs={{0,8},{8,0},{1,9},{9,1},{2,10},{10,2},{3,11},{11,3},{4,12},{12,4},... | collective-permute-start | bytes 786440 | tf_op jit(solution)/shard_map/ppermute | solution.py:242
  125.3 4.8 %collective-permute-start.18 = (f32[8,128]{1,0:T(8,128)S(1)}, f32[8,128]{1,0:T(8,128)S(1)}, u32[]{:S(2)}, u32[]{:S(2)}) collective-permute-start(f32[8,128]{1,0:T(8,128)S(1)} %slice_bitcast_fusion), channel_id=1, source_target_pairs={{0,8},{8,0},{1,9},{9,1},{2,10},{10,2},{3,11},{11,3},{4,12},{12,4},... | collective-permute-start | bytes 12296 | tf_op jit(solution)/shard_map/ppermute | solution.py:249
  (11 other events, 99.8 us)

commit v6 on v5

--- a/solution.py
+++ b/solution.py
@@ -16,43 +16,47 @@
 SMEM = pl.BlockSpec(memory_space=pltpu.SMEM)
 
 
-def mask_kernel(ids, mask, panel, own, pieces):
-    ic, col, t = ids[2], ids[3], pl.program_id(0)
+def mask_kernel(mask, panel, own):
+    col = lax.axis_index("zl") * 4 + lax.axis_index("y")
     upper = lax.broadcasted_iota(jnp.int32, (16, 256), 0) < 8
-    low = lax.broadcasted_iota(jnp.int32, (16, 128), 1) < 64
-    blocks = []
-    for i in range(8):
-        lanes = slice(256 * i, 256 * i + 256)
-        here = jnp.where(upper, mask[2 * t, col * 8 + i], mask[2 * t + 1, col * 8 + i]).astype(jnp.float32)
-        blocks.append(panel[:, lanes].astype(jnp.float32) * here)
-        own[:, lanes] = blocks[-1].astype(own.dtype)
+    for t in range(4):
+        rows = slice(16 * t, 16 * t + 16)
+        for i in range(8):
+            lanes = slice(256 * i, 256 * i + 256)
+            here = jnp.where(upper, mask[2 * t, col * 8 + i], mask[2 * t + 1, col * 8 + i]).astype(jnp.float32)
+            own[rows, lanes] = (panel[rows, lanes].astype(jnp.float32) * here).astype(own.dtype)
+
+
+def mask_call(mask, panel):
+    return pl.pallas_call(
+        mask_kernel,
+        out_shape=jax.ShapeDtypeStruct((64, 2048), jnp.bfloat16),
+        in_specs=[SMEM, VMEM],
+        out_specs=VMEM,
+        cost_estimate=pl.CostEstimate(flops=1, bytes_accessed=2**19, transcendentals=0),
+    )(mask, panel)
+
+
+def pieces_kernel(ids, own, pieces):
+    ic = ids[2]
+    low = lax.broadcasted_iota(jnp.int32, (64, 128), 1) < 64
     for b in range(2):
-        for h in range(2):
-            even, odd = blocks[4 * b + h], blocks[4 * b + 2 + h]
-            first, second = jnp.where(ic == 0, even, odd), jnp.where(ic == 0, odd, even)
-            for u in range(2):
-                p, q = first[:, 128 * u:128 * u + 128], second[:, 128 * u:128 * u + 128]
-                j = 4 * h + 2 * u
-                pieces[j, b] = jnp.where(low, p, pltpu.roll(q, 64, 1)).astype(pieces.dtype)
-                pieces[j + 1, b] = jnp.where(low, pltpu.roll(p, 64, 1), q).astype(pieces.dtype)
-
-
-def mask_call(ids, mask, panel):
-    return pl.pallas_call(
-        mask_kernel,
-        grid=(4,),
-        out_shape=(
-            jax.ShapeDtypeStruct((64, 2048), jnp.bfloat16),
-            jax.ShapeDtypeStruct((8, 2, 64, 128), jnp.bfloat16),
-        ),
-        in_specs=[SMEM, SMEM, pl.BlockSpec((16, 2048), lambda t: (t, 0))],
-        out_specs=(
-            pl.BlockSpec((16, 2048), lambda t: (t, 0)),
-            pl.BlockSpec((8, 2, 16, 128), lambda t: (0, 0, t, 0)),
-        ),
-        compiler_params=pltpu.CompilerParams(vmem_limit_bytes=60 * 2**20),
-        cost_estimate=pl.CostEstimate(flops=1, bytes_accessed=2**20, transcendentals=0),
-    )(ids, mask, panel)
+        for u in range(4):
+            lanes = [slice(1024 * b + 512 * c + 128 * u, 1024 * b + 512 * c + 128 * u + 128) for c in range(2)]
+            even, odd = own[:, lanes[0]].astype(jnp.float32), own[:, lanes[1]].astype(jnp.float32)
+            p, q = jnp.where(ic == 0, even, odd), jnp.where(ic == 0, odd, even)
+            pieces[2 * u, b] = jnp.where(low, p, pltpu.roll(q, 64, 1)).astype(pieces.dtype)
+            pieces[2 * u + 1, b] = jnp.where(low, pltpu.roll(p, 64, 1), q).astype(pieces.dtype)
+
+
+def pieces_call(ids, own):
+    return pl.pallas_call(
+        pieces_kernel,
+        out_shape=jax.ShapeDtypeStruct((8, 2, 64, 128), jnp.bfloat16),
+        in_specs=[SMEM, VMEM],
+        out_specs=VMEM,
+        cost_estimate=pl.CostEstimate(flops=1, bytes_accessed=2**19, transcendentals=0),
+    )(ids, own)
 
 
 def product_kernel(ids, *refs):
@@ -213,7 +217,8 @@
         return lax.all_to_all(value, ("x", "zh"), 0, 0, tiled=True)
 
     other_root = lax.ppermute(inverse_root, "core", swap)
-    own, pieces = mask_call(ids, block_mask, jnp.transpose(panel, (1, 2, 0)).reshape(64, 2048))
+    own = mask_call(block_mask, jnp.transpose(panel, (1, 2, 0)).reshape(64, 2048))
+    pieces = pieces_call(ids, own)
 
     z1, z3 = (lax.ppermute(own, "zh", turn(4, s)) for s in (1, 3))
     near0, pieces = pin((around(own), pieces))

time: 132 us -> 131 us (level)
  waiting for transfers between devices: 24.3 us -> 22.2 us
    ppermute x4, waiting for transfers between devices: 3.66 us -> 0.44 us  [around(): lax.ppermute(slab, 'x', turn(4, -1))]
    ppermute x1, waiting for transfers between devices: 0.01 us -> 2.38 us  [shards(): z2 = lax.ppermute(z1, 'zh', turn(4, 1))]
    ppermute x4, waiting for transfers between devices: 3.35 us -> 1.09 us  [around(): lax.ppermute(slab, 'x', turn(4, 1))]
    unnamed x22 -> x20, local copies, waits for them, and re-layouts: 3.1 us -> 2.31 us
    pallas_call x1 -> x2, Pallas kernels: 3.2 us -> 3.58 us  [the longest x1 1.84 us: pieces_call(): pl.pallas_call(pieces_kernel, out_shape=jax.ShapeDtypeStruct((8, 2, 64, 1...]
  transfers between devices with their start and end apart: 24 -> 24, of which waited for: 10 -> 10; matrix products, arithmetic and copies ran while one was open for 5% -> 5% of each run, Pallas kernels for 12% -> 13%
where the time goes in v6:
time: 131 us; the launch traced here: 130 us
  starting transfers between devices  60.5 us (46%)
  waiting for transfers between devices  22.2 us (17%)
  Pallas kernels  17.8 us (14%)
  blocking collectives  17.5 us (13%)
  other arithmetic  8.04 us (6%)
  local copies, waits for them, and re-layouts  2.95 us (2%)
    all_to_all x4, starting transfers between devices, to_columns(): return lax.all_to_all(value, ('zl', 'y'), 0, 0, tiled=True)  19.9 us
    all_to_all x1, blocking collectives, to_rows(): return lax.all_to_all(value, ('x', 'zh'), 0, 0, tiled=True)  17.5 us
    pallas_call x2, Pallas kernels, product_call(): pl.pallas_call(product_kernel, grid=(4,), out_shape=jax.ShapeDtypeStruct(...  10.8 us
    ppermute x4, starting transfers between devices, around(): lax.ppermute(slab, 'x', turn(4, -1))  8.08 us
    ppermute x2, waiting for transfers between devices, shards(): z1, z3 = (lax.ppermute(own, 'zh', turn(4, s)) for s in (1, 3))  6.74 us
    ppermute x1, waiting for transfers between devices, shards(): far2 = lax.ppermute(near2[0], 'x', turn(4, 1))  6.42 us
    ppermute x1, starting transfers between devices, shards(): got = lax.ppermute(give, 'core', swap)  5.3 us
    ppermute x1, starting transfers between devices, shards(): other = lax.ppermute(mine, 'core', swap)  4.47 us
  transfers between devices with their start and end apart: 24, of which 10 were waited for; matrix products, arithmetic and copies ran while one was open for 5% of the time, Pallas kernels for 13%

profile of v6, /device:TPU:1, one launch (start us, length us, event | category | flops | bytes accessed | tf_op | source)
XLA Modules:
  0.0 129.9 jit_solution(18163026021080533518)
XLA Ops:
  0.6 3.3 %collective-permute-start.5 = (bf16[512,2048]{1,0:T(8,128)(2,1)}, bf16[512,2048]{1,0:T(8,128)(2,1)S(1)}, u32[]{:S(2)}, u32[]{:S(2)}) collective-permute-start(bf16[512,2048]{1,0:T(8,128)(2,1)} %refs_6_.1), channel_id=1, source_target_pairs={{0,8},{8,0},{1,9},{9,1},{2,10},{10,2},{3,11},{11,3},{4,12},{12,4},... | collective-permute-start | bytes 6291464 | tf_op jit(solution)/shard_map/ppermute | solution.py:219
  5.7 2.7 %collective-permute-start.3 = (bf16[64,2048]{1,0:T(8,128)(2,1)}, bf16[64,2048]{1,0:T(8,128)(2,1)S(1)}, u32[]{:S(2)}, u32[]{:S(2)}) collective-permute-start(bf16[64,2048]{1,0:T(8,128)(2,1)} %shard_map.59.own.refs_0_.source), channel_id=1, source_target_pairs={{0,192},{64,0},{128,64},{192,128},{1,193},{65,1},{129,65},{193,129... | collective-permute-start | bytes 786440 | tf_op jit(solution)/shard_map/ppermute | solution.py:211
  10.2 3.0 %collective-permute-start.1 = (bf16[64,2048]{1,0:T(8,128)(2,1)}, bf16[64,2048]{1,0:T(8,128)(2,1)S(1)}, u32[]{:S(2)}, u32[]{:S(2)}) collective-permute-start(bf16[64,2048]{1,0:T(8,128)(2,1)} %shard_map.59.own.refs_0_.source), channel_id=1, source_target_pairs={{0,48},{16,0},{32,16},{48,32},{1,49},{17,1},{33,17},{49,33},{2,50}... | collective-permute-start | bytes 786440 | tf_op jit(solution)/shard_map/ppermute | solution.py:223
  13.3 1.8 %shard_map.60 = bf16[8,2,64,128]{3,2,1,0:T(8,128)(2,1)} custom-call(s32[4]{0:T(128)} %pad_add_fusion.ids, bf16[64,2048]{1,0:T(8,128)(2,1)} %shard_map.59.own.refs_0_.source), custom_call_target="tpu_custom_call" | custom-call | flops 1 | bytes 524288 | tf_op jit(solution)/shard_map/pallas_call | solution.py:53
  15.2 4.7 %all-to-all-start = ((bf16[8,2,64,128]{3,2,1,0:T(8,128)(2,1)}), bf16[8,2,64,128]{3,2,1,0:T(8,128)(2,1)S(1)}, u32[]{:S(2)}, u32[]{:S(2)}) async-start(bf16[8,2,64,128]{3,2,1,0:T(8,128)(2,1)} %shard_map.60), calls=%async_computation | async-start | bytes 524288 | tf_op jit(solution)/shard_map/all_to_all | solution.py:214
  20.6 6.0 %collective-permute-done.1.refs_7_ = bf16[64,2048]{1,0:T(8,128)(2,1)S(1)} collective-permute-done((bf16[64,2048]{1,0:T(8,128)(2,1)}, bf16[64,2048]{1,0:T(8,128)(2,1)S(1)}, u32[]{:S(2)}, u32[]{:S(2)}) %collective-permute-start.1) | collective-permute-done | bytes 262176 | tf_op jit(solution)/shard_map/ppermute | solution.py:223
  26.7 3.2 %collective-permute-start.6 = (bf16[64,2048]{1,0:T(8,128)(2,1)S(1)}, bf16[64,2048]{1,0:T(8,128)(2,1)S(1)}, u32[]{:S(2)}, u32[]{:S(2)}) collective-permute-start(bf16[64,2048]{1,0:T(8,128)(2,1)S(1)} %collective-permute-done.refs_4_), channel_id=1, source_target_pairs={{0,16},{16,32},{32,48},{48,0},{1,17},{17,33},{33,49},{49,1},{2,18}... | collective-permute-start | bytes 786440 | tf_op jit(solution)/shard_map/ppermute | solution.py:229
  29.8 2.7 %collective-permute-start.8 = (bf16[64,2048]{1,0:T(8,128)(2,1)S(1)}, bf16[64,2048]{1,0:T(8,128)(2,1)}, u32[]{:S(2)}, u32[]{:S(2)}) collective-permute-start(bf16[64,2048]{1,0:T(8,128)(2,1)S(1)} %collective-permute-done.refs_4_), channel_id=1, source_target_pairs={{0,192},{64,0},{128,64},{192,128},{1,193},{65,1},{129,65},{193,129... | collective-permute-start | bytes 786440 | tf_op jit(solution)/shard_map/ppermute | solution.py:211
  35.3 3.7 %all-to-all-start.1 = ((bf16[16,64,128]{2,1,0:T(8,128)(2,1)}), bf16[16,64,128]{2,1,0:T(8,128)(2,1)S(1)}, u32[]{:S(2)}, u32[]{:S(2)}) async-start(bf16[16,64,128]{2,1,0:T(8,128)(2,1)} %shard_map.63), calls=%async_computation.1 | async-start | bytes 524288 | tf_op jit(solution)/shard_map/all_to_all | solution.py:217
  39.0 2.4 %collective-permute-done.6.refs_2_ = bf16[64,2048]{1,0:T(8,128)(2,1)S(1)} collective-permute-done((bf16[64,2048]{1,0:T(8,128)(2,1)S(1)}, bf16[64,2048]{1,0:T(8,128)(2,1)S(1)}, u32[]{:S(2)}, u32[]{:S(2)}) %collective-permute-start.6) | collective-permute-done | bytes 262176 | tf_op jit(solution)/shard_map/ppermute | solution.py:229
  42.9 2.7 %collective-permute-start.12 = (bf16[64,2048]{1,0:T(8,128)(2,1)}, bf16[64,2048]{1,0:T(8,128)(2,1)S(1)}, u32[]{:S(2)}, u32[]{:S(2)}) collective-permute-start(bf16[64,2048]{1,0:T(8,128)(2,1)} %collective-permute-done.10.refs_9_), channel_id=1, source_target_pairs={{0,192},{64,0},{128,64},{192,128},{1,193},{65,1},{129,65},{193,129... | collective-permute-start | bytes 786440 | tf_op jit(solution)/shard_map/ppermute | solution.py:234
  45.6 2.7 %collective-permute-start.14 = (bf16[64,2048]{1,0:T(8,128)(2,1)S(1)}, bf16[64,2048]{1,0:T(8,128)(2,1)}, u32[]{:S(2)}, u32[]{:S(2)}) collective-permute-start(bf16[64,2048]{1,0:T(8,128)(2,1)S(1)} %collective-permute-done.6.refs_2_), channel_id=1, source_target_pairs={{0,192},{64,0},{128,64},{192,128},{1,193},{65,1},{129,65},{193,129... | collective-permute-start | bytes 786440 | tf_op jit(solution)/shard_map/ppermute | solution.py:211
  48.3 7.3 %shard_map.61 = f32[8,640,128]{2,1,0:T(8,128)} custom-call(s32[4]{0:T(128)} %pad_add_fusion.ids, bf16[64,2048]{1,0:T(8,128)(2,1)} %shard_map.59.own.refs_0_.source, bf16[64,2048]{1,0:T(8,128)(2,1)} %copy-done.6, bf16[64,2048]{1,0:T(8,128)(2,1)} %copy-done.7, bf16[64,2048]{1,0:T(8,128)(2,1)} %collective-permute-done.4.refs_3_, bf16[64,2048]{1,0:T(8,128)(2,1)} %copy-done.8, ...), custom_call_target="tpu_custom_call" | custom-call | flops 2684354560 | bytes 8912896 | tf_op jit(solution)/shard_map/pallas_call | solution.py:82
  55.5 3.0 %convert_element_type.18 = f16[8,640,128]{2,1,0:T(8,128)(2,1)} convert(f32[8,640,128]{2,1,0:T(8,128)} %shard_map.61) | non-fusion elementwise | flops 655360 | bytes 3932160 | tf_op jit(solution)/shard_map/convert_element_type | solution.py:208
  58.6 4.4 %all-to-all-start.2 = ((f16[8,640,128]{2,1,0:T(8,128)(2,1)}), f16[8,640,128]{2,1,0:T(8,128)(2,1)}, u32[]{:S(2)}, u32[]{:S(2)}) async-start(f16[8,640,128]{2,1,0:T(8,128)(2,1)} %convert_element_type.18), calls=%async_computation.2 | async-start | bytes 2621440 | tf_op jit(solution)/shard_map/all_to_all | solution.py:214
  63.1 6.4 %collective-permute-done.15.refs_5_ = bf16[64,2048]{1,0:T(8,128)(2,1)S(1)} collective-permute-done((bf16[64,2048]{1,0:T(8,128)(2,1)S(1)}, bf16[64,2048]{1,0:T(8,128)(2,1)S(1)}, u32[]{:S(2)}, u32[]{:S(2)}) %collective-permute-start.15) | collective-permute-done | bytes 262176 | tf_op jit(solution)/shard_map/ppermute | solution.py:240
  71.1 3.6 %shard_map.64 = f32[8,384,128]{2,1,0:T(8,128)S(1)} custom-call(s32[4]{0:T(128)S(1)} %copy-done.3, bf16[64,2048]{1,0:T(8,128)(2,1)S(1)} %collective-permute-done.11.refs_0_, bf16[64,2048]{1,0:T(8,128)(2,1)S(1)} %collective-permute-done.12.refs_1_, bf16[64,2048]{1,0:T(8,128)(2,1)S(1)} %collective-permute-done.6.refs_2_, ...), custom_call_target="tpu_custom_call" | custom-call | flops 1610612736 | bytes 7864320 | tf_op jit(solution)/shard_map/pallas_call | solution.py:82
  76.5 6.9 %all-to-all-start.3 = ((f16[8,384,128]{2,1,0:T(8,128)(2,1)}), f16[8,384,128]{2,1,0:T(8,128)(2,1)S(1)}, u32[]{:S(2)}, u32[]{:S(2)}) async-start(f16[8,384,128]{2,1,0:T(8,128)(2,1)} %convert_element_type.19), calls=%async_computation.3 | async-start | bytes 1572864 | tf_op jit(solution)/shard_map/all_to_all | solution.py:214
  83.4 4.5 %collective-permute-start.16 = (bf16[16,64,128]{2,1,0:T(8,128)(2,1)S(1)}, bf16[16,64,128]{2,1,0:T(8,128)(2,1)S(1)}, u32[]{:S(2)}, u32[]{:S(2)}) collective-permute-start(bf16[16,64,128]{2,1,0:T(8,128)(2,1)S(1)} %all-to-all-done.1.mine), channel_id=1, source_target_pairs={{0,8},{8,0},{1,9},{9,1},{2,10},{10,2},{3,11},{11,3},{4,12},{12,4},... | collective-permute-start | bytes 786440 | tf_op jit(solution)/shard_map/ppermute | solution.py:245
  89.4 2.3 %all-to-all-done.3 = f16[8,384,128]{2,1,0:T(8,128)(2,1)S(1)} async-done(((f16[8,384,128]{2,1,0:T(8,128)(2,1)}), f16[8,384,128]{2,1,0:T(8,128)(2,1)S(1)}, u32[]{:S(2)}, u32[]{:S(2)}) %all-to-all-start.3) | async-done | bytes 786464 | tf_op jit(solution)/shard_map/all_to_all | solution.py:214
  94.0 3.9 %all-to-all-start.4 = ((f16[8,8,2,8,256]{4,3,2,1,0:T(8,128)(2,1)}), f16[8,8,2,8,256]{4,3,2,1,0:T(8,128)(2,1)S(1)}, u32[]{:S(2)}, u32[]{:S(2)}) async-start(f16[8,8,2,8,256]{4,3,2,1,0:T(8,128)(2,1)} %convert_element_type.22), calls=%async_computation.4 | async-start | bytes 1048576 | tf_op jit(solution)/shard_map/all_to_all | solution.py:214
  97.9 5.3 %collective-permute-start.17 = (f32[4,4,4,8,128]{4,3,2,1,0:T(8,128)S(1)}, f32[4,4,4,8,128]{4,3,2,1,0:T(8,128)S(1)}, u32[]{:S(2)}, u32[]{:S(2)}) collective-permute-start(f32[4,4,4,8,128]{4,3,2,1,0:T(8,128)S(1)} %get-tuple-element.55), channel_id=1, source_target_pairs={{0,8},{8,0},{1,9},{9,1},{2,10},{10,2},{3,11},{11,3},{4,12},{12,4},... | collective-permute-start | bytes 786440 | tf_op jit(solution)/shard_map/ppermute | solution.py:247
  106.2 17.5 %all_to_all.30 = f32[16,2,8,128]{3,2,1,0:T(8,128)S(1)} all-to-all(f32[16,2,8,128]{3,2,1,0:T(8,128)S(1)} %copy.10), channel_id=1, replica_groups=mesh['x'=4,'zh'=4,'core'=2,'zl'=2,'y'=4] {'x','zh'}, dimensions={0} | all-to-all | bytes 262144 | tf_op jit(solution)/shard_map/all_to_all | solution.py:217
  123.7 4.0 %collective-permute-start.18 = (f32[8,128]{1,0:T(8,128)S(1)}, f32[8,128]{1,0:T(8,128)S(1)}, u32[]{:S(2)}, u32[]{:S(2)}) collective-permute-start(f32[8,128]{1,0:T(8,128)S(1)} %slice_bitcast_fusion), channel_id=1, source_target_pairs={{0,8},{8,0},{1,9},{9,1},{2,10},{10,2},{3,11},{11,3},{4,12},{12,4},... | collective-permute-start | bytes 12296 | tf_op jit(solution)/shard_map/ppermute | solution.py:254
  (73 shorter events, 21.0 us)
Async XLA Ops:
  0.6 26.0 %collective-permute-start.5 = (bf16[512,2048]{1,0:T(8,128)(2,1)}, bf16[512,2048]{1,0:T(8,128)(2,1)S(1)}, u32[]{:S(2)}, u32[]{:S(2)}) collective-permute-start(bf16[512,2048]{1,0:T(8,128)(2,1)} %refs_6_.1), channel_id=1, source_target_pairs={{0,8},{8,0},{1,9},{9,1},{2,10},{10,2},{3,11},{11,3},{4,12},{12,4},... | collective-permute-start | bytes 6291464 | tf_op jit(solution)/shard_map/ppermute | solution.py:219
  5.7 9.4 %collective-permute-start.2 = (bf16[64,2048]{1,0:T(8,128)(2,1)}, bf16[64,2048]{1,0:T(8,128)(2,1)S(1)}, u32[]{:S(2)}, u32[]{:S(2)}) collective-permute-start(bf16[64,2048]{1,0:T(8,128)(2,1)} %shard_map.59.own.refs_0_.source), channel_id=1, source_target_pairs={{0,64},{64,128},{128,192},{192,0},{1,65},{65,129},{129,193},{193,1... | collective-permute-start | bytes 786440 | tf_op jit(solution)/shard_map/ppermute | solution.py:211
  5.7 9.4 %collective-permute-start.3 = (bf16[64,2048]{1,0:T(8,128)(2,1)}, bf16[64,2048]{1,0:T(8,128)(2,1)S(1)}, u32[]{:S(2)}, u32[]{:S(2)}) collective-permute-start(bf16[64,2048]{1,0:T(8,128)(2,1)} %shard_map.59.own.refs_0_.source), channel_id=1, source_target_pairs={{0,192},{64,0},{128,64},{192,128},{1,193},{65,1},{129,65},{193,129... | collective-permute-start | bytes 786440 | tf_op jit(solution)/shard_map/ppermute | solution.py:211
  8.4 12.2 %collective-permute-start = (bf16[64,2048]{1,0:T(8,128)(2,1)}, bf16[64,2048]{1,0:T(8,128)(2,1)S(1)}, u32[]{:S(2)}, u32[]{:S(2)}) collective-permute-start(bf16[64,2048]{1,0:T(8,128)(2,1)} %shard_map.59.own.refs_0_.source), channel_id=1, source_target_pairs={{0,16},{16,32},{32,48},{48,0},{1,17},{17,33},{33,49},{49,1},{2,18}... | collective-permute-start | bytes 786440 | tf_op jit(solution)/shard_map/ppermute | solution.py:223
  10.2 16.4 %collective-permute-start.1 = (bf16[64,2048]{1,0:T(8,128)(2,1)}, bf16[64,2048]{1,0:T(8,128)(2,1)S(1)}, u32[]{:S(2)}, u32[]{:S(2)}) collective-permute-start(bf16[64,2048]{1,0:T(8,128)(2,1)} %shard_map.59.own.refs_0_.source), channel_id=1, source_target_pairs={{0,48},{16,0},{32,16},{48,32},{1,49},{17,1},{33,17},{49,33},{2,50}... | collective-permute-start | bytes 786440 | tf_op jit(solution)/shard_map/ppermute | solution.py:223
  15.1 11.5 %collective-permute-start.4 = (bf16[64,2048]{1,0:T(8,128)(2,1)S(1)}, bf16[64,2048]{1,0:T(8,128)(2,1)}, u32[]{:S(2)}, u32[]{:S(2)}) collective-permute-start(bf16[64,2048]{1,0:T(8,128)(2,1)S(1)} %collective-permute-done.2.refs_1_), channel_id=1, source_target_pairs={{0,64},{64,128},{128,192},{192,0},{1,65},{65,129},{129,193},{193,1... | collective-permute-start | bytes 786440 | tf_op jit(solution)/shard_map/ppermute | solution.py:225
  15.2 19.4 %all-to-all-start = ((bf16[8,2,64,128]{3,2,1,0:T(8,128)(2,1)}), bf16[8,2,64,128]{3,2,1,0:T(8,128)(2,1)S(1)}, u32[]{:S(2)}, u32[]{:S(2)}) async-start(bf16[8,2,64,128]{3,2,1,0:T(8,128)(2,1)} %shard_map.60), calls=%async_computation | async-start | bytes 524288 | tf_op jit(solution)/shard_map/all_to_all | solution.py:214
  26.7 14.7 %collective-permute-start.6 = (bf16[64,2048]{1,0:T(8,128)(2,1)S(1)}, bf16[64,2048]{1,0:T(8,128)(2,1)S(1)}, u32[]{:S(2)}, u32[]{:S(2)}) collective-permute-start(bf16[64,2048]{1,0:T(8,128)(2,1)S(1)} %collective-permute-done.refs_4_), channel_id=1, source_target_pairs={{0,16},{16,32},{32,48},{48,0},{1,17},{17,33},{33,49},{49,1},{2,18}... | collective-permute-start | bytes 786440 | tf_op jit(solution)/shard_map/ppermute | solution.py:229
  29.8 11.6 %collective-permute-start.7 = (bf16[64,2048]{1,0:T(8,128)(2,1)S(1)}, bf16[64,2048]{1,0:T(8,128)(2,1)}, u32[]{:S(2)}, u32[]{:S(2)}) collective-permute-start(bf16[64,2048]{1,0:T(8,128)(2,1)S(1)} %collective-permute-done.refs_4_), channel_id=1, source_target_pairs={{0,64},{64,128},{128,192},{192,0},{1,65},{65,129},{129,193},{193,1... | collective-permute-start | bytes 786440 | tf_op jit(solution)/shard_map/ppermute | solution.py:211
  29.8 11.6 %collective-permute-start.8 = (bf16[64,2048]{1,0:T(8,128)(2,1)S(1)}, bf16[64,2048]{1,0:T(8,128)(2,1)}, u32[]{:S(2)}, u32[]{:S(2)}) collective-permute-start(bf16[64,2048]{1,0:T(8,128)(2,1)S(1)} %collective-permute-done.refs_4_), channel_id=1, source_target_pairs={{0,192},{64,0},{128,64},{192,128},{1,193},{65,1},{129,65},{193,129... | collective-permute-start | bytes 786440 | tf_op jit(solution)/shard_map/ppermute | solution.py:211
  32.5 9.3 %collective-permute-start.10 = (bf16[64,2048]{1,0:T(8,128)(2,1)S(1)}, bf16[64,2048]{1,0:T(8,128)(2,1)}, u32[]{:S(2)}, u32[]{:S(2)}) collective-permute-start(bf16[64,2048]{1,0:T(8,128)(2,1)S(1)} %collective-permute-done.1.refs_7_), channel_id=1, source_target_pairs={{0,192},{64,0},{128,64},{192,128},{1,193},{65,1},{129,65},{193,129... | collective-permute-start | bytes 786440 | tf_op jit(solution)/shard_map/ppermute | solution.py:211
  32.6 10.3 %collective-permute-start.9 = (bf16[64,2048]{1,0:T(8,128)(2,1)S(1)}, bf16[64,2048]{1,0:T(8,128)(2,1)}, u32[]{:S(2)}, u32[]{:S(2)}) collective-permute-start(bf16[64,2048]{1,0:T(8,128)(2,1)S(1)} %collective-permute-done.1.refs_7_), channel_id=1, source_target_pairs={{0,64},{64,128},{128,192},{192,0},{1,65},{65,129},{129,193},{193,1... | collective-permute-start | bytes 786440 | tf_op jit(solution)/shard_map/ppermute | solution.py:211
  35.3 23.3 %all-to-all-start.1 = ((bf16[16,64,128]{2,1,0:T(8,128)(2,1)}), bf16[16,64,128]{2,1,0:T(8,128)(2,1)S(1)}, u32[]{:S(2)}, u32[]{:S(2)}) async-start(bf16[16,64,128]{2,1,0:T(8,128)(2,1)} %shard_map.63), calls=%async_computation.1 | async-start | bytes 524288 | tf_op jit(solution)/shard_map/all_to_all | solution.py:217
  42.9 15.7 %collective-permute-start.11 = (bf16[64,2048]{1,0:T(8,128)(2,1)}, bf16[64,2048]{1,0:T(8,128)(2,1)S(1)}, u32[]{:S(2)}, u32[]{:S(2)}) collective-permute-start(bf16[64,2048]{1,0:T(8,128)(2,1)} %collective-permute-done.7.refs_5_), channel_id=1, source_target_pairs={{0,64},{64,128},{128,192},{192,0},{1,65},{65,129},{129,193},{193,1... | collective-permute-start | bytes 786440 | tf_op jit(solution)/shard_map/ppermute | solution.py:234
  42.9 15.7 %collective-permute-start.12 = (bf16[64,2048]{1,0:T(8,128)(2,1)}, bf16[64,2048]{1,0:T(8,128)(2,1)S(1)}, u32[]{:S(2)}, u32[]{:S(2)}) collective-permute-start(bf16[64,2048]{1,0:T(8,128)(2,1)} %collective-permute-done.10.refs_9_), channel_id=1, source_target_pairs={{0,192},{64,0},{128,64},{192,128},{1,193},{65,1},{129,65},{193,129... | collective-permute-start | bytes 786440 | tf_op jit(solution)/shard_map/ppermute | solution.py:234
  45.6 13.0 %collective-permute-start.13 = (bf16[64,2048]{1,0:T(8,128)(2,1)S(1)}, bf16[64,2048]{1,0:T(8,128)(2,1)S(1)}, u32[]{:S(2)}, u32[]{:S(2)}) collective-permute-start(bf16[64,2048]{1,0:T(8,128)(2,1)S(1)} %collective-permute-done.6.refs_2_), channel_id=1, source_target_pairs={{0,64},{64,128},{128,192},{192,0},{1,65},{65,129},{129,193},{193,1... | collective-permute-start | bytes 786440 | tf_op jit(solution)/shard_map/ppermute | solution.py:211
  45.6 13.0 %collective-permute-start.14 = (bf16[64,2048]{1,0:T(8,128)(2,1)S(1)}, bf16[64,2048]{1,0:T(8,128)(2,1)}, u32[]{:S(2)}, u32[]{:S(2)}) collective-permute-start(bf16[64,2048]{1,0:T(8,128)(2,1)S(1)} %collective-permute-done.6.refs_2_), channel_id=1, source_target_pairs={{0,192},{64,0},{128,64},{192,128},{1,193},{65,1},{129,65},{193,129... | collective-permute-start | bytes 786440 | tf_op jit(solution)/shard_map/ppermute | solution.py:211
  58.6 17.9 %all-to-all-start.2 = ((f16[8,640,128]{2,1,0:T(8,128)(2,1)}), f16[8,640,128]{2,1,0:T(8,128)(2,1)}, u32[]{:S(2)}, u32[]{:S(2)}) async-start(f16[8,640,128]{2,1,0:T(8,128)(2,1)} %convert_element_type.18), calls=%async_computation.2 | async-start | bytes 2621440 | tf_op jit(solution)/shard_map/all_to_all | solution.py:214
  63.0 6.5 %collective-permute-start.15 = (bf16[64,2048]{1,0:T(8,128)(2,1)S(1)}, bf16[64,2048]{1,0:T(8,128)(2,1)S(1)}, u32[]{:S(2)}, u32[]{:S(2)}) collective-permute-start(bf16[64,2048]{1,0:T(8,128)(2,1)S(1)} %collective-permute-done.13.refs_3_), channel_id=1, source_target_pairs={{0,64},{64,128},{128,192},{192,0},{1,65},{65,129},{129,193},{193,1... | collective-permute-start | bytes 786440 | tf_op jit(solution)/shard_map/ppermute | solution.py:240
  76.5 15.3 %all-to-all-start.3 = ((f16[8,384,128]{2,1,0:T(8,128)(2,1)}), f16[8,384,128]{2,1,0:T(8,128)(2,1)S(1)}, u32[]{:S(2)}, u32[]{:S(2)}) async-start(f16[8,384,128]{2,1,0:T(8,128)(2,1)} %convert_element_type.19), calls=%async_computation.3 | async-start | bytes 1572864 | tf_op jit(solution)/shard_map/all_to_all | solution.py:214
  83.4 8.5 %collective-permute-start.16 = (bf16[16,64,128]{2,1,0:T(8,128)(2,1)S(1)}, bf16[16,64,128]{2,1,0:T(8,128)(2,1)S(1)}, u32[]{:S(2)}, u32[]{:S(2)}) collective-permute-start(bf16[16,64,128]{2,1,0:T(8,128)(2,1)S(1)} %all-to-all-done.1.mine), channel_id=1, source_target_pairs={{0,8},{8,0},{1,9},{9,1},{2,10},{10,2},{3,11},{11,3},{4,12},{12,4},... | collective-permute-start | bytes 786440 | tf_op jit(solution)/shard_map/ppermute | solution.py:245
  94.0 11.9 %all-to-all-start.4 = ((f16[8,8,2,8,256]{4,3,2,1,0:T(8,128)(2,1)}), f16[8,8,2,8,256]{4,3,2,1,0:T(8,128)(2,1)S(1)}, u32[]{:S(2)}, u32[]{:S(2)}) async-start(f16[8,8,2,8,256]{4,3,2,1,0:T(8,128)(2,1)} %convert_element_type.22), calls=%async_computation.4 | async-start | bytes 1048576 | tf_op jit(solution)/shard_map/all_to_all | solution.py:214
  97.9 6.5 %collective-permute-start.17 = (f32[4,4,4,8,128]{4,3,2,1,0:T(8,128)S(1)}, f32[4,4,4,8,128]{4,3,2,1,0:T(8,128)S(1)}, u32[]{:S(2)}, u32[]{:S(2)}) collective-permute-start(f32[4,4,4,8,128]{4,3,2,1,0:T(8,128)S(1)} %get-tuple-element.55), channel_id=1, source_target_pairs={{0,8},{8,0},{1,9},{9,1},{2,10},{10,2},{3,11},{11,3},{4,12},{12,4},... | collective-permute-start | bytes 786440 | tf_op jit(solution)/shard_map/ppermute | solution.py:247
  123.7 4.8 %collective-permute-start.18 = (f32[8,128]{1,0:T(8,128)S(1)}, f32[8,128]{1,0:T(8,128)S(1)}, u32[]{:S(2)}, u32[]{:S(2)}) collective-permute-start(f32[8,128]{1,0:T(8,128)S(1)} %slice_bitcast_fusion), channel_id=1, source_target_pairs={{0,8},{8,0},{1,9},{9,1},{2,10},{10,2},{3,11},{11,3},{4,12},{12,4},... | collective-permute-start | bytes 12296 | tf_op jit(solution)/shard_map/ppermute | solution.py:254
  (10 other events, 109.9 us)

commit v7 on v6

--- a/solution.py
+++ b/solution.py
@@ -7,8 +7,8 @@
 from jax.experimental.pallas import tpu as pltpu
 from jax.sharding import Mesh, PartitionSpec as P
 
-EARLY = ((0, 0), (3, 0), (1, 0), (2, 0), (0, 1), (3, 1), (1, 1), (0, 3), (3, 3), (1, 3))
-LATE = ((2, 1), (2, 3), (0, 2), (3, 2), (1, 2), (2, 2))
+EARLY = ((0, 0), (3, 0), (1, 0), (2, 0), (0, 1), (3, 1), (1, 1), (0, 3))
+LATE = ((3, 3), (1, 3), (2, 1), (2, 3), (0, 2), (3, 2), (1, 2), (2, 2))
 SCALE = 64.0
 NT = (((1,), (1,)), ((), ()))
 VMEM = pl.BlockSpec(memory_space=pltpu.VMEM)
@@ -37,8 +37,8 @@
     )(mask, panel)
 
 
-def pieces_kernel(ids, own, pieces):
-    ic = ids[2]
+def pieces_kernel(own, pieces):
+    ic = lax.axis_index("core")
     low = lax.broadcasted_iota(jnp.int32, (64, 128), 1) < 64
     for b in range(2):
         for u in range(4):
@@ -49,17 +49,17 @@
             pieces[2 * u + 1, b] = jnp.where(low, pltpu.roll(p, 64, 1), q).astype(pieces.dtype)
 
 
-def pieces_call(ids, own):
+def pieces_call(own):
     return pl.pallas_call(
         pieces_kernel,
         out_shape=jax.ShapeDtypeStruct((8, 2, 64, 128), jnp.bfloat16),
-        in_specs=[SMEM, VMEM],
+        in_specs=[VMEM],
         out_specs=VMEM,
         cost_estimate=pl.CostEstimate(flops=1, bytes_accessed=2**19, transcendentals=0),
-    )(ids, own)
-
-
-def product_kernel(ids, *refs):
+    )(own)
+
+
+def product_kernel(*refs):
     slabs, (root, other_root, out, gathered, pair) = refs[:-5], refs[-5:]
 
     @pl.when(pl.program_id(0) == 0)
@@ -77,19 +77,19 @@
     out[1] = prod[:, 128:256] * SCALE
 
 
-def product_call(ids, slabs, root, other_root, vmem):
+def product_call(slabs, root, other_root, vmem):
     n = sum(slab.shape[0] for slab in slabs)
     return pl.pallas_call(
         product_kernel,
         grid=(4,),
         out_shape=jax.ShapeDtypeStruct((8, n, 128), jnp.float32),
-        in_specs=[SMEM] + [pl.BlockSpec(slab.shape, lambda t: (0, 0)) for slab in slabs]
+        in_specs=[pl.BlockSpec(slab.shape, lambda t: (0, 0)) for slab in slabs]
         + [pl.BlockSpec((128, 2048), lambda t: (t, 0))] * 2,
         out_specs=pl.BlockSpec((2, n, 128), lambda t: (t, 0, 0)),
         scratch_shapes=[pltpu.VMEM((n, 2048), jnp.bfloat16), pltpu.VMEM((256, 2048), jnp.bfloat16)],
         compiler_params=pltpu.CompilerParams(vmem_limit_bytes=vmem * 2**20),
         cost_estimate=pl.CostEstimate(flops=2 * n * 2048 * 1024, bytes_accessed=2 * n * 2048 + 6 * 2**20, transcendentals=0),
-    )(ids, *slabs, root, other_root)
+    )(*slabs, root, other_root)
 
 
 def mark_kernel(source, out):
@@ -121,8 +121,8 @@
     )(after, value)
 
 
-def diag_kernel(ids, early, late, mine, other, keep, give, diag):
-    ix, iz = ids[0], ids[1]
+def diag_kernel(early, late, mine, other, keep, give, diag):
+    ix, iz = lax.axis_index("x"), lax.axis_index("zh")
     low = lax.broadcasted_iota(jnp.int32, (8, 128), 1) < 64
     left = mine[...].astype(jnp.float32).reshape(16, 8, 8, 128)
     right = pltpu.roll(other[...].astype(jnp.float32), 64, 2).reshape(16, 8, 8, 128)
@@ -151,7 +151,7 @@
             diag[column, k, z] = d[i * 8:(i + 1) * 8, :]
 
 
-def diag_call(ids, early, late, mine, other):
+def diag_call(early, late, mine, other):
     return pl.pallas_call(
         diag_kernel,
         out_shape=(
@@ -159,15 +159,15 @@
             jax.ShapeDtypeStruct((4, 4, 4, 8, 128), jnp.float32),
             jax.ShapeDtypeStruct((8, 8, 2, 8, 256), jnp.float32),
         ),
-        in_specs=[SMEM] + [VMEM] * 4,
+        in_specs=[VMEM] * 4,
         out_specs=(VMEM,) * 3,
         compiler_params=pltpu.CompilerParams(vmem_limit_bytes=16 * 2**20),
         cost_estimate=pl.CostEstimate(flops=2 * 8 * 3 * 128 * 128 * 256, bytes_accessed=2**23, transcendentals=0),
-    )(ids, early, late, mine, other)
-
-
-def rows_kernel(ids, keep, got, out):
-    first = ids[2] == 0
+    )(early, late, mine, other)
+
+
+def rows_kernel(keep, got, out):
+    first = lax.axis_index("core") == 0
     for t in range(4):
         a, b = keep[t].reshape(16, 1, 8, 128), got[t].reshape(16, 1, 8, 128)
         even, odd = jnp.where(first, a, b), jnp.where(first, b, a)
@@ -176,15 +176,15 @@
         out[:, 2 * t + 1, :] = both[64:128, :]
 
 
-def rows_call(ids, keep, got):
+def rows_call(keep, got):
     return pl.pallas_call(
         rows_kernel,
         out_shape=jax.ShapeDtypeStruct((64, 8, 256), jnp.float32),
-        in_specs=[SMEM, VMEM, VMEM],
+        in_specs=[VMEM, VMEM],
         out_specs=VMEM,
         compiler_params=pltpu.CompilerParams(vmem_limit_bytes=16 * 2**20),
         cost_estimate=pl.CostEstimate(flops=0, bytes_accessed=2**20, transcendentals=0),
-    )(ids, keep, got)
+    )(keep, got)
 
 
 def pin(values):
@@ -198,7 +198,6 @@
 def shards(inverse_root, panel, block_mask, diag_inverse):
     ix, iz, ic = lax.axis_index("x"), lax.axis_index("zh"), lax.axis_index("core")
     col = lax.axis_index("zl") * 4 + lax.axis_index("y")
-    ids = jnp.stack([ix, iz, ic, col]).astype(jnp.int32)
     swap = [(0, 1), (1, 0)]
 
     def sum_parts(parts):
@@ -218,7 +217,7 @@
 
     other_root = lax.ppermute(inverse_root, "core", swap)
     own = mask_call(block_mask, jnp.transpose(panel, (1, 2, 0)).reshape(64, 2048))
-    pieces = pieces_call(ids, own)
+    pieces = pieces_call(own)
 
     z1, z3 = (lax.ppermute(own, "zh", turn(4, s)) for s in (1, 3))
     near0, pieces = pin((around(own), pieces))
@@ -233,20 +232,20 @@
 
     far1, far3 = lax.ppermute(near1[0], "x", turn(4, 1)), lax.ppermute(near3[1], "x", turn(4, -1))
     near2 = around(z2)
-    early = send_parts(product_call(ids, [own, *near0, far0, z1, *near1, z3, *near3], inverse_root, other_root, 58))
+    early = send_parts(product_call([own, *near0, far0, z1, *near1, z3], inverse_root, other_root, 58))
     far1, far3, near2, early, mine = pin((far1, far3, near2, early, mine))
 
     parts = to_columns(early)
     far2 = lax.ppermute(near2[0], "x", turn(4, 1))
     far2 = pin((far2,))[0]
 
-    late = send_parts(product_call(ids, [far1, far3, z2, *near2, far2], inverse_root, other_root, 24))
+    late = send_parts(product_call([*near3, far1, far3, z2, *near2, far2], inverse_root, other_root, 24))
     late, parts = pin((late, parts))
     other = lax.ppermute(mine, "core", swap)
-    keep, give, diag = diag_call(ids, sum_parts(parts), sum_parts(to_columns(late)), mine, other)
+    keep, give, diag = diag_call(sum_parts(parts), sum_parts(to_columns(late)), mine, other)
     got = lax.ppermute(give, "core", swap)
     here = jnp.sum(to_columns(diag.astype(jnp.float16)).astype(jnp.float32), axis=0)
-    panel_inverse = rows_call(ids, keep, got)
+    panel_inverse = rows_call(keep, got)
     here, panel_inverse = lax.optimization_barrier((here, panel_inverse))
     across = here.reshape(128, 256).T.reshape(2, 16, 8, 128)
     across = jnp.transpose(across, (1, 0, 2, 3))

time: 131 us -> 129 us (0.985)
  starting transfers between devices: 60.5 us -> 64.6 us
  blocking collectives: 17.5 us -> 15.3 us
  waiting for transfers between devices: 22.2 us -> 20.5 us
    ppermute x1, starting transfers between devices: 4.47 us -> 7.3 us  [shards(): other = lax.ppermute(mine, 'core', swap)]
    all_to_all x4, waiting for transfers between devices: 3.09 us -> 0.73 us  [to_columns(): return lax.all_to_all(value, ('zl', 'y'), 0, 0, tiled=True)]
    all_to_all x1, blocking collectives: 17.5 us -> 15.3 us  [to_rows(): return lax.all_to_all(value, ('x', 'zh'), 0, 0, tiled=True)]
    ppermute x1, starting transfers between devices: 5.3 us -> 7.39 us  [shards(): got = lax.ppermute(give, 'core', swap)]
    all_to_all x4, starting transfers between devices: 19.9 us -> 18.6 us  [to_columns(): return lax.all_to_all(value, ('zl', 'y'), 0, 0, tiled=True)]
  transfers between devices with their start and end apart: 24 -> 24, of which waited for: 10 -> 9; matrix products, arithmetic and copies ran while one was open for 5% -> 4% of each run, Pallas kernels for 13% -> 12%
where the time goes in v7:
time: 129 us; the launch traced here: 128 us
  starting transfers between devices  64.6 us (50%)
  waiting for transfers between devices  20.5 us (16%)
  Pallas kernels  16.6 us (13%)
  blocking collectives  15.3 us (12%)
  other arithmetic  7.31 us (6%)
  local copies, waits for them, and re-layouts  2.96 us (2%)
    all_to_all x4, starting transfers between devices, to_columns(): return lax.all_to_all(value, ('zl', 'y'), 0, 0, tiled=True)  18.6 us
    all_to_all x1, blocking collectives, to_rows(): return lax.all_to_all(value, ('x', 'zh'), 0, 0, tiled=True)  15.3 us
    pallas_call x2, Pallas kernels, product_call(): pl.pallas_call(product_kernel, grid=(4,), out_shape=jax.ShapeDtypeStruct(...  10.8 us
    ppermute x4, starting transfers between devices, around(): lax.ppermute(slab, 'x', turn(4, -1))  8.08 us
    ppermute x1, starting transfers between devices, shards(): got = lax.ppermute(give, 'core', swap)  7.39 us
    ppermute x1, starting transfers between devices, shards(): other = lax.ppermute(mine, 'core', swap)  7.3 us
    ppermute x1, waiting for transfers between devices, shards(): far2 = lax.ppermute(near2[0], 'x', turn(4, 1))  6.63 us
    ppermute x2, waiting for transfers between devices, shards(): z1, z3 = (lax.ppermute(own, 'zh', turn(4, s)) for s in (1, 3))  6.4 us
  transfers between devices with their start and end apart: 24, of which 9 were waited for; matrix products, arithmetic and copies ran while one was open for 4% of the time, Pallas kernels for 12%

profile of v7, /device:TPU:1, one launch (start us, length us, event | category | flops | bytes accessed | tf_op | source)
XLA Modules:
  0.0 128.2 jit_solution(8560882929030814212)
XLA Ops:
  0.6 3.3 %collective-permute-start.5 = (bf16[512,2048]{1,0:T(8,128)(2,1)}, bf16[512,2048]{1,0:T(8,128)(2,1)S(1)}, u32[]{:S(2)}, u32[]{:S(2)}) collective-permute-start(bf16[512,2048]{1,0:T(8,128)(2,1)} %refs_8_.3), channel_id=1, source_target_pairs={{0,8},{8,0},{1,9},{9,1},{2,10},{10,2},{3,11},{11,3},{4,12},{12,4},... | collective-permute-start | bytes 6291464 | tf_op jit(solution)/shard_map/ppermute | solution.py:218
  4.0 1.7 %shard_map.59.own.refs_0_.source = bf16[64,2048]{1,0:T(8,128)(2,1)} custom-call(s32[8,64]{1,0:T(8,128)} %mask.1, bf16[64,2048]{1,0:T(8,128)(2,1)} %bitcast.23), custom_call_target="tpu_custom_call" | custom-call | flops 1 | bytes 524288 | tf_op jit(solution)/shard_map/pallas_call | solution.py:31
  5.7 2.7 %collective-permute-start.3 = (bf16[64,2048]{1,0:T(8,128)(2,1)}, bf16[64,2048]{1,0:T(8,128)(2,1)S(1)}, u32[]{:S(2)}, u32[]{:S(2)}) collective-permute-start(bf16[64,2048]{1,0:T(8,128)(2,1)} %shard_map.59.own.refs_0_.source), channel_id=1, source_target_pairs={{0,192},{64,0},{128,64},{192,128},{1,193},{65,1},{129,65},{193,129... | collective-permute-start | bytes 786440 | tf_op jit(solution)/shard_map/ppermute | solution.py:210
  9.6 3.0 %collective-permute-start.1 = (bf16[64,2048]{1,0:T(8,128)(2,1)}, bf16[64,2048]{1,0:T(8,128)(2,1)}, u32[]{:S(2)}, u32[]{:S(2)}) collective-permute-start(bf16[64,2048]{1,0:T(8,128)(2,1)} %shard_map.59.own.refs_0_.source), channel_id=1, source_target_pairs={{0,48},{16,0},{32,16},{48,32},{1,49},{17,1},{33,17},{49,33},{2,50}... | collective-permute-start | bytes 786440 | tf_op jit(solution)/shard_map/ppermute | solution.py:222
  12.7 1.8 %shard_map.60 = bf16[8,2,64,128]{3,2,1,0:T(8,128)(2,1)} custom-call(bf16[64,2048]{1,0:T(8,128)(2,1)} %shard_map.59.own.refs_0_.source), custom_call_target="tpu_custom_call" | custom-call | flops 1 | bytes 524288 | tf_op jit(solution)/shard_map/pallas_call | solution.py:53
  15.2 4.5 %all-to-all-start = ((bf16[8,2,64,128]{3,2,1,0:T(8,128)(2,1)}), bf16[8,2,64,128]{3,2,1,0:T(8,128)(2,1)S(1)}, u32[]{:S(2)}, u32[]{:S(2)}) async-start(bf16[8,2,64,128]{3,2,1,0:T(8,128)(2,1)} %shard_map.60), calls=%async_computation | async-start | bytes 524288 | tf_op jit(solution)/shard_map/all_to_all | solution.py:213
  20.7 5.4 %collective-permute-done.1.refs_7_ = bf16[64,2048]{1,0:T(8,128)(2,1)} collective-permute-done((bf16[64,2048]{1,0:T(8,128)(2,1)}, bf16[64,2048]{1,0:T(8,128)(2,1)}, u32[]{:S(2)}, u32[]{:S(2)}) %collective-permute-start.1) | collective-permute-done | bytes 262176 | tf_op jit(solution)/shard_map/ppermute | solution.py:222
  26.2 3.1 %collective-permute-start.6 = (bf16[64,2048]{1,0:T(8,128)(2,1)}, bf16[64,2048]{1,0:T(8,128)(2,1)S(1)}, u32[]{:S(2)}, u32[]{:S(2)}) collective-permute-start(bf16[64,2048]{1,0:T(8,128)(2,1)} %collective-permute-done.refs_4_), channel_id=1, source_target_pairs={{0,16},{16,32},{32,48},{48,0},{1,17},{17,33},{33,49},{49,1},{2,18}... | collective-permute-start | bytes 786440 | tf_op jit(solution)/shard_map/ppermute | solution.py:228
  29.3 2.7 %collective-permute-start.8 = (bf16[64,2048]{1,0:T(8,128)(2,1)}, bf16[64,2048]{1,0:T(8,128)(2,1)}, u32[]{:S(2)}, u32[]{:S(2)}) collective-permute-start(bf16[64,2048]{1,0:T(8,128)(2,1)} %collective-permute-done.refs_4_), channel_id=1, source_target_pairs={{0,192},{64,0},{128,64},{192,128},{1,193},{65,1},{129,65},{193,129... | collective-permute-start | bytes 786440 | tf_op jit(solution)/shard_map/ppermute | solution.py:210
  34.8 3.7 %all-to-all-start.1 = ((bf16[16,64,128]{2,1,0:T(8,128)(2,1)}), bf16[16,64,128]{2,1,0:T(8,128)(2,1)S(1)}, u32[]{:S(2)}, u32[]{:S(2)}) async-start(bf16[16,64,128]{2,1,0:T(8,128)(2,1)} %shard_map.63), calls=%async_computation.1 | async-start | bytes 524288 | tf_op jit(solution)/shard_map/all_to_all | solution.py:216
  38.5 3.2 %collective-permute-done.6.refs_4_ = bf16[64,2048]{1,0:T(8,128)(2,1)S(1)} collective-permute-done((bf16[64,2048]{1,0:T(8,128)(2,1)}, bf16[64,2048]{1,0:T(8,128)(2,1)S(1)}, u32[]{:S(2)}, u32[]{:S(2)}) %collective-permute-start.6) | collective-permute-done | bytes 262176 | tf_op jit(solution)/shard_map/ppermute | solution.py:228
  42.6 2.7 %collective-permute-start.12 = (bf16[64,2048]{1,0:T(8,128)(2,1)S(1)}, bf16[64,2048]{1,0:T(8,128)(2,1)}, u32[]{:S(2)}, u32[]{:S(2)}) collective-permute-start(bf16[64,2048]{1,0:T(8,128)(2,1)S(1)} %collective-permute-done.10.refs_1_), channel_id=1, source_target_pairs={{0,192},{64,0},{128,64},{192,128},{1,193},{65,1},{129,65},{193,129... | collective-permute-start | bytes 786440 | tf_op jit(solution)/shard_map/ppermute | solution.py:233
  45.3 2.7 %collective-permute-start.14 = (bf16[64,2048]{1,0:T(8,128)(2,1)S(1)}, bf16[64,2048]{1,0:T(8,128)(2,1)}, u32[]{:S(2)}, u32[]{:S(2)}) collective-permute-start(bf16[64,2048]{1,0:T(8,128)(2,1)S(1)} %collective-permute-done.6.refs_4_), channel_id=1, source_target_pairs={{0,192},{64,0},{128,64},{192,128},{1,193},{65,1},{129,65},{193,129... | collective-permute-start | bytes 786440 | tf_op jit(solution)/shard_map/ppermute | solution.py:210
  47.9 6.5 %shard_map.61 = f32[8,512,128]{2,1,0:T(8,128)} custom-call(bf16[64,2048]{1,0:T(8,128)(2,1)} %shard_map.59.own.refs_0_.source, bf16[64,2048]{1,0:T(8,128)(2,1)} %copy-done.4, bf16[64,2048]{1,0:T(8,128)(2,1)} %copy-done.5, bf16[64,2048]{1,0:T(8,128)(2,1)} %copy-done.6, bf16[64,2048]{1,0:T(8,128)(2,1)} %collective-permute-done.refs_4_, ...), custom_call_target="tpu_custom_call" | custom-call | flops 2147483648 | bytes 8388608 | tf_op jit(solution)/shard_map/pallas_call | solution.py:82
  54.5 2.9 %convert_element_type.18 = f16[8,512,128]{2,1,0:T(8,128)(2,1)} convert(f32[8,512,128]{2,1,0:T(8,128)} %shard_map.61) | non-fusion elementwise | flops 524288 | bytes 3145728 | tf_op jit(solution)/shard_map/convert_element_type | solution.py:207
  57.4 4.2 %all-to-all-start.2 = ((f16[8,512,128]{2,1,0:T(8,128)(2,1)}), f16[8,512,128]{2,1,0:T(8,128)(2,1)}, u32[]{:S(2)}, u32[]{:S(2)}) async-start(f16[8,512,128]{2,1,0:T(8,128)(2,1)} %convert_element_type.18), calls=%async_computation.2 | async-start | bytes 2097152 | tf_op jit(solution)/shard_map/all_to_all | solution.py:213
  61.7 6.6 %collective-permute-done.15.refs_7_ = bf16[64,2048]{1,0:T(8,128)(2,1)S(1)} collective-permute-done((bf16[64,2048]{1,0:T(8,128)(2,1)}, bf16[64,2048]{1,0:T(8,128)(2,1)S(1)}, u32[]{:S(2)}, u32[]{:S(2)}) %collective-permute-start.15) | collective-permute-done | bytes 262176 | tf_op jit(solution)/shard_map/ppermute | solution.py:239
  70.0 4.3 %shard_map.64 = f32[8,512,128]{2,1,0:T(8,128)S(1)} custom-call(bf16[64,2048]{1,0:T(8,128)(2,1)S(1)} %collective-permute-done.9.refs_0_, bf16[64,2048]{1,0:T(8,128)(2,1)S(1)} %collective-permute-done.10.refs_1_, bf16[64,2048]{1,0:T(8,128)(2,1)S(1)} %collective-permute-done.11.refs_2_, bf16[64,2048]{1,0:T(8,128)(2,1)} %collective-permute-done.12.refs_3_, ...), custom_call_target="tpu_custom_call" | custom-call | flops 2147483648 | bytes 8388608 | tf_op jit(solution)/shard_map/pallas_call | solution.py:82
  75.4 5.0 %all-to-all-start.3 = ((f16[8,512,128]{2,1,0:T(8,128)(2,1)}), f16[8,512,128]{2,1,0:T(8,128)(2,1)S(1)}, u32[]{:S(2)}, u32[]{:S(2)}) async-start(f16[8,512,128]{2,1,0:T(8,128)(2,1)} %convert_element_type.19), calls=%async_computation.3 | async-start | bytes 2097152 | tf_op jit(solution)/shard_map/all_to_all | solution.py:213
  80.3 7.3 %collective-permute-start.16 = (bf16[16,64,128]{2,1,0:T(8,128)(2,1)S(1)}, bf16[16,64,128]{2,1,0:T(8,128)(2,1)S(1)}, u32[]{:S(2)}, u32[]{:S(2)}) collective-permute-start(bf16[16,64,128]{2,1,0:T(8,128)(2,1)S(1)} %all-to-all-done.1.mine), channel_id=1, source_target_pairs={{0,8},{8,0},{1,9},{9,1},{2,10},{10,2},{3,11},{11,3},{4,12},{12,4},... | collective-permute-start | bytes 786440 | tf_op jit(solution)/shard_map/ppermute | solution.py:244
  91.6 4.8 %all-to-all-start.4 = ((f16[8,8,2,8,256]{4,3,2,1,0:T(8,128)(2,1)}), f16[8,8,2,8,256]{4,3,2,1,0:T(8,128)(2,1)S(1)}, u32[]{:S(2)}, u32[]{:S(2)}) async-start(f16[8,8,2,8,256]{4,3,2,1,0:T(8,128)(2,1)} %convert_element_type.22), calls=%async_computation.4 | async-start | bytes 1048576 | tf_op jit(solution)/shard_map/all_to_all | solution.py:213
  96.4 7.4 %collective-permute-start.17 = (f32[4,4,4,8,128]{4,3,2,1,0:T(8,128)S(1)}, f32[4,4,4,8,128]{4,3,2,1,0:T(8,128)S(1)}, u32[]{:S(2)}, u32[]{:S(2)}) collective-permute-start(f32[4,4,4,8,128]{4,3,2,1,0:T(8,128)S(1)} %get-tuple-element.55), channel_id=1, source_target_pairs={{0,8},{8,0},{1,9},{9,1},{2,10},{10,2},{3,11},{11,3},{4,12},{12,4},... | collective-permute-start | bytes 786440 | tf_op jit(solution)/shard_map/ppermute | solution.py:246
  106.2 15.3 %all_to_all.30 = f32[16,2,8,128]{3,2,1,0:T(8,128)S(1)} all-to-all(f32[16,2,8,128]{3,2,1,0:T(8,128)S(1)} %copy.10), channel_id=1, replica_groups=mesh['x'=4,'zh'=4,'core'=2,'zl'=2,'y'=4] {'x','zh'}, dimensions={0} | all-to-all | bytes 262144 | tf_op jit(solution)/shard_map/all_to_all | solution.py:216
  121.6 4.5 %collective-permute-start.18 = (f32[8,128]{1,0:T(8,128)S(1)}, f32[8,128]{1,0:T(8,128)S(1)}, u32[]{:S(2)}, u32[]{:S(2)}) collective-permute-start(f32[8,128]{1,0:T(8,128)S(1)} %slice_bitcast_fusion), channel_id=1, source_target_pairs={{0,8},{8,0},{1,9},{9,1},{2,10},{10,2},{3,11},{11,3},{4,12},{12,4},... | collective-permute-start | bytes 12296 | tf_op jit(solution)/shard_map/ppermute | solution.py:253
  (68 shorter events, 17.8 us)
Async XLA Ops:
  0.6 25.5 %collective-permute-start.5 = (bf16[512,2048]{1,0:T(8,128)(2,1)}, bf16[512,2048]{1,0:T(8,128)(2,1)S(1)}, u32[]{:S(2)}, u32[]{:S(2)}) collective-permute-start(bf16[512,2048]{1,0:T(8,128)(2,1)} %refs_8_.3), channel_id=1, source_target_pairs={{0,8},{8,0},{1,9},{9,1},{2,10},{10,2},{3,11},{11,3},{4,12},{12,4},... | collective-permute-start | bytes 6291464 | tf_op jit(solution)/shard_map/ppermute | solution.py:218
  5.7 9.4 %collective-permute-start.2 = (bf16[64,2048]{1,0:T(8,128)(2,1)}, bf16[64,2048]{1,0:T(8,128)(2,1)S(1)}, u32[]{:S(2)}, u32[]{:S(2)}) collective-permute-start(bf16[64,2048]{1,0:T(8,128)(2,1)} %shard_map.59.own.refs_0_.source), channel_id=1, source_target_pairs={{0,64},{64,128},{128,192},{192,0},{1,65},{65,129},{129,193},{193,1... | collective-permute-start | bytes 786440 | tf_op jit(solution)/shard_map/ppermute | solution.py:210
  5.7 9.4 %collective-permute-start.3 = (bf16[64,2048]{1,0:T(8,128)(2,1)}, bf16[64,2048]{1,0:T(8,128)(2,1)S(1)}, u32[]{:S(2)}, u32[]{:S(2)}) collective-permute-start(bf16[64,2048]{1,0:T(8,128)(2,1)} %shard_map.59.own.refs_0_.source), channel_id=1, source_target_pairs={{0,192},{64,0},{128,64},{192,128},{1,193},{65,1},{129,65},{193,129... | collective-permute-start | bytes 786440 | tf_op jit(solution)/shard_map/ppermute | solution.py:210
  8.4 12.4 %collective-permute-start = (bf16[64,2048]{1,0:T(8,128)(2,1)}, bf16[64,2048]{1,0:T(8,128)(2,1)}, u32[]{:S(2)}, u32[]{:S(2)}) collective-permute-start(bf16[64,2048]{1,0:T(8,128)(2,1)} %shard_map.59.own.refs_0_.source), channel_id=1, source_target_pairs={{0,16},{16,32},{32,48},{48,0},{1,17},{17,33},{33,49},{49,1},{2,18}... | collective-permute-start | bytes 786440 | tf_op jit(solution)/shard_map/ppermute | solution.py:222
  9.6 16.5 %collective-permute-start.1 = (bf16[64,2048]{1,0:T(8,128)(2,1)}, bf16[64,2048]{1,0:T(8,128)(2,1)}, u32[]{:S(2)}, u32[]{:S(2)}) collective-permute-start(bf16[64,2048]{1,0:T(8,128)(2,1)} %shard_map.59.own.refs_0_.source), channel_id=1, source_target_pairs={{0,48},{16,0},{32,16},{48,32},{1,49},{17,1},{33,17},{49,33},{2,50}... | collective-permute-start | bytes 786440 | tf_op jit(solution)/shard_map/ppermute | solution.py:222
  15.1 11.0 %collective-permute-start.4 = (bf16[64,2048]{1,0:T(8,128)(2,1)S(1)}, bf16[64,2048]{1,0:T(8,128)(2,1)S(1)}, u32[]{:S(2)}, u32[]{:S(2)}) collective-permute-start(bf16[64,2048]{1,0:T(8,128)(2,1)S(1)} %collective-permute-done.2.refs_1_), channel_id=1, source_target_pairs={{0,64},{64,128},{128,192},{192,0},{1,65},{65,129},{129,193},{193,1... | collective-permute-start | bytes 786440 | tf_op jit(solution)/shard_map/ppermute | solution.py:224
  15.2 18.8 %all-to-all-start = ((bf16[8,2,64,128]{3,2,1,0:T(8,128)(2,1)}), bf16[8,2,64,128]{3,2,1,0:T(8,128)(2,1)S(1)}, u32[]{:S(2)}, u32[]{:S(2)}) async-start(bf16[8,2,64,128]{3,2,1,0:T(8,128)(2,1)} %shard_map.60), calls=%async_computation | async-start | bytes 524288 | tf_op jit(solution)/shard_map/all_to_all | solution.py:213
  26.2 15.6 %collective-permute-start.6 = (bf16[64,2048]{1,0:T(8,128)(2,1)}, bf16[64,2048]{1,0:T(8,128)(2,1)S(1)}, u32[]{:S(2)}, u32[]{:S(2)}) collective-permute-start(bf16[64,2048]{1,0:T(8,128)(2,1)} %collective-permute-done.refs_4_), channel_id=1, source_target_pairs={{0,16},{16,32},{32,48},{48,0},{1,17},{17,33},{33,49},{49,1},{2,18}... | collective-permute-start | bytes 786440 | tf_op jit(solution)/shard_map/ppermute | solution.py:228
  29.3 12.4 %collective-permute-start.7 = (bf16[64,2048]{1,0:T(8,128)(2,1)}, bf16[64,2048]{1,0:T(8,128)(2,1)}, u32[]{:S(2)}, u32[]{:S(2)}) collective-permute-start(bf16[64,2048]{1,0:T(8,128)(2,1)} %collective-permute-done.refs_4_), channel_id=1, source_target_pairs={{0,64},{64,128},{128,192},{192,0},{1,65},{65,129},{129,193},{193,1... | collective-permute-start | bytes 786440 | tf_op jit(solution)/shard_map/ppermute | solution.py:210
  29.3 12.4 %collective-permute-start.8 = (bf16[64,2048]{1,0:T(8,128)(2,1)}, bf16[64,2048]{1,0:T(8,128)(2,1)}, u32[]{:S(2)}, u32[]{:S(2)}) collective-permute-start(bf16[64,2048]{1,0:T(8,128)(2,1)} %collective-permute-done.refs_4_), channel_id=1, source_target_pairs={{0,192},{64,0},{128,64},{192,128},{1,193},{65,1},{129,65},{193,129... | collective-permute-start | bytes 786440 | tf_op jit(solution)/shard_map/ppermute | solution.py:210
  32.0 9.7 %collective-permute-start.10 = (bf16[64,2048]{1,0:T(8,128)(2,1)}, bf16[64,2048]{1,0:T(8,128)(2,1)S(1)}, u32[]{:S(2)}, u32[]{:S(2)}) collective-permute-start(bf16[64,2048]{1,0:T(8,128)(2,1)} %collective-permute-done.1.refs_7_), channel_id=1, source_target_pairs={{0,192},{64,0},{128,64},{192,128},{1,193},{65,1},{129,65},{193,129... | collective-permute-start | bytes 786440 | tf_op jit(solution)/shard_map/ppermute | solution.py:210
  32.1 10.5 %collective-permute-start.9 = (bf16[64,2048]{1,0:T(8,128)(2,1)}, bf16[64,2048]{1,0:T(8,128)(2,1)S(1)}, u32[]{:S(2)}, u32[]{:S(2)}) collective-permute-start(bf16[64,2048]{1,0:T(8,128)(2,1)} %collective-permute-done.1.refs_7_), channel_id=1, source_target_pairs={{0,64},{64,128},{128,192},{192,0},{1,65},{65,129},{129,193},{193,1... | collective-permute-start | bytes 786440 | tf_op jit(solution)/shard_map/ppermute | solution.py:210
  34.8 22.6 %all-to-all-start.1 = ((bf16[16,64,128]{2,1,0:T(8,128)(2,1)}), bf16[16,64,128]{2,1,0:T(8,128)(2,1)S(1)}, u32[]{:S(2)}, u32[]{:S(2)}) async-start(bf16[16,64,128]{2,1,0:T(8,128)(2,1)} %shard_map.63), calls=%async_computation.1 | async-start | bytes 524288 | tf_op jit(solution)/shard_map/all_to_all | solution.py:216
  42.6 14.8 %collective-permute-start.11 = (bf16[64,2048]{1,0:T(8,128)(2,1)}, bf16[64,2048]{1,0:T(8,128)(2,1)S(1)}, u32[]{:S(2)}, u32[]{:S(2)}) collective-permute-start(bf16[64,2048]{1,0:T(8,128)(2,1)} %collective-permute-done.7.refs_5_), channel_id=1, source_target_pairs={{0,64},{64,128},{128,192},{192,0},{1,65},{65,129},{129,193},{193,1... | collective-permute-start | bytes 786440 | tf_op jit(solution)/shard_map/ppermute | solution.py:233
  42.6 14.8 %collective-permute-start.12 = (bf16[64,2048]{1,0:T(8,128)(2,1)S(1)}, bf16[64,2048]{1,0:T(8,128)(2,1)}, u32[]{:S(2)}, u32[]{:S(2)}) collective-permute-start(bf16[64,2048]{1,0:T(8,128)(2,1)S(1)} %collective-permute-done.10.refs_1_), channel_id=1, source_target_pairs={{0,192},{64,0},{128,64},{192,128},{1,193},{65,1},{129,65},{193,129... | collective-permute-start | bytes 786440 | tf_op jit(solution)/shard_map/ppermute | solution.py:233
  45.3 12.1 %collective-permute-start.13 = (bf16[64,2048]{1,0:T(8,128)(2,1)S(1)}, bf16[64,2048]{1,0:T(8,128)(2,1)}, u32[]{:S(2)}, u32[]{:S(2)}) collective-permute-start(bf16[64,2048]{1,0:T(8,128)(2,1)S(1)} %collective-permute-done.6.refs_4_), channel_id=1, source_target_pairs={{0,64},{64,128},{128,192},{192,0},{1,65},{65,129},{129,193},{193,1... | collective-permute-start | bytes 786440 | tf_op jit(solution)/shard_map/ppermute | solution.py:210
  45.3 12.1 %collective-permute-start.14 = (bf16[64,2048]{1,0:T(8,128)(2,1)S(1)}, bf16[64,2048]{1,0:T(8,128)(2,1)}, u32[]{:S(2)}, u32[]{:S(2)}) collective-permute-start(bf16[64,2048]{1,0:T(8,128)(2,1)S(1)} %collective-permute-done.6.refs_4_), channel_id=1, source_target_pairs={{0,192},{64,0},{128,64},{192,128},{1,193},{65,1},{129,65},{193,129... | collective-permute-start | bytes 786440 | tf_op jit(solution)/shard_map/ppermute | solution.py:210
  57.4 18.0 %all-to-all-start.2 = ((f16[8,512,128]{2,1,0:T(8,128)(2,1)}), f16[8,512,128]{2,1,0:T(8,128)(2,1)}, u32[]{:S(2)}, u32[]{:S(2)}) async-start(f16[8,512,128]{2,1,0:T(8,128)(2,1)} %convert_element_type.18), calls=%async_computation.2 | async-start | bytes 2097152 | tf_op jit(solution)/shard_map/all_to_all | solution.py:213
  61.6 6.7 %collective-permute-start.15 = (bf16[64,2048]{1,0:T(8,128)(2,1)}, bf16[64,2048]{1,0:T(8,128)(2,1)S(1)}, u32[]{:S(2)}, u32[]{:S(2)}) collective-permute-start(bf16[64,2048]{1,0:T(8,128)(2,1)} %collective-permute-done.13.refs_5_), channel_id=1, source_target_pairs={{0,64},{64,128},{128,192},{192,0},{1,65},{65,129},{129,193},{193,1... | collective-permute-start | bytes 786440 | tf_op jit(solution)/shard_map/ppermute | solution.py:239
  75.4 14.4 %all-to-all-start.3 = ((f16[8,512,128]{2,1,0:T(8,128)(2,1)}), f16[8,512,128]{2,1,0:T(8,128)(2,1)S(1)}, u32[]{:S(2)}, u32[]{:S(2)}) async-start(f16[8,512,128]{2,1,0:T(8,128)(2,1)} %convert_element_type.19), calls=%async_computation.3 | async-start | bytes 2097152 | tf_op jit(solution)/shard_map/all_to_all | solution.py:213
  80.3 9.6 %collective-permute-start.16 = (bf16[16,64,128]{2,1,0:T(8,128)(2,1)S(1)}, bf16[16,64,128]{2,1,0:T(8,128)(2,1)S(1)}, u32[]{:S(2)}, u32[]{:S(2)}) collective-permute-start(bf16[16,64,128]{2,1,0:T(8,128)(2,1)S(1)} %all-to-all-done.1.mine), channel_id=1, source_target_pairs={{0,8},{8,0},{1,9},{9,1},{2,10},{10,2},{3,11},{11,3},{4,12},{12,4},... | collective-permute-start | bytes 786440 | tf_op jit(solution)/shard_map/ppermute | solution.py:244
  91.6 14.4 %all-to-all-start.4 = ((f16[8,8,2,8,256]{4,3,2,1,0:T(8,128)(2,1)}), f16[8,8,2,8,256]{4,3,2,1,0:T(8,128)(2,1)S(1)}, u32[]{:S(2)}, u32[]{:S(2)}) async-start(f16[8,8,2,8,256]{4,3,2,1,0:T(8,128)(2,1)} %convert_element_type.22), calls=%async_computation.4 | async-start | bytes 1048576 | tf_op jit(solution)/shard_map/all_to_all | solution.py:213
  96.4 8.6 %collective-permute-start.17 = (f32[4,4,4,8,128]{4,3,2,1,0:T(8,128)S(1)}, f32[4,4,4,8,128]{4,3,2,1,0:T(8,128)S(1)}, u32[]{:S(2)}, u32[]{:S(2)}) collective-permute-start(f32[4,4,4,8,128]{4,3,2,1,0:T(8,128)S(1)} %get-tuple-element.55), channel_id=1, source_target_pairs={{0,8},{8,0},{1,9},{9,1},{2,10},{10,2},{3,11},{11,3},{4,12},{12,4},... | collective-permute-start | bytes 786440 | tf_op jit(solution)/shard_map/ppermute | solution.py:246
  121.6 5.4 %collective-permute-start.18 = (f32[8,128]{1,0:T(8,128)S(1)}, f32[8,128]{1,0:T(8,128)S(1)}, u32[]{:S(2)}, u32[]{:S(2)}) collective-permute-start(f32[8,128]{1,0:T(8,128)S(1)} %slice_bitcast_fusion), channel_id=1, source_target_pairs={{0,8},{8,0},{1,9},{9,1},{2,10},{10,2},{3,11},{11,3},{4,12},{12,4},... | collective-permute-start | bytes 12296 | tf_op jit(solution)/shard_map/ppermute | solution.py:253
  (8 other events, 93.2 us)

commit v8 on v7

--- a/solution.py
+++ b/solution.py
@@ -233,7 +233,7 @@
     far1, far3 = lax.ppermute(near1[0], "x", turn(4, 1)), lax.ppermute(near3[1], "x", turn(4, -1))
     near2 = around(z2)
     early = send_parts(product_call([own, *near0, far0, z1, *near1, z3], inverse_root, other_root, 58))
-    far1, far3, near2, early, mine = pin((far1, far3, near2, early, mine))
+    near2, early, mine = pin((near2, early, mine))
 
     parts = to_columns(early)
     far2 = lax.ppermute(near2[0], "x", turn(4, 1))

time: 129 us -> 128 us (level)
  waiting for transfers between devices: 20.5 us -> 22 us
    ppermute x1, waiting for transfers between devices: 0.01 us -> 3.48 us  [shards(): lax.ppermute(near1[0], 'x', turn(4, 1))]
    ppermute x1, waiting for transfers between devices: 6.63 us -> 3.66 us  [shards(): far2 = lax.ppermute(near2[0], 'x', turn(4, 1))]
    all_to_all x4, starting transfers between devices: 18.6 us -> 17.2 us  [to_columns(): return lax.all_to_all(value, ('zl', 'y'), 0, 0, tiled=True)]
  transfers between devices with their start and end apart: 24 -> 24, of which waited for: 9 -> 10; matrix products, arithmetic and copies ran while one was open for 4% -> 4% of each run, Pallas kernels for 12% -> 12%
where the time goes in v8:
time: 128 us; the launch traced here: 127 us
  starting transfers between devices  63.4 us (50%)
  waiting for transfers between devices  22 us (17%)
  Pallas kernels  16.5 us (13%)
  blocking collectives  14.2 us (11%)
  other arithmetic  7.31 us (6%)
  local copies, waits for them, and re-layouts  2.95 us (2%)
    all_to_all x4, starting transfers between devices, to_columns(): return lax.all_to_all(value, ('zl', 'y'), 0, 0, tiled=True)  17.2 us
    all_to_all x1, blocking collectives, to_rows(): return lax.all_to_all(value, ('x', 'zh'), 0, 0, tiled=True)  14.2 us
    pallas_call x2, Pallas kernels, product_call(): pl.pallas_call(product_kernel, grid=(4,), out_shape=jax.ShapeDtypeStruct(...  10.6 us
    ppermute x4, starting transfers between devices, around(): lax.ppermute(slab, 'x', turn(4, -1))  8.08 us
    ppermute x1, starting transfers between devices, shards(): got = lax.ppermute(give, 'core', swap)  7.39 us
    ppermute x2, waiting for transfers between devices, shards(): z1, z3 = (lax.ppermute(own, 'zh', turn(4, s)) for s in (1, 3))  6.4 us
    ppermute x1, starting transfers between devices, shards(): other = lax.ppermute(mine, 'core', swap)  6.35 us
    ppermute x1, starting transfers between devices, shards(): came = lax.ppermute(here[1], 'core', swap)  5.48 us
  transfers between devices with their start and end apart: 24, of which 10 were waited for; matrix products, arithmetic and copies ran while one was open for 4% of the time, Pallas kernels for 12%

profile of v8, /device:TPU:1, one launch (start us, length us, event | category | flops | bytes accessed | tf_op | source)
XLA Modules:
  0.0 127.2 jit_solution(10596194993642587743)
XLA Ops:
  0.6 3.3 %collective-permute-start.5 = (bf16[512,2048]{1,0:T(8,128)(2,1)}, bf16[512,2048]{1,0:T(8,128)(2,1)S(1)}, u32[]{:S(2)}, u32[]{:S(2)}) collective-permute-start(bf16[512,2048]{1,0:T(8,128)(2,1)} %refs_8_.3), channel_id=1, source_target_pairs={{0,8},{8,0},{1,9},{9,1},{2,10},{10,2},{3,11},{11,3},{4,12},{12,4},... | collective-permute-start | bytes 6291464 | tf_op jit(solution)/shard_map/ppermute | solution.py:218
  5.7 2.7 %collective-permute-start.3 = (bf16[64,2048]{1,0:T(8,128)(2,1)}, bf16[64,2048]{1,0:T(8,128)(2,1)S(1)}, u32[]{:S(2)}, u32[]{:S(2)}) collective-permute-start(bf16[64,2048]{1,0:T(8,128)(2,1)} %shard_map.59.own.refs_0_.source), channel_id=1, source_target_pairs={{0,192},{64,0},{128,64},{192,128},{1,193},{65,1},{129,65},{193,129... | collective-permute-start | bytes 786440 | tf_op jit(solution)/shard_map/ppermute | solution.py:210
  9.6 3.0 %collective-permute-start.1 = (bf16[64,2048]{1,0:T(8,128)(2,1)}, bf16[64,2048]{1,0:T(8,128)(2,1)}, u32[]{:S(2)}, u32[]{:S(2)}) collective-permute-start(bf16[64,2048]{1,0:T(8,128)(2,1)} %shard_map.59.own.refs_0_.source), channel_id=1, source_target_pairs={{0,48},{16,0},{32,16},{48,32},{1,49},{17,1},{33,17},{49,33},{2,50}... | collective-permute-start | bytes 786440 | tf_op jit(solution)/shard_map/ppermute | solution.py:222
  12.7 1.8 %shard_map.60 = bf16[8,2,64,128]{3,2,1,0:T(8,128)(2,1)} custom-call(bf16[64,2048]{1,0:T(8,128)(2,1)} %shard_map.59.own.refs_0_.source), custom_call_target="tpu_custom_call" | custom-call | flops 1 | bytes 524288 | tf_op jit(solution)/shard_map/pallas_call | solution.py:53
  15.2 4.5 %all-to-all-start = ((bf16[8,2,64,128]{3,2,1,0:T(8,128)(2,1)}), bf16[8,2,64,128]{3,2,1,0:T(8,128)(2,1)S(1)}, u32[]{:S(2)}, u32[]{:S(2)}) async-start(bf16[8,2,64,128]{3,2,1,0:T(8,128)(2,1)} %shard_map.60), calls=%async_computation | async-start | bytes 524288 | tf_op jit(solution)/shard_map/all_to_all | solution.py:213
  20.7 5.4 %collective-permute-done.1.refs_7_ = bf16[64,2048]{1,0:T(8,128)(2,1)} collective-permute-done((bf16[64,2048]{1,0:T(8,128)(2,1)}, bf16[64,2048]{1,0:T(8,128)(2,1)}, u32[]{:S(2)}, u32[]{:S(2)}) %collective-permute-start.1) | collective-permute-done | bytes 262176 | tf_op jit(solution)/shard_map/ppermute | solution.py:222
  26.2 3.1 %collective-permute-start.6 = (bf16[64,2048]{1,0:T(8,128)(2,1)}, bf16[64,2048]{1,0:T(8,128)(2,1)S(1)}, u32[]{:S(2)}, u32[]{:S(2)}) collective-permute-start(bf16[64,2048]{1,0:T(8,128)(2,1)} %collective-permute-done.refs_4_), channel_id=1, source_target_pairs={{0,16},{16,32},{32,48},{48,0},{1,17},{17,33},{33,49},{49,1},{2,18}... | collective-permute-start | bytes 786440 | tf_op jit(solution)/shard_map/ppermute | solution.py:228
  29.3 2.7 %collective-permute-start.8 = (bf16[64,2048]{1,0:T(8,128)(2,1)}, bf16[64,2048]{1,0:T(8,128)(2,1)}, u32[]{:S(2)}, u32[]{:S(2)}) collective-permute-start(bf16[64,2048]{1,0:T(8,128)(2,1)} %collective-permute-done.refs_4_), channel_id=1, source_target_pairs={{0,192},{64,0},{128,64},{192,128},{1,193},{65,1},{129,65},{193,129... | collective-permute-start | bytes 786440 | tf_op jit(solution)/shard_map/ppermute | solution.py:210
  34.8 3.7 %all-to-all-start.1 = ((bf16[16,64,128]{2,1,0:T(8,128)(2,1)}), bf16[16,64,128]{2,1,0:T(8,128)(2,1)S(1)}, u32[]{:S(2)}, u32[]{:S(2)}) async-start(bf16[16,64,128]{2,1,0:T(8,128)(2,1)} %shard_map.63), calls=%async_computation.1 | async-start | bytes 524288 | tf_op jit(solution)/shard_map/all_to_all | solution.py:216
  38.5 3.2 %collective-permute-done.6.refs_4_ = bf16[64,2048]{1,0:T(8,128)(2,1)S(1)} collective-permute-done((bf16[64,2048]{1,0:T(8,128)(2,1)}, bf16[64,2048]{1,0:T(8,128)(2,1)S(1)}, u32[]{:S(2)}, u32[]{:S(2)}) %collective-permute-start.6) | collective-permute-done | bytes 262176 | tf_op jit(solution)/shard_map/ppermute | solution.py:228
  42.6 2.7 %collective-permute-start.14 = (bf16[64,2048]{1,0:T(8,128)(2,1)S(1)}, bf16[64,2048]{1,0:T(8,128)(2,1)}, u32[]{:S(2)}, u32[]{:S(2)}) collective-permute-start(bf16[64,2048]{1,0:T(8,128)(2,1)S(1)} %collective-permute-done.6.refs_4_), channel_id=1, source_target_pairs={{0,192},{64,0},{128,64},{192,128},{1,193},{65,1},{129,65},{193,129... | collective-permute-start | bytes 786440 | tf_op jit(solution)/shard_map/ppermute | solution.py:210
  45.3 6.5 %shard_map.61 = f32[8,512,128]{2,1,0:T(8,128)} custom-call(bf16[64,2048]{1,0:T(8,128)(2,1)} %shard_map.59.own.refs_0_.source, bf16[64,2048]{1,0:T(8,128)(2,1)} %copy-done.4, bf16[64,2048]{1,0:T(8,128)(2,1)} %copy-done.5, bf16[64,2048]{1,0:T(8,128)(2,1)} %copy-done.6, bf16[64,2048]{1,0:T(8,128)(2,1)} %collective-permute-done.refs_4_, ...), custom_call_target="tpu_custom_call" | custom-call | flops 2147483648 | bytes 8388608 | tf_op jit(solution)/shard_map/pallas_call | solution.py:82
  51.8 2.9 %convert_element_type.18 = f16[8,512,128]{2,1,0:T(8,128)(2,1)} convert(f32[8,512,128]{2,1,0:T(8,128)} %shard_map.61) | non-fusion elementwise | flops 524288 | bytes 3145728 | tf_op jit(solution)/shard_map/convert_element_type | solution.py:207
  54.7 4.2 %all-to-all-start.2 = ((f16[8,512,128]{2,1,0:T(8,128)(2,1)}), f16[8,512,128]{2,1,0:T(8,128)(2,1)}, u32[]{:S(2)}, u32[]{:S(2)}) async-start(f16[8,512,128]{2,1,0:T(8,128)(2,1)} %convert_element_type.18), calls=%async_computation.2 | async-start | bytes 2097152 | tf_op jit(solution)/shard_map/all_to_all | solution.py:213
  60.0 2.0 %collective-permute-start.12 = (bf16[64,2048]{1,0:T(8,128)(2,1)S(1)}, bf16[64,2048]{1,0:T(8,128)(2,1)S(1)}, u32[]{:S(2)}, u32[]{:S(2)}) collective-permute-start(bf16[64,2048]{1,0:T(8,128)(2,1)S(1)} %collective-permute-done.10.refs_1_), channel_id=1, source_target_pairs={{0,192},{64,0},{128,64},{192,128},{1,193},{65,1},{129,65},{193,129... | collective-permute-start | bytes 786440 | tf_op jit(solution)/shard_map/ppermute | solution.py:233
  62.0 3.7 %collective-permute-done.15.refs_7_ = bf16[64,2048]{1,0:T(8,128)(2,1)S(1)} collective-permute-done((bf16[64,2048]{1,0:T(8,128)(2,1)S(1)}, bf16[64,2048]{1,0:T(8,128)(2,1)S(1)}, u32[]{:S(2)}, u32[]{:S(2)}) %collective-permute-start.15) | collective-permute-done | bytes 262176 | tf_op jit(solution)/shard_map/ppermute | solution.py:239
  65.6 3.5 %collective-permute-done.11.refs_2_ = bf16[64,2048]{1,0:T(8,128)(2,1)S(1)} collective-permute-done((bf16[64,2048]{1,0:T(8,128)(2,1)}, bf16[64,2048]{1,0:T(8,128)(2,1)S(1)}, u32[]{:S(2)}, u32[]{:S(2)}) %collective-permute-start.11) | collective-permute-done | bytes 262176 | tf_op jit(solution)/shard_map/ppermute | solution.py:233
  70.7 4.1 %shard_map.64 = f32[8,512,128]{2,1,0:T(8,128)S(1)} custom-call(bf16[64,2048]{1,0:T(8,128)(2,1)S(1)} %collective-permute-done.9.refs_0_, bf16[64,2048]{1,0:T(8,128)(2,1)S(1)} %collective-permute-done.10.refs_1_, bf16[64,2048]{1,0:T(8,128)(2,1)S(1)} %collective-permute-done.11.refs_2_, bf16[64,2048]{1,0:T(8,128)(2,1)S(1)} %collective-permute-done.12.refs_3_, ...), custom_call_target="tpu_custom_call" | custom-call | flops 2147483648 | bytes 8388608 | tf_op jit(solution)/shard_map/pallas_call | solution.py:82
  75.9 4.5 %all-to-all-start.3 = ((f16[8,512,128]{2,1,0:T(8,128)(2,1)}), f16[8,512,128]{2,1,0:T(8,128)(2,1)S(1)}, u32[]{:S(2)}, u32[]{:S(2)}) async-start(f16[8,512,128]{2,1,0:T(8,128)(2,1)} %convert_element_type.19), calls=%async_computation.3 | async-start | bytes 2097152 | tf_op jit(solution)/shard_map/all_to_all | solution.py:213
  80.5 6.4 %collective-permute-start.16 = (bf16[16,64,128]{2,1,0:T(8,128)(2,1)S(1)}, bf16[16,64,128]{2,1,0:T(8,128)(2,1)S(1)}, u32[]{:S(2)}, u32[]{:S(2)}) collective-permute-start(bf16[16,64,128]{2,1,0:T(8,128)(2,1)S(1)} %all-to-all-done.1.mine), channel_id=1, source_target_pairs={{0,8},{8,0},{1,9},{9,1},{2,10},{10,2},{3,11},{11,3},{4,12},{12,4},... | collective-permute-start | bytes 786440 | tf_op jit(solution)/shard_map/ppermute | solution.py:244
  91.7 3.9 %all-to-all-start.4 = ((f16[8,8,2,8,256]{4,3,2,1,0:T(8,128)(2,1)}), f16[8,8,2,8,256]{4,3,2,1,0:T(8,128)(2,1)S(1)}, u32[]{:S(2)}, u32[]{:S(2)}) async-start(f16[8,8,2,8,256]{4,3,2,1,0:T(8,128)(2,1)} %convert_element_type.22), calls=%async_computation.4 | async-start | bytes 1048576 | tf_op jit(solution)/shard_map/all_to_all | solution.py:213
  95.6 7.4 %collective-permute-start.17 = (f32[4,4,4,8,128]{4,3,2,1,0:T(8,128)S(1)}, f32[4,4,4,8,128]{4,3,2,1,0:T(8,128)S(1)}, u32[]{:S(2)}, u32[]{:S(2)}) collective-permute-start(f32[4,4,4,8,128]{4,3,2,1,0:T(8,128)S(1)} %get-tuple-element.51), channel_id=1, source_target_pairs={{0,8},{8,0},{1,9},{9,1},{2,10},{10,2},{3,11},{11,3},{4,12},{12,4},... | collective-permute-start | bytes 786440 | tf_op jit(solution)/shard_map/ppermute | solution.py:246
  105.4 14.2 %all_to_all.30 = f32[16,2,8,128]{3,2,1,0:T(8,128)S(1)} all-to-all(f32[16,2,8,128]{3,2,1,0:T(8,128)S(1)} %copy.10), channel_id=1, replica_groups=mesh['x'=4,'zh'=4,'core'=2,'zl'=2,'y'=4] {'x','zh'}, dimensions={0} | all-to-all | bytes 262144 | tf_op jit(solution)/shard_map/all_to_all | solution.py:216
  119.7 5.5 %collective-permute-start.18 = (f32[8,128]{1,0:T(8,128)S(1)}, f32[8,128]{1,0:T(8,128)S(1)}, u32[]{:S(2)}, u32[]{:S(2)}) collective-permute-start(f32[8,128]{1,0:T(8,128)S(1)} %slice_bitcast_fusion), channel_id=1, source_target_pairs={{0,8},{8,0},{1,9},{9,1},{2,10},{10,2},{3,11},{11,3},{4,12},{12,4},... | collective-permute-start | bytes 12296 | tf_op jit(solution)/shard_map/ppermute | solution.py:253
  (68 shorter events, 21.4 us)
Async XLA Ops:
  0.6 25.5 %collective-permute-start.5 = (bf16[512,2048]{1,0:T(8,128)(2,1)}, bf16[512,2048]{1,0:T(8,128)(2,1)S(1)}, u32[]{:S(2)}, u32[]{:S(2)}) collective-permute-start(bf16[512,2048]{1,0:T(8,128)(2,1)} %refs_8_.3), channel_id=1, source_target_pairs={{0,8},{8,0},{1,9},{9,1},{2,10},{10,2},{3,11},{11,3},{4,12},{12,4},... | collective-permute-start | bytes 6291464 | tf_op jit(solution)/shard_map/ppermute | solution.py:218
  5.7 9.4 %collective-permute-start.2 = (bf16[64,2048]{1,0:T(8,128)(2,1)}, bf16[64,2048]{1,0:T(8,128)(2,1)S(1)}, u32[]{:S(2)}, u32[]{:S(2)}) collective-permute-start(bf16[64,2048]{1,0:T(8,128)(2,1)} %shard_map.59.own.refs_0_.source), channel_id=1, source_target_pairs={{0,64},{64,128},{128,192},{192,0},{1,65},{65,129},{129,193},{193,1... | collective-permute-start | bytes 786440 | tf_op jit(solution)/shard_map/ppermute | solution.py:210
  5.7 9.4 %collective-permute-start.3 = (bf16[64,2048]{1,0:T(8,128)(2,1)}, bf16[64,2048]{1,0:T(8,128)(2,1)S(1)}, u32[]{:S(2)}, u32[]{:S(2)}) collective-permute-start(bf16[64,2048]{1,0:T(8,128)(2,1)} %shard_map.59.own.refs_0_.source), channel_id=1, source_target_pairs={{0,192},{64,0},{128,64},{192,128},{1,193},{65,1},{129,65},{193,129... | collective-permute-start | bytes 786440 | tf_op jit(solution)/shard_map/ppermute | solution.py:210
  8.4 12.4 %collective-permute-start = (bf16[64,2048]{1,0:T(8,128)(2,1)}, bf16[64,2048]{1,0:T(8,128)(2,1)}, u32[]{:S(2)}, u32[]{:S(2)}) collective-permute-start(bf16[64,2048]{1,0:T(8,128)(2,1)} %shard_map.59.own.refs_0_.source), channel_id=1, source_target_pairs={{0,16},{16,32},{32,48},{48,0},{1,17},{17,33},{33,49},{49,1},{2,18}... | collective-permute-start | bytes 786440 | tf_op jit(solution)/shard_map/ppermute | solution.py:222
  9.6 16.5 %collective-permute-start.1 = (bf16[64,2048]{1,0:T(8,128)(2,1)}, bf16[64,2048]{1,0:T(8,128)(2,1)}, u32[]{:S(2)}, u32[]{:S(2)}) collective-permute-start(bf16[64,2048]{1,0:T(8,128)(2,1)} %shard_map.59.own.refs_0_.source), channel_id=1, source_target_pairs={{0,48},{16,0},{32,16},{48,32},{1,49},{17,1},{33,17},{49,33},{2,50}... | collective-permute-start | bytes 786440 | tf_op jit(solution)/shard_map/ppermute | solution.py:222
  15.1 11.0 %collective-permute-start.4 = (bf16[64,2048]{1,0:T(8,128)(2,1)S(1)}, bf16[64,2048]{1,0:T(8,128)(2,1)S(1)}, u32[]{:S(2)}, u32[]{:S(2)}) collective-permute-start(bf16[64,2048]{1,0:T(8,128)(2,1)S(1)} %collective-permute-done.2.refs_1_), channel_id=1, source_target_pairs={{0,64},{64,128},{128,192},{192,0},{1,65},{65,129},{129,193},{193,1... | collective-permute-start | bytes 786440 | tf_op jit(solution)/shard_map/ppermute | solution.py:224
  15.2 18.8 %all-to-all-start = ((bf16[8,2,64,128]{3,2,1,0:T(8,128)(2,1)}), bf16[8,2,64,128]{3,2,1,0:T(8,128)(2,1)S(1)}, u32[]{:S(2)}, u32[]{:S(2)}) async-start(bf16[8,2,64,128]{3,2,1,0:T(8,128)(2,1)} %shard_map.60), calls=%async_computation | async-start | bytes 524288 | tf_op jit(solution)/shard_map/all_to_all | solution.py:213
  26.2 15.6 %collective-permute-start.6 = (bf16[64,2048]{1,0:T(8,128)(2,1)}, bf16[64,2048]{1,0:T(8,128)(2,1)S(1)}, u32[]{:S(2)}, u32[]{:S(2)}) collective-permute-start(bf16[64,2048]{1,0:T(8,128)(2,1)} %collective-permute-done.refs_4_), channel_id=1, source_target_pairs={{0,16},{16,32},{32,48},{48,0},{1,17},{17,33},{33,49},{49,1},{2,18}... | collective-permute-start | bytes 786440 | tf_op jit(solution)/shard_map/ppermute | solution.py:228
  29.3 12.4 %collective-permute-start.7 = (bf16[64,2048]{1,0:T(8,128)(2,1)}, bf16[64,2048]{1,0:T(8,128)(2,1)}, u32[]{:S(2)}, u32[]{:S(2)}) collective-permute-start(bf16[64,2048]{1,0:T(8,128)(2,1)} %collective-permute-done.refs_4_), channel_id=1, source_target_pairs={{0,64},{64,128},{128,192},{192,0},{1,65},{65,129},{129,193},{193,1... | collective-permute-start | bytes 786440 | tf_op jit(solution)/shard_map/ppermute | solution.py:210
  29.3 12.4 %collective-permute-start.8 = (bf16[64,2048]{1,0:T(8,128)(2,1)}, bf16[64,2048]{1,0:T(8,128)(2,1)}, u32[]{:S(2)}, u32[]{:S(2)}) collective-permute-start(bf16[64,2048]{1,0:T(8,128)(2,1)} %collective-permute-done.refs_4_), channel_id=1, source_target_pairs={{0,192},{64,0},{128,64},{192,128},{1,193},{65,1},{129,65},{193,129... | collective-permute-start | bytes 786440 | tf_op jit(solution)/shard_map/ppermute | solution.py:210
  32.0 9.7 %collective-permute-start.10 = (bf16[64,2048]{1,0:T(8,128)(2,1)}, bf16[64,2048]{1,0:T(8,128)(2,1)S(1)}, u32[]{:S(2)}, u32[]{:S(2)}) collective-permute-start(bf16[64,2048]{1,0:T(8,128)(2,1)} %collective-permute-done.1.refs_7_), channel_id=1, source_target_pairs={{0,192},{64,0},{128,64},{192,128},{1,193},{65,1},{129,65},{193,129... | collective-permute-start | bytes 786440 | tf_op jit(solution)/shard_map/ppermute | solution.py:210
  32.1 10.5 %collective-permute-start.9 = (bf16[64,2048]{1,0:T(8,128)(2,1)}, bf16[64,2048]{1,0:T(8,128)(2,1)S(1)}, u32[]{:S(2)}, u32[]{:S(2)}) collective-permute-start(bf16[64,2048]{1,0:T(8,128)(2,1)} %collective-permute-done.1.refs_7_), channel_id=1, source_target_pairs={{0,64},{64,128},{128,192},{192,0},{1,65},{65,129},{129,193},{193,1... | collective-permute-start | bytes 786440 | tf_op jit(solution)/shard_map/ppermute | solution.py:210
  34.8 19.9 %all-to-all-start.1 = ((bf16[16,64,128]{2,1,0:T(8,128)(2,1)}), bf16[16,64,128]{2,1,0:T(8,128)(2,1)S(1)}, u32[]{:S(2)}, u32[]{:S(2)}) async-start(bf16[16,64,128]{2,1,0:T(8,128)(2,1)} %shard_map.63), calls=%async_computation.1 | async-start | bytes 524288 | tf_op jit(solution)/shard_map/all_to_all | solution.py:216
  42.6 12.1 %collective-permute-start.13 = (bf16[64,2048]{1,0:T(8,128)(2,1)S(1)}, bf16[64,2048]{1,0:T(8,128)(2,1)S(1)}, u32[]{:S(2)}, u32[]{:S(2)}) collective-permute-start(bf16[64,2048]{1,0:T(8,128)(2,1)S(1)} %collective-permute-done.6.refs_4_), channel_id=1, source_target_pairs={{0,64},{64,128},{128,192},{192,0},{1,65},{65,129},{129,193},{193,1... | collective-permute-start | bytes 786440 | tf_op jit(solution)/shard_map/ppermute | solution.py:210
  42.6 12.1 %collective-permute-start.14 = (bf16[64,2048]{1,0:T(8,128)(2,1)S(1)}, bf16[64,2048]{1,0:T(8,128)(2,1)}, u32[]{:S(2)}, u32[]{:S(2)}) collective-permute-start(bf16[64,2048]{1,0:T(8,128)(2,1)S(1)} %collective-permute-done.6.refs_4_), channel_id=1, source_target_pairs={{0,192},{64,0},{128,64},{192,128},{1,193},{65,1},{129,65},{193,129... | collective-permute-start | bytes 786440 | tf_op jit(solution)/shard_map/ppermute | solution.py:210
  54.7 21.2 %all-to-all-start.2 = ((f16[8,512,128]{2,1,0:T(8,128)(2,1)}), f16[8,512,128]{2,1,0:T(8,128)(2,1)}, u32[]{:S(2)}, u32[]{:S(2)}) async-start(f16[8,512,128]{2,1,0:T(8,128)(2,1)} %convert_element_type.18), calls=%async_computation.2 | async-start | bytes 2097152 | tf_op jit(solution)/shard_map/all_to_all | solution.py:213
  58.9 6.7 %collective-permute-start.15 = (bf16[64,2048]{1,0:T(8,128)(2,1)S(1)}, bf16[64,2048]{1,0:T(8,128)(2,1)S(1)}, u32[]{:S(2)}, u32[]{:S(2)}) collective-permute-start(bf16[64,2048]{1,0:T(8,128)(2,1)S(1)} %collective-permute-done.13.refs_5_), channel_id=1, source_target_pairs={{0,64},{64,128},{128,192},{192,0},{1,65},{65,129},{129,193},{193,1... | collective-permute-start | bytes 786440 | tf_op jit(solution)/shard_map/ppermute | solution.py:239
  59.2 9.9 %collective-permute-start.11 = (bf16[64,2048]{1,0:T(8,128)(2,1)}, bf16[64,2048]{1,0:T(8,128)(2,1)S(1)}, u32[]{:S(2)}, u32[]{:S(2)}) collective-permute-start(bf16[64,2048]{1,0:T(8,128)(2,1)} %collective-permute-done.7.refs_5_), channel_id=1, source_target_pairs={{0,64},{64,128},{128,192},{192,0},{1,65},{65,129},{129,193},{193,1... | collective-permute-start | bytes 786440 | tf_op jit(solution)/shard_map/ppermute | solution.py:233
  60.0 9.1 %collective-permute-start.12 = (bf16[64,2048]{1,0:T(8,128)(2,1)S(1)}, bf16[64,2048]{1,0:T(8,128)(2,1)S(1)}, u32[]{:S(2)}, u32[]{:S(2)}) collective-permute-start(bf16[64,2048]{1,0:T(8,128)(2,1)S(1)} %collective-permute-done.10.refs_1_), channel_id=1, source_target_pairs={{0,192},{64,0},{128,64},{192,128},{1,193},{65,1},{129,65},{193,129... | collective-permute-start | bytes 786440 | tf_op jit(solution)/shard_map/ppermute | solution.py:233
  75.9 14.0 %all-to-all-start.3 = ((f16[8,512,128]{2,1,0:T(8,128)(2,1)}), f16[8,512,128]{2,1,0:T(8,128)(2,1)S(1)}, u32[]{:S(2)}, u32[]{:S(2)}) async-start(f16[8,512,128]{2,1,0:T(8,128)(2,1)} %convert_element_type.19), calls=%async_computation.3 | async-start | bytes 2097152 | tf_op jit(solution)/shard_map/all_to_all | solution.py:213
  80.5 9.6 %collective-permute-start.16 = (bf16[16,64,128]{2,1,0:T(8,128)(2,1)S(1)}, bf16[16,64,128]{2,1,0:T(8,128)(2,1)S(1)}, u32[]{:S(2)}, u32[]{:S(2)}) collective-permute-start(bf16[16,64,128]{2,1,0:T(8,128)(2,1)S(1)} %all-to-all-done.1.mine), channel_id=1, source_target_pairs={{0,8},{8,0},{1,9},{9,1},{2,10},{10,2},{3,11},{11,3},{4,12},{12,4},... | collective-permute-start | bytes 786440 | tf_op jit(solution)/shard_map/ppermute | solution.py:244
  91.7 13.5 %all-to-all-start.4 = ((f16[8,8,2,8,256]{4,3,2,1,0:T(8,128)(2,1)}), f16[8,8,2,8,256]{4,3,2,1,0:T(8,128)(2,1)S(1)}, u32[]{:S(2)}, u32[]{:S(2)}) async-start(f16[8,8,2,8,256]{4,3,2,1,0:T(8,128)(2,1)} %convert_element_type.22), calls=%async_computation.4 | async-start | bytes 1048576 | tf_op jit(solution)/shard_map/all_to_all | solution.py:213
  95.6 8.6 %collective-permute-start.17 = (f32[4,4,4,8,128]{4,3,2,1,0:T(8,128)S(1)}, f32[4,4,4,8,128]{4,3,2,1,0:T(8,128)S(1)}, u32[]{:S(2)}, u32[]{:S(2)}) collective-permute-start(f32[4,4,4,8,128]{4,3,2,1,0:T(8,128)S(1)} %get-tuple-element.51), channel_id=1, source_target_pairs={{0,8},{8,0},{1,9},{9,1},{2,10},{10,2},{3,11},{11,3},{4,12},{12,4},... | collective-permute-start | bytes 786440 | tf_op jit(solution)/shard_map/ppermute | solution.py:246
  119.7 6.3 %collective-permute-start.18 = (f32[8,128]{1,0:T(8,128)S(1)}, f32[8,128]{1,0:T(8,128)S(1)}, u32[]{:S(2)}, u32[]{:S(2)}) collective-permute-start(f32[8,128]{1,0:T(8,128)S(1)} %slice_bitcast_fusion), channel_id=1, source_target_pairs={{0,8},{8,0},{1,9},{9,1},{2,10},{10,2},{3,11},{11,3},{4,12},{12,4},... | collective-permute-start | bytes 12296 | tf_op jit(solution)/shard_map/ppermute | solution.py:253
  (8 other events, 95.6 us)
